TPU v7x, 128 devices: a whole 4x4x4 slice. The times are simulated.
128 devices in a mesh: band: 16 (over x, z_hi, core), slab: 8 (over y, z_lo).
Axes of the slice: x: 4, y: 4, z: 4 (z_hi: 2, z_lo: 2; z = z_hi * 2 + z_lo), core: 2. Of those that a mesh axis runs over, the one named last changes fastest.
Arguments:
- orbitals: bfloat16 [16, 128, 128, 128], P('band', 'slab'), may hold values from -6 to 6
- projections: bfloat16 [16, 9, 512], P('band'), may hold values from -4 to 4
- aug_blocks: bfloat16 [512, 8, 9, 128], P(('band', 'slab')), may hold values from -3 to 3
- atom_home: int32 [3, 512], replicated, may hold values from 0 to 62, as said below
Outputs:
- exchange_applied: float32 [16, 128, 128, 128], P('band', 'slab')
Inputs may be any that keep to these rules, and one draw needn't show every extreme that they name: `atom_home`: row 0 holds an atom's first brick along the first dimension, rows 1 and 2 along the second and third; its box of 2 x 2 x 2 bricks lies inside one slab of 16 planes. `atom_home`: atoms are numbered by device, 4 to a device in mesh order (band first). Of one device's atoms at most 1 lie in one slab, and exactly 1 lie in one slab that is the same for every device.
All inputs are finite; a program needn't handle non-finite values.
Results may differ from a plain program's by a relative error of at most 0.0012.
Values may be sent and summed in bfloat16 or wider, within the bound.
No kernel may reach another device: no remote copies, remote signals or barrier semaphores. Data moves between devices by JAX's collectives and lax.ppermute only.
A program may use at most 192 MiB of HBM per device.

v0:
```python
import functools
import math

import numpy as np
import jax
import jax.numpy as jnp
from jax import lax
from jax.experimental import pallas as pl
from jax.experimental.pallas import tpu as pltpu
from jax.sharding import PartitionSpec as P

KERNEL_SCALE = 0.5
SCREENING_RANGE = 0.002
NG = 128
SLABS = 8
ROWS = NG // SLABS
PLANES = NG // SLABS
BLOCK_LIMIT = 3.0
QMAX = 32760.0
STEPS = 8.0
FWD_TILES = PLANES + 2
BACK_TILES = PLANES + 1
BF = jnp.bfloat16
F32 = jnp.float32
VMEM_LIMIT = 50 * 1024 * 1024


def hartley_host():
    index = np.arange(NG)
    angle = (index[:, None] * index[None, :] % NG) * (2.0 * math.pi / NG)
    return (np.cos(angle) + np.sin(angle)).astype(np.float32)


def split_host(table):
    high = table.astype(jnp.bfloat16)
    low = (table - high.astype(np.float32)).astype(jnp.bfloat16)
    return high, low


def row_order():
    by_size = sorted(range(NG), key=lambda k: (min(k, NG - k), k))
    return np.array([[by_size[d + SLABS * r] for r in range(ROWS)] for d in range(SLABS)])


def fold_square_host():
    index = np.arange(NG)
    return ((np.minimum(index, NG - index)).astype(np.float32) * np.float32(2.0 * math.pi / NG)) ** 2


def tables():
    table = hartley_host()
    high, low = split_host(table)
    order = row_order().reshape(-1)
    high_y, low_y = high[order], low[order]
    right = np.concatenate([high, high, low], axis=0)
    left = np.concatenate([high, low, high], axis=1)
    left_y = np.concatenate([high_y, low_y, high_y], axis=1)
    left_y_back = np.concatenate([high_y.T, low_y.T, high_y.T], axis=1)
    return right, left, left_y, left_y_back


def split(value):
    high = value.astype(BF)
    low = (value - high.astype(F32)).astype(BF)
    return high, low


def dot(a, b):
    return jnp.dot(a, b, preferred_element_type=F32)


def times_right(value, right_ref):
    high, low = split(value)
    both = jnp.concatenate([high, low], axis=1)
    return dot(both, right_ref[: 2 * NG, :]) + dot(high, right_ref[2 * NG :, :])


def times_left(left_ref, value):
    high, low = split(value)
    return dot(left_ref[...], jnp.concatenate([high, high, low], axis=0))


def step_code(largest):
    return jnp.ceil(jnp.log(jnp.maximum(largest, 1e-30)) * (STEPS / math.log(2.0)))


def step_size(code):
    return jnp.exp(code * (math.log(2.0) / STEPS)) * (1.001 / QMAX)


def to_int16(value):
    return value.astype(jnp.int32).astype(jnp.int16)


def from_int16(value):
    return value.astype(jnp.int32).astype(F32)


def charge_kernel(weight_ref, block_ref, out_ref, held):
    weight = weight_ref[...]
    bound = jnp.sum(jnp.abs(weight), axis=1, keepdims=True) * BLOCK_LIMIT
    factor = QMAX / jnp.maximum(bound, 1e-30)
    high, low = split(weight)
    both = jnp.concatenate([high, low], axis=0)
    rows = weight.shape[0]
    for y in range(8):
        product = dot(both, block_ref[y])
        held[:, y, :] = (product[:rows] + product[rows:]) * factor
    half = rows // 2
    both_pairs = jnp.concatenate([held[:half], held[half:]], axis=1)
    out_ref[...] = to_int16(jnp.round(both_pairs))


def density_kernel(home_ref, scale_ref, charge_ref, own_ref, next_ref, right_ref, left_ref, out_ref, field):
    for x in range(PLANES):
        own = own_ref[x].astype(F32)
        field[0, x] = own * own
        field[1, x] = own * next_ref[x].astype(F32)
    lane = lax.broadcasted_iota(jnp.int32, (8, NG), 1)

    def add_atom(d, carry):
        plane = home_ref[0, d]
        brick_y = home_ref[1, d]
        shift = home_ref[2, d] * 8
        values = from_int16(charge_ref[d])
        inside = ((lane - shift) & (NG - 1)) < 16
        places = []
        for p in range(2):
            tile = values[8 * p : 8 * p + 8] * scale_ref[p, d]
            for g in range(8):
                turned = pltpu.roll(tile, (shift + (NG - 16 * g)) & (NG - 1), 1)
                row = pl.multiple_of(((brick_y + g % 2) & (NG // 8 - 1)) * 8, 8)
                at = (p, plane + g // 2, pl.ds(row, 8))
                places.append((at, field[at] + jnp.where(inside, turned, 0.0)))
        for at, total in places:
            field[at] = total
        return carry

    lax.fori_loop(0, charge_ref.shape[0], add_atom, 0)

    def transform(p, carry):
        for x in range(0, PLANES, 2):
            first = times_right(field[p, x], right_ref)
            second = times_right(field[p, x + 1], right_ref)
            both = times_left(left_ref, jnp.concatenate([first, second], axis=1))
            field[p, x] = both[:, :NG]
            field[p, x + 1] = both[:, NG:]
        return carry

    lax.fori_loop(0, 2, transform, 0)

    def pack(n, carry):
        p = n // SLABS
        d = n % SLABS
        rows = pl.ds(pl.multiple_of(d * ROWS, ROWS), ROWS)
        largest = jnp.abs(field[p, 0, rows])
        for x in range(1, PLANES):
            largest = jnp.maximum(largest, jnp.abs(field[p, x, rows]))
        code = step_code(largest)
        factor = 1.0 / step_size(code)
        base = p * FWD_TILES
        lows = []
        for x in range(PLANES):
            scaled = field[p, x, rows] * factor
            whole = jnp.round(scaled)
            out_ref[d, base + x] = to_int16(whole)
            lows.append((scaled - whole)[0:1])
        out_ref[d, base + PLANES] = to_int16(code)
        low = jnp.concatenate(lows, axis=0) * (2.0 * QMAX)
        out_ref[d, base + PLANES + 1] = to_int16(jnp.round(low))
        return carry

    lax.fori_loop(0, 2 * SLABS, pack, 0)


def solve_kernel(square_ref, in_ref, fold_x_ref, fold_z_ref, left_ref, out_ref, field):
    def unpack(n, carry):
        p = n // SLABS
        s = n % SLABS
        base = p * FWD_TILES
        step = step_size(from_int16(in_ref[s, base + PLANES]))
        for x in range(PLANES):
            field[p, s * PLANES + x] = from_int16(in_ref[s, base + x]) * step
        low = from_int16(in_ref[s, base + PLANES + 1]) * (step[0:1] * (0.5 / QMAX))
        planes = pl.ds(s * PLANES, PLANES)
        field[p, planes, 0, :] = field[p, planes, 0, :] + low
        return carry

    lax.fori_loop(0, 2 * SLABS, unpack, 0)
    fold = fold_x_ref[...] + fold_z_ref[...]
    for r in range(ROWS):
        total = fold + square_ref[r]
        table = jnp.where(total > 0, KERNEL_SCALE / (total + SCREENING_RANGE), 0.0) * (1.0 / NG**3)
        columns = jnp.concatenate([field[0, :, r, :], field[1, :, r, :]], axis=1)
        spectrum = times_left(left_ref, columns)
        spectrum = spectrum * jnp.concatenate([table, table], axis=1)
        columns = times_left(left_ref, spectrum)
        field[0, :, r, :] = columns[:, :NG]
        field[1, :, r, :] = columns[:, NG:]

    def pack(n, carry):
        p = n // SLABS
        s = n % SLABS
        base = p * BACK_TILES
        largest = jnp.abs(field[p, s * PLANES])
        for x in range(1, PLANES):
            largest = jnp.maximum(largest, jnp.abs(field[p, s * PLANES + x]))
        code = step_code(largest)
        factor = 1.0 / step_size(code)
        for x in range(PLANES):
            out_ref[s, base + x] = to_int16(jnp.round(field[p, s * PLANES + x] * factor))
        out_ref[s, base + PLANES] = to_int16(code)
        return carry

    lax.fori_loop(0, 2 * SLABS, pack, 0)


def potential_pair(in_ref, steps, x, p, left_ref, right_ref):
    base = p * BACK_TILES + x
    halves = []
    for k in range(2):
        halves.append(jnp.concatenate([from_int16(in_ref[s, base + k]) * steps[s] for s in range(SLABS)], axis=0))
    both = times_left(left_ref, jnp.concatenate(halves, axis=1))
    return times_right(both[:, :NG], right_ref), times_right(both[:, NG:], right_ref)


def back_cross_kernel(in_ref, own_ref, next_ref, left_ref, right_ref, kept_ref, sent_ref, codes):
    steps = [step_size(from_int16(in_ref[s, BACK_TILES + PLANES])) for s in range(SLABS)]
    for x in range(0, PLANES, 2):
        pair = potential_pair(in_ref, steps, x, 1, left_ref, right_ref)
        for k in range(2):
            potential = pair[k]
            kept_ref[x + k] = potential * next_ref[x + k].astype(F32)
            product = potential * own_ref[x + k].astype(F32)
            code = step_code(jnp.max(jnp.abs(product), axis=0, keepdims=True))
            codes[x + k : x + k + 1, :] = code
            sent_ref[pl.ds((x + k) * NG, NG), :] = to_int16(jnp.round(product * (1.0 / step_size(code))))
    sent_ref[pl.ds(PLANES * NG, PLANES), :] = to_int16(codes[...])


def back_own_kernel(in_ref, own_ref, kept_ref, left_ref, right_ref, out_ref):
    steps = [step_size(from_int16(in_ref[s, PLANES])) for s in range(SLABS)]
    for x in range(0, PLANES, 2):
        pair = potential_pair(in_ref, steps, x, 0, left_ref, right_ref)
        for k in range(2):
            out_ref[x + k] = kept_ref[x + k] + pair[k] * own_ref[x + k].astype(F32)


def add_kernel(sum_ref, sent_ref, out_ref):
    steps = step_size(from_int16(sent_ref[pl.ds(PLANES * NG, PLANES), :]))
    for x in range(PLANES):
        out_ref[0, x] = sum_ref[x] + from_int16(sent_ref[pl.ds(x * NG, NG), :]) * steps[x : x + 1]


def vmem():
    return pl.BlockSpec(memory_space=pltpu.VMEM)


def smem():
    return pl.BlockSpec(memory_space=pltpu.SMEM)


def call(kernel, in_specs, out_shape, scratch, name):
    many = isinstance(out_shape, (list, tuple))
    return pl.pallas_call(
        kernel,
        in_specs=in_specs,
        out_specs=[vmem() for _ in out_shape] if many else vmem(),
        out_shape=out_shape,
        scratch_shapes=scratch,
        name=name,
        compiler_params=pltpu.CompilerParams(vmem_limit_bytes=VMEM_LIMIT),
    )


def from_behind(block, axis, distance):
    count = lax.axis_size(axis)
    return lax.ppermute(block, axis, [((i - distance) % count, i) for i in range(count)])


def per_device(orbitals, projections, aug_blocks, atom_home):
    n_band = lax.axis_size("band")
    n_slab = lax.axis_size("slab")
    owners = n_band * n_slab
    atom_dev = aug_blocks.shape[0]
    channels = projections.shape[1]
    slab_bricks = PLANES // 2
    my_slab = lax.axis_index("slab")
    owner_me = lax.axis_index("band") * n_slab + my_slab
    right, left, left_y, left_y_back = (jnp.asarray(t) for t in tables())
    squares = fold_square_host()
    fold_rows = jnp.asarray(squares[row_order()])

    own = orbitals[0]
    own_proj = projections[0]
    next_proj = from_behind(own_proj, "band", -1)
    nxt = from_behind(own, "band", -1)

    by_owner = own_proj.reshape(channels, n_band, n_slab, atom_dev)
    mine = lax.dynamic_index_in_dim(by_owner, my_slab, 2, keepdims=False)
    mine = mine.transpose(1, 2, 0).reshape(n_band, atom_dev * channels)
    all_proj = lax.all_to_all(mine, "band", split_axis=0, concat_axis=0, tiled=True).astype(F32)

    slab_of = (atom_home[0] // slab_bricks).reshape(owners, atom_dev)
    here = slab_of == my_slab
    home = atom_home.reshape(3, owners, atom_dev)
    home = home - jnp.array([1, 0, 0], jnp.int32)[:, None, None] * (my_slab * slab_bricks)
    home = jnp.sum(jnp.where(here[None], home, 0), axis=2) * jnp.array([2, 1, 1], jnp.int32)[:, None]

    my_slabs = lax.dynamic_index_in_dim(slab_of, owner_me, 0, keepdims=False)
    goes = (my_slabs[None, :] == jnp.arange(n_slab, dtype=jnp.int32)[:, None]).astype(F32)
    goes = jnp.repeat(goes, channels, axis=1)
    pairs = jnp.stack([all_proj * all_proj, all_proj * jnp.roll(all_proj, -1, axis=0)])
    weight = (pairs[:, :, None, :] * goes[None, None]).reshape(2 * owners, atom_dev * channels)
    blocks = aug_blocks.reshape(atom_dev, 2, 2, 2, channels, 2, 8, 8)
    blocks = blocks.transpose(6, 0, 4, 1, 5, 2, 3, 7).reshape(8, atom_dev * channels, NG)
    charges = call(
        charge_kernel,
        [vmem(), vmem()],
        jax.ShapeDtypeStruct((owners, 16, NG), jnp.int16),
        [pltpu.VMEM((2 * owners, 8, NG), F32)],
        "charges",
    )(weight, blocks)
    charges = lax.all_to_all(charges, ("band", "slab"), split_axis=0, concat_axis=0, tiled=True)

    own_wide = own_proj.astype(F32)
    bound = jnp.stack([own_wide * own_wide, own_wide * next_proj.astype(F32)])
    bound = jnp.sum(jnp.abs(bound), axis=1).reshape(2, owners, atom_dev)
    bound = jnp.sum(jnp.where(here[None], bound, 0.0), axis=2) * (BLOCK_LIMIT / QMAX)

    spectrum = call(
        density_kernel,
        [smem(), smem()] + [vmem()] * 5,
        jax.ShapeDtypeStruct((n_slab, 2 * FWD_TILES, 16, NG), jnp.int16),
        [pltpu.VMEM((2, PLANES, NG, NG), F32)],
        "density",
    )(home, bound, charges, own, nxt, right, left_y)
    spectrum = lax.all_to_all(spectrum, "slab", split_axis=0, concat_axis=0, tiled=True)

    columns = call(
        solve_kernel,
        [smem()] + [vmem()] * 4,
        jax.ShapeDtypeStruct((n_slab, 2 * BACK_TILES, 16, NG), jnp.int16),
        [pltpu.VMEM((2, NG, ROWS, NG), F32)],
        "solve",
    )(
        lax.dynamic_index_in_dim(fold_rows, my_slab, 0, keepdims=False),
        spectrum,
        jnp.asarray(np.broadcast_to(squares[:, None], (NG, NG)).copy()),
        jnp.asarray(squares[None, :]),
        left,
    )
    columns = lax.all_to_all(columns, "slab", split_axis=0, concat_axis=0, tiled=True)

    kept, sent = call(
        back_cross_kernel,
        [vmem()] * 5,
        [
            jax.ShapeDtypeStruct((PLANES, NG, NG), F32),
            jax.ShapeDtypeStruct((PLANES * NG + PLANES, NG), jnp.int16),
        ],
        [pltpu.VMEM((PLANES, NG), F32)],
        "back_cross",
    )(columns, own, nxt, left_y_back, right)
    got = from_behind(sent, "band", 1)
    total = call(
        back_own_kernel,
        [vmem()] * 5,
        jax.ShapeDtypeStruct((PLANES, NG, NG), F32),
        [],
        "back_own",
    )(columns, own, kept, left_y_back, right)
    return call(
        add_kernel,
        [vmem()] * 2,
        jax.ShapeDtypeStruct((1, PLANES, NG, NG), F32),
        [],
        "add_previous",
    )(total, got)


def solution(mesh):
    in_specs = (
        P("band", "slab", None, None),
        P("band", None, None),
        P(("band", "slab"), None, None, None),
        P(),
    )
    out_specs = P("band", "slab", None, None)
    return jax.shard_map(
        per_device, mesh=mesh, in_specs=in_specs, out_specs=out_specs, check_vma=False
    )
```

profile of v0, /device:TPU:1, one launch (start us, length us, event | category | flops | bytes accessed | tf_op | source)
XLA Modules:
  0.0 126.2 jit_solution(15152172946173881883)
XLA Ops:
  0.0 1.4 %collective-permute-start = (bf16[9,512]{1,0:T(8,128)(2,1)}, bf16[9,512]{1,0:T(8,128)(2,1)S(1)}, u32[]{:S(2)}, u32[]{:S(2)}) collective-permute-start(bf16[9,512]{1,0:T(8,128)(2,1)} %bitcast.34), channel_id=1, source_target_pairs={{8,0},{16,8},{24,16},{32,24},{40,32},{48,40},{56,48},{64,56},{72,6... | collective-permute-start | bytes 27656 | tf_op jit(solution)/shard_map/ppermute | solution.py:278
  1.4 0.9 copy.22
  2.3 0.7 all_to_all.20
  3.0 8.9 %all-to-all-start = ((bf16[16,1,36]{2,1,0:T(2,128)(2,1)}), bf16[16,1,36]{2,1,0:T(2,128)(2,1)S(1)}, u32[]{:S(2)}, u32[]{:S(2)}) async-start(bf16[16,1,36]{2,1,0:T(2,128)(2,1)} %all_to_all.20), calls=%async_computation | async-start | bytes 16384 | tf_op jit(solution)/shard_map/all_to_all | solution.py:302
  11.9 0.3 collective-permute-start.1
  12.2 0.7 convert_multiply_fusion
  12.9 0.7 slice_reduce_fusion
  13.6 0.9 reshape.109
  14.5 0.1 squeeze.20
  14.7 0.7 broadcast_multiply_fusion.3
  15.4 0.2 select_reduce_fusion
  15.6 0.7 broadcast_multiply_fusion.1.home_ref
  16.4 0.1 mul.86
  16.5 3.1 %reshape.111 = bf16[4,2,2,2,9,2,8,8]{7,6,5,3,2,1,4,0:T(8,128)(2,1)} reshape(bf16[4,8,9,128]{3,1,2,0:T(8,128)(2,1)} %param.15) | data formatting | bytes 147456 | tf_op jit(solution)/shard_map/reshape | solution.py:315
  19.6 2.2 %copy.31 = bf16[8,4,9,2,2,2,2,8]{7,6,5,4,3,2,1,0:T(2,128)(2,1)S(1)} copy(bf16[8,4,9,2,2,2,2,8]{7,0,4,6,5,3,2,1:T(8,128)(2,1)} %bitcast.32) | data formatting | bytes 147456 | tf_op jit(solution)/shard_map/reshape | solution.py:316
  21.8 1.3 %reshape.115.block_ref = bf16[8,36,128]{2,1,0:T(8,128)(2,1)S(1)} reshape(bf16[8,4,9,2,2,2,2,8]{7,6,5,4,3,2,1,0:T(2,128)(2,1)S(1)} %copy.31) | data formatting | bytes 147456 | tf_op jit(solution)/shard_map/reshape | solution.py:316
  23.2 1.8 %charges.1 = s16[128,16,128]{2,1,0:T(8,128)(2,1)} custom-call(f32[256,36]{1,0:T(8,128)S(1)} %bitcast.31, bf16[8,36,128]{2,1,0:T(8,128)(2,1)S(1)} %reshape.115.block_ref), custom_call_target="tpu_custom_call" | custom-call | tf_op jit(solution)/shard_map/charges/pallas_call | solution.py:317
  25.1 10.0 %all-to-all-start.1 = ((s16[128,16,128]{2,1,0:T(8,128)(2,1)}), s16[128,16,128]{2,1,0:T(8,128)(2,1)S(1)}, u32[]{:S(2)}, u32[]{:S(2)}) async-start(s16[128,16,128]{2,1,0:T(8,128)(2,1)} %charges.1), calls=%async_computation.1 | async-start | bytes 1048576 | tf_op jit(solution)/shard_map/all_to_all | solution.py:324
  35.1 0.1 reshape.110
  35.2 0.1 select_reduce_fusion.1
  35.4 13.1 %all-to-all-done.1.charge_ref = s16[128,16,128]{2,1,0:T(8,128)(2,1)S(1)} async-done(((s16[128,16,128]{2,1,0:T(8,128)(2,1)}), s16[128,16,128]{2,1,0:T(8,128)(2,1)S(1)}, u32[]{:S(2)}, u32[]{:S(2)}) %all-to-all-start.1) | async-done | bytes 524320 | tf_op jit(solution)/shard_map/all_to_all | solution.py:324
  48.5 18.3 %density.1 = s16[8,36,16,128]{3,2,1,0:T(8,128)(2,1)} custom-call(s32[3,128]{1,0:T(4,128)S(1)} %broadcast_multiply_fusion.1.home_ref, f32[2,128]{1,0:T(2,128)S(1)} %broadcast_multiply_fusion.2.scale_ref, s16[128,16,128]{2,1,0:T(8,128)(2,1)S(1)} %all-to-all-done.1.charge_ref, bf16[16,128,128]{2,1,0:T(8,128)(2,1)S(1)} %bitcast.28, ...), custom_call_target="tpu_custom_call" | custom-call | tf_op jit(solution)/shard_map/density/pallas_call | solution.py:331
  66.8 3.7 %all-to-all-start.2 = ((s16[8,36,16,128]{3,2,1,0:T(8,128)(2,1)}), s16[8,36,16,128]{3,2,1,0:T(8,128)(2,1)S(1)}, u32[]{:S(2)}, u32[]{:S(2)}) async-start(s16[8,36,16,128]{3,2,1,0:T(8,128)(2,1)} %density.1), calls=%async_computation.2 | async-start | bytes 2359296 | tf_op jit(solution)/shard_map/all_to_all | solution.py:338
  70.5 0.7 fusion.4.square_ref
  71.2 16.0 %all-to-all-done.2.in_ref = s16[8,36,16,128]{3,2,1,0:T(8,128)(2,1)S(1)} async-done(((s16[8,36,16,128]{3,2,1,0:T(8,128)(2,1)}), s16[8,36,16,128]{3,2,1,0:T(8,128)(2,1)S(1)}, u32[]{:S(2)}, u32[]{:S(2)}) %all-to-all-start.2) | async-done | bytes 1179680 | tf_op jit(solution)/shard_map/all_to_all | solution.py:338
  87.2 5.3 %solve.1 = s16[8,34,16,128]{3,2,1,0:T(8,128)(2,1)S(1)} custom-call(f32[16]{0:T(128)S(1)} %fusion.4.square_ref, s16[8,36,16,128]{3,2,1,0:T(8,128)(2,1)S(1)} %all-to-all-done.2.in_ref, f32[128,128]{1,0:T(8,128)S(1)} %copy-done.5, f32[1,128]{1,0:T(1,128)S(1)} %copy-done.6, bf16[128,384]{1,0:T(8,128)(2,1)S(1)} %copy-done.3), custom_call_target="tpu_custom_call" | custom-call | tf_op jit(solution)/shard_map/solve/pallas_call | solution.py:340
  92.5 16.9 %all_to_all.25.in_ref = s16[8,34,16,128]{3,2,1,0:T(8,128)(2,1)S(1)} all-to-all(s16[8,34,16,128]{3,2,1,0:T(8,128)(2,1)S(1)} %solve.1), channel_id=1, replica_groups=mesh['band'=16,'slab'=8] {'slab'}, dimensions={0} | all-to-all | bytes 2228224 | tf_op jit(solution)/shard_map/all_to_all | solution.py:353
  109.4 2.1 %back_cross.1 = (f32[16,128,128]{2,1,0:T(8,128)S(1)}, s16[2064,128]{1,0:T(8,128)(2,1)S(1)}) custom-call(s16[8,34,16,128]{3,2,1,0:T(8,128)(2,1)S(1)} %all_to_all.25.in_ref, bf16[16,128,128]{2,1,0:T(8,128)(2,1)S(1)} %bitcast.29, bf16[16,128,128]{2,1,0:T(8,128)(2,1)S(1)} %collective-permute-done.1.next_ref, bf16[128,384]{1,0:T(8,128)(2,1)S(1)} %copy-done.2, ...), custom_call_target="tpu_custom_call" | custom-call | tf_op jit(solution)/shard_map/back_cross/pallas_call | solution.py:355
  111.5 7.4 %collective-permute-start.2 = (s16[2064,128]{1,0:T(8,128)(2,1)S(1)}, s16[2064,128]{1,0:T(8,128)(2,1)S(1)}, u32[]{:S(2)}, u32[]{:S(2)}) collective-permute-start(s16[2064,128]{1,0:T(8,128)(2,1)S(1)} %get-tuple-element.8), channel_id=1, source_target_pairs={{120,0},{0,8},{8,16},{16,24},{24,32},{32,40},{40,48},{48,56},{56,6... | collective-permute-start | bytes 1585160 | tf_op jit(solution)/shard_map/ppermute | solution.py:278
  118.9 2.0 %back_own.1.sum_ref = f32[16,128,128]{2,1,0:T(8,128)S(1)} custom-call(s16[8,34,16,128]{3,2,1,0:T(8,128)(2,1)S(1)} %all_to_all.25.in_ref, bf16[16,128,128]{2,1,0:T(8,128)(2,1)S(1)} %bitcast.30, f32[16,128,128]{2,1,0:T(8,128)S(1)} %get-tuple-element.7.kept_ref, bf16[128,384]{1,0:T(8,128)(2,1)S(1)} %copy-done.2, bf16[384,128]{1,0:T(8,128)(2,1)S(1)} %copy-done.1), custom_call_target="tpu_custom_call" | custom-call | tf_op jit(solution)/shard_map/back_own/pallas_call | solution.py:366
  120.9 4.2 %collective-permute-done.2.sent_ref = s16[2064,128]{1,0:T(8,128)(2,1)S(1)} collective-permute-done((s16[2064,128]{1,0:T(8,128)(2,1)S(1)}, s16[2064,128]{1,0:T(8,128)(2,1)S(1)}, u32[]{:S(2)}, u32[]{:S(2)}) %collective-permute-start.2) | collective-permute-done | bytes 528416 | tf_op jit(solution)/shard_map/ppermute | solution.py:278
  125.0 1.1 add_previous.1
  (34 shorter events, 0.3 us)
Async XLA Ops:
  0.0 35.0 %collective-permute-start = (bf16[9,512]{1,0:T(8,128)(2,1)}, bf16[9,512]{1,0:T(8,128)(2,1)S(1)}, u32[]{:S(2)}, u32[]{:S(2)}) collective-permute-start(bf16[9,512]{1,0:T(8,128)(2,1)} %bitcast.34), channel_id=1, source_target_pairs={{8,0},{16,8},{24,16},{32,24},{40,32},{48,40},{56,48},{64,56},{72,6... | collective-permute-start | bytes 27656 | tf_op jit(solution)/shard_map/ppermute | solution.py:278
  3.0 20.0 %all-to-all-start = ((bf16[16,1,36]{2,1,0:T(2,128)(2,1)}), bf16[16,1,36]{2,1,0:T(2,128)(2,1)S(1)}, u32[]{:S(2)}, u32[]{:S(2)}) async-start(bf16[16,1,36]{2,1,0:T(2,128)(2,1)} %all_to_all.20), calls=%async_computation | async-start | bytes 16384 | tf_op jit(solution)/shard_map/all_to_all | solution.py:302
  11.9 36.6 %collective-permute-start.1 = (bf16[16,128,128]{2,1,0:T(8,128)(2,1)}, bf16[16,128,128]{2,1,0:T(8,128)(2,1)S(1)}, u32[]{:S(2)}, u32[]{:S(2)}) collective-permute-start(bf16[16,128,128]{2,1,0:T(8,128)(2,1)} %bitcast.27), channel_id=1, source_target_pairs={{8,0},{16,8},{24,16},{32,24},{40,32},{48,40},{56,48},{64,56},{72,6... | collective-permute-start | bytes 1572872 | tf_op jit(solution)/shard_map/ppermute | solution.py:278
  23.0 12.0 %copy-start.7 = (bf16[1,9,512]{2,1,0:T(8,128)(2,1)S(1)}, bf16[1,9,512]{2,1,0:T(8,128)(2,1)}, u32[]{:S(2)}) copy-start(bf16[1,9,512]{2,1,0:T(8,128)(2,1)} %param.14) | copy-start | bytes 27652
  23.2 25.3 %copy-start = (bf16[1,16,128,128]{3,2,1,0:T(8,128)(2,1)S(1)}, bf16[1,16,128,128]{3,2,1,0:T(8,128)(2,1)}, u32[]{:S(2)}) copy-start(bf16[1,16,128,128]{3,2,1,0:T(8,128)(2,1)} %param.13) | copy-start | bytes 1572868
  23.2 25.3 %copy-start.1 = (bf16[384,128]{1,0:T(8,128)(2,1)S(1)}, bf16[384,128]{1,0:T(8,128)(2,1)}, u32[]{:S(2)}) copy-start(bf16[384,128]{1,0:T(8,128)(2,1)} %constant.62.clone.right_ref) | copy-start | bytes 294916
  23.2 25.3 %copy-start.4 = (bf16[128,384]{1,0:T(8,128)(2,1)S(1)}, bf16[128,384]{1,0:T(8,128)(2,1)}, u32[]{:S(2)}) copy-start(bf16[128,384]{1,0:T(8,128)(2,1)} %constant.64.clone.left_ref) | copy-start | bytes 294916
  25.1 23.4 %all-to-all-start.1 = ((s16[128,16,128]{2,1,0:T(8,128)(2,1)}), s16[128,16,128]{2,1,0:T(8,128)(2,1)S(1)}, u32[]{:S(2)}, u32[]{:S(2)}) async-start(s16[128,16,128]{2,1,0:T(8,128)(2,1)} %charges.1), calls=%async_computation.1 | async-start | bytes 1048576 | tf_op jit(solution)/shard_map/all_to_all | solution.py:324
  66.8 20.4 %copy-start.3 = (bf16[128,384]{1,0:T(8,128)(2,1)S(1)}, bf16[128,384]{1,0:T(8,128)(2,1)}, u32[]{:S(2)}) copy-start(bf16[128,384]{1,0:T(8,128)(2,1)} %constant.63.clone.left_ref) | copy-start | bytes 294916
  66.8 20.4 %copy-start.5 = (f32[128,128]{1,0:T(8,128)S(1)}, f32[128,128]{1,0:T(8,128)}, u32[]{:S(2)}) copy-start(f32[128,128]{1,0:T(8,128)} %constant.69.clone.fold_x_ref) | copy-start | bytes 196612
  66.8 20.4 %copy-start.6 = (f32[1,128]{1,0:T(1,128)S(1)}, f32[1,128]{1,0:T(1,128)}, u32[]{:S(2)}) copy-start(f32[1,128]{1,0:T(1,128)} %constant.70.clone.fold_z_ref) | copy-start | bytes 1540
  66.8 20.4 %all-to-all-start.2 = ((s16[8,36,16,128]{3,2,1,0:T(8,128)(2,1)}), s16[8,36,16,128]{3,2,1,0:T(8,128)(2,1)S(1)}, u32[]{:S(2)}, u32[]{:S(2)}) async-start(s16[8,36,16,128]{3,2,1,0:T(8,128)(2,1)} %density.1), calls=%async_computation.2 | async-start | bytes 2359296 | tf_op jit(solution)/shard_map/all_to_all | solution.py:338
  92.4 17.0 %copy-start.2 = (bf16[128,384]{1,0:T(8,128)(2,1)S(1)}, bf16[128,384]{1,0:T(8,128)(2,1)}, u32[]{:S(2)}) copy-start(bf16[128,384]{1,0:T(8,128)(2,1)} %constant.65.clone.left_ref) | copy-start | bytes 294916
  111.5 13.6 %collective-permute-start.2 = (s16[2064,128]{1,0:T(8,128)(2,1)S(1)}, s16[2064,128]{1,0:T(8,128)(2,1)S(1)}, u32[]{:S(2)}, u32[]{:S(2)}) collective-permute-start(s16[2064,128]{1,0:T(8,128)(2,1)S(1)} %get-tuple-element.8), channel_id=1, source_target_pairs={{120,0},{0,8},{8,16},{16,24},{24,32},{32,40},{40,48},{48,56},{56,6... | collective-permute-start | bytes 1585160 | tf_op jit(solution)/shard_map/ppermute | solution.py:278
where the time goes:
time: 127 us; the launch traced here: 126 us
  waiting for transfers between devices  33.2 us (26%)
  starting transfers between devices  31.7 us (25%)
  Pallas kernels  30.6 us (24%)
  blocking collectives  16.9 us (13%)
  local copies, waits for them, and re-layouts  10.9 us (9%)
  other arithmetic  2.6 us (2%)
    pallas_call x1, Pallas kernels, per_device(): call(density_kernel, [smem(), smem()] + [vmem()] * 5, jax.ShapeDtypeStruc...  18.3 us
    all_to_all x1, blocking collectives, per_device(): lax.all_to_all(columns, 'slab', split_axis=0, concat_axis=0, tiled=True)  16.9 us
    all_to_all x1, waiting for transfers between devices, per_device(): lax.all_to_all(spectrum, 'slab', split_axis=0, concat_axis=0, tiled=True)  16 us
    all_to_all x1, waiting for transfers between devices, per_device(): lax.all_to_all(charges, ('band', 'slab'), split_axis=0, concat_axis=0, ti...  13.1 us
    all_to_all x1, starting transfers between devices, per_device(): lax.all_to_all(charges, ('band', 'slab'), split_axis=0, concat_axis=0, ti...  9.97 us
    ppermute x3, starting transfers between devices, from_behind(): lax.ppermute(block, axis, [((i - distance) % count, i) for i in range(cou...  9.11 us
    all_to_all x1, starting transfers between devices, per_device(): lax.all_to_all(mine, 'band', split_axis=0, concat_axis=0, tiled=True)  8.89 us
    pallas_call x1, Pallas kernels, per_device(): call(solve_kernel, [smem()] + [vmem()] * 4, jax.ShapeDtypeStruct((n_slab,...  5.25 us
  transfers between devices with their start and end apart: 6, of which 3 were waited for; matrix products, arithmetic and copies ran while one was open for 10% of the time, Pallas kernels for 3%

commit v1 on v0

v1 whole, which is shorter than its diff:
```python
import functools
import math

import numpy as np
import jax
import jax.numpy as jnp
from jax import lax
from jax.experimental import pallas as pl
from jax.experimental.pallas import tpu as pltpu
from jax.sharding import PartitionSpec as P

KERNEL_SCALE = 0.5
SCREENING_RANGE = 0.002
NG = 128
SLABS = 8
ROWS = NG // SLABS
PLANES = NG // SLABS
BLOCK_LIMIT = 3.0
QMAX = 32760.0
STEPS = 8.0
CHANNELS = 9
CHANNEL_ROWS = 16
FWD_TILES = PLANES + 2
BACK_TILES = PLANES + 1
BF = jnp.bfloat16
F32 = jnp.float32
VMEM_LIMIT = 50 * 1024 * 1024


def hartley_host():
    index = np.arange(NG)
    angle = (index[:, None] * index[None, :] % NG) * (2.0 * math.pi / NG)
    return (np.cos(angle) + np.sin(angle)).astype(np.float32)


def split_host(table):
    high = table.astype(jnp.bfloat16)
    low = (table - high.astype(np.float32)).astype(jnp.bfloat16)
    return high, low


def row_order():
    by_size = sorted(range(NG), key=lambda k: (min(k, NG - k), k))
    return np.array([[by_size[d + SLABS * r] for r in range(ROWS)] for d in range(SLABS)])


def fold_square_host():
    index = np.arange(NG)
    return ((np.minimum(index, NG - index)).astype(np.float32) * np.float32(2.0 * math.pi / NG)) ** 2


def tables():
    table = hartley_host()
    high, low = split_host(table)
    order = row_order().reshape(-1)
    high_y, low_y = high[order], low[order]
    top = np.concatenate([high, low], axis=1)
    bottom = np.concatenate([high, np.zeros_like(high)], axis=1)
    right = np.concatenate([top, bottom], axis=0)
    left = np.concatenate([high, low, high], axis=1)
    left_y = np.concatenate([high_y, low_y, high_y], axis=1)
    left_y_back = np.concatenate([high_y.T, low_y.T, high_y.T], axis=1)
    return right, left, left_y, left_y_back


def split(value):
    high = value.astype(BF)
    low = (value - high.astype(F32)).astype(BF)
    return high, low


def dot(a, b):
    return jnp.dot(a, b, preferred_element_type=F32)


def times_right(value, right_ref):
    high, low = split(value)
    both = dot(jnp.concatenate([high, low], axis=1), right_ref[...])
    return both[:, :NG] + both[:, NG:]


def times_left(left_ref, value):
    high, low = split(value)
    return dot(left_ref[...], jnp.concatenate([high, high, low], axis=0))


def step_code(largest):
    return jnp.ceil(jnp.log(jnp.maximum(largest, 1e-30)) * (STEPS / math.log(2.0)))


def step_size(code):
    return jnp.exp(code * (math.log(2.0) / STEPS)) * (1.001 / QMAX)


def to_int16(value):
    return value.astype(jnp.int32).astype(jnp.int16)


def from_int16(value):
    return value.astype(jnp.int32).astype(F32)


def block_kernel(block_ref, out_ref, rows, turned):
    lane = lax.broadcasted_iota(jnp.int32, (1, NG), 1) // 8
    atoms, bricks, channels = block_ref.shape[:3]
    rows[...] = jnp.zeros_like(rows)
    for k in range(bricks):
        for t in range(atoms):
            rows[k, pl.ds(CHANNEL_ROWS * t, channels), :] = block_ref[t, k].astype(F32)
    for k in range(bricks):
        values = rows[k]
        first = (k // 4) * 8 + (k // 2 % 2) * 2 + k % 2
        for back in range(12):
            moved = pltpu.roll(values, (first - back) % 16 * 8, 1)
            for x in range(2):
                y = back - 4 * x
                if 0 <= y < 8:
                    inside = lane == first + 4 * x
                    turned[y] = moved if k == 0 and x == 0 else jnp.where(inside, moved, turned[y])
    out_ref[...] = turned[...].astype(BF)


def message_kernel(proj_ref, out_ref, rows):
    rows[...] = jnp.zeros_like(rows)
    rows[pl.ds(0, proj_ref.shape[1]), :] = proj_ref[0].astype(F32)
    total = rows.shape[1]
    count = out_ref.shape[0]
    for b in range(count):
        moved = pltpu.roll(rows[...], (total - b * (total // count)) % total, 1)
        out_ref[b] = moved[:, :NG].astype(BF)


def charge_kernel(home_ref, proj_ref, block_ref, out_ref, held):
    slab = lax.axis_index("slab")
    owner = lax.axis_index("band") * SLABS + slab
    groups = proj_ref.shape[0]
    atoms = block_ref.shape[1] // CHANNEL_ROWS
    lane = lax.broadcasted_iota(jnp.int32, (CHANNEL_ROWS, NG), 1)
    weights = [jnp.zeros((CHANNEL_ROWS, NG), F32)] * atoms
    for b in range(groups):
        mine = pltpu.roll(proj_ref[b].astype(F32), (NG - slab * atoms) & (NG - 1), 1)
        for t in range(atoms):
            weights[t] = jnp.where(lane // SLABS == b, mine[:, t : t + 1], weights[t])
    pieces = []
    for t in range(atoms):
        goes = (lane & (SLABS - 1)) == home_ref[0, owner * atoms + t] // (PLANES // 2)
        behind = pltpu.roll(weights[t], NG - SLABS, 1)
        pairs = [jnp.where(goes, weights[t] * other, 0.0) for other in (weights[t], behind)]
        pieces.append(jnp.concatenate(pairs, axis=1))
    weight = jnp.concatenate(pieces, axis=0)
    bound = jnp.sum(jnp.abs(weight), axis=0, keepdims=True) * BLOCK_LIMIT
    weight = jnp.transpose(weight * (QMAX / jnp.maximum(bound, 1e-30)))
    both = jnp.concatenate(split(weight), axis=1)
    for y in range(8):
        held[:, y, :] = dot(both, jnp.concatenate([block_ref[y], block_ref[y]], axis=0))
    half = weight.shape[0] // 2
    both_pairs = jnp.concatenate([held[:half], held[half:]], axis=1)
    out_ref[...] = to_int16(jnp.round(both_pairs))


def mark_kernel(in_ref, out_ref):
    out_ref[...] = jnp.zeros_like(out_ref)


def density_kernel(p, home_ref, here_ref, charge_ref, own_ref, next_ref, right_ref, left_ref, out_ref, field, scales):
    rows, owners = here_ref.shape[0], charge_ref.shape[0]
    proj = pl.ds(PLANES * NG, own_ref.shape[0] - PLANES * NG)
    sizes = jnp.abs(own_ref[proj, :].astype(F32) * next_ref[proj, :].astype(F32))
    bound = sizes[:rows]
    for c in range(1, CHANNELS):
        bound = bound + sizes[c * rows : (c + 1) * rows]
    bound = bound * here_ref[...] * (BLOCK_LIMIT / QMAX)
    count = owners // rows
    wide = lax.broadcasted_iota(jnp.int32, (count, NG), 1) // (NG // count)
    own_lane = wide == lax.broadcasted_iota(jnp.int32, (count, NG), 0)
    for r in range(rows):
        picked = jnp.where(own_lane, bound[r : r + 1], 0.0)
        total = jnp.sum(picked, axis=1, keepdims=True)
        scales[pl.ds(r * count, count), :] = jnp.broadcast_to(total, (count, NG))
    for x in range(PLANES):
        plane = pl.ds(x * NG, NG)
        field[x] = own_ref[plane, :].astype(F32) * next_ref[plane, :].astype(F32)
    lane = lax.broadcasted_iota(jnp.int32, (8, NG), 1)

    def add_atom(d, carry):
        plane = home_ref[0, d]
        brick_y = home_ref[1, d]
        shift = home_ref[2, d] * 8
        inside = ((lane - shift) & (NG - 1)) < 16
        places = []
        tile = from_int16(charge_ref[d])[8 * p : 8 * p + 8] * scales[pl.ds(d, 1), :]
        for g in range(8):
            turned = pltpu.roll(tile, (shift + (NG - 16 * g)) & (NG - 1), 1)
            row = pl.multiple_of(((brick_y + g % 2) & (NG // 8 - 1)) * 8, 8)
            at = (plane + g // 2, pl.ds(row, 8))
            places.append((at, field[at] + jnp.where(inside, turned, 0.0)))
        for at, total in places:
            field[at] = total
        return carry

    lax.fori_loop(0, charge_ref.shape[0], add_atom, 0, unroll=32)
    for x in range(0, PLANES, 2):
        both = times_right(jnp.concatenate([field[x], field[x + 1]], axis=0), right_ref)
        both = times_left(left_ref, jnp.concatenate([both[:NG], both[NG:]], axis=1))
        field[x] = both[:, :NG]
        field[x + 1] = both[:, NG:]

    def pack(d, carry):
        rows = pl.ds(pl.multiple_of(d * ROWS, ROWS), ROWS)
        largest = jnp.abs(field[0, rows])
        for x in range(1, PLANES):
            largest = jnp.maximum(largest, jnp.abs(field[x, rows]))
        code = step_code(largest)
        factor = 1.0 / step_size(code)
        lows = []
        for x in range(PLANES):
            scaled = field[x, rows] * factor
            whole = jnp.round(scaled)
            out_ref[d, x] = to_int16(whole)
            lows.append((scaled - whole)[0:1])
        out_ref[d, PLANES] = to_int16(code)
        low = jnp.concatenate(lows, axis=0) * (2.0 * QMAX)
        out_ref[d, PLANES + 1] = to_int16(jnp.round(low))
        return carry

    lax.fori_loop(0, SLABS, pack, 0, unroll=True)


def solve_kernel(square_ref, in_ref, fold_x_ref, fold_z_ref, left_ref, out_ref, field):
    def unpack(s, carry):
        step = step_size(from_int16(in_ref[s, PLANES]))
        for x in range(PLANES):
            field[s * PLANES + x] = from_int16(in_ref[s, x]) * step
        low = from_int16(in_ref[s, PLANES + 1]) * (step[0:1] * (0.5 / QMAX))
        planes = pl.ds(s * PLANES, PLANES)
        field[planes, 0, :] = field[planes, 0, :] + low
        return carry

    lax.fori_loop(0, SLABS, unpack, 0, unroll=True)
    fold = fold_x_ref[...] + fold_z_ref[...]
    for r in range(0, ROWS, 2):
        halves = []
        for k in range(2):
            total = fold + square_ref[r + k]
            halves.append(jnp.where(total > 0, KERNEL_SCALE / (total + SCREENING_RANGE), 0.0) * (1.0 / NG**3))
        columns = jnp.concatenate([field[:, r, :], field[:, r + 1, :]], axis=1)
        spectrum = times_left(left_ref, columns) * jnp.concatenate(halves, axis=1)
        columns = times_left(left_ref, spectrum)
        field[:, r, :] = columns[:, :NG]
        field[:, r + 1, :] = columns[:, NG:]

    def pack(s, carry):
        largest = jnp.abs(field[s * PLANES])
        for x in range(1, PLANES):
            largest = jnp.maximum(largest, jnp.abs(field[s * PLANES + x]))
        code = step_code(largest)
        factor = 1.0 / step_size(code)
        for x in range(PLANES):
            out_ref[s, x] = to_int16(jnp.round(field[s * PLANES + x] * factor))
        out_ref[s, PLANES] = to_int16(code)
        return carry

    lax.fori_loop(0, SLABS, pack, 0, unroll=True)


def potential_pair(in_ref, steps, x, left_ref, right_ref):
    halves = []
    for k in range(2):
        halves.append(jnp.concatenate([from_int16(in_ref[s, x + k]) * steps[s] for s in range(SLABS)], axis=0))
    both = times_left(left_ref, jnp.concatenate(halves, axis=1))
    both = times_right(jnp.concatenate([both[:, :NG], both[:, NG:]], axis=0), right_ref)
    return both[:NG], both[NG:]


def back_cross_kernel(in_ref, own_ref, next_ref, left_ref, right_ref, kept_ref, sent_ref, codes):
    steps = [step_size(from_int16(in_ref[s, PLANES])) for s in range(SLABS)]
    for x in range(0, PLANES, 2):
        pair = potential_pair(in_ref, steps, x, left_ref, right_ref)
        for k in range(2):
            potential = pair[k]
            kept_ref[x + k] = potential * next_ref[pl.ds((x + k) * NG, NG), :].astype(F32)
            product = potential * own_ref[pl.ds((x + k) * NG, NG), :].astype(F32)
            code = step_code(jnp.max(jnp.abs(product), axis=0, keepdims=True))
            codes[x + k : x + k + 1, :] = code
            sent_ref[pl.ds((x + k) * NG, NG), :] = to_int16(jnp.round(product * (1.0 / step_size(code))))
    sent_ref[pl.ds(PLANES * NG, PLANES), :] = to_int16(codes[...])


def back_own_kernel(in_ref, own_ref, kept_ref, sent_ref, left_ref, right_ref, out_ref):
    steps = [step_size(from_int16(in_ref[s, PLANES])) for s in range(SLABS)]
    sent_steps = step_size(from_int16(sent_ref[pl.ds(PLANES * NG, PLANES), :]))
    for x in range(0, PLANES, 2):
        pair = potential_pair(in_ref, steps, x, left_ref, right_ref)
        for k in range(2):
            sent = from_int16(sent_ref[pl.ds((x + k) * NG, NG), :]) * sent_steps[x + k : x + k + 1]
            out_ref[0, x + k] = kept_ref[x + k] + sent + pair[k] * own_ref[pl.ds((x + k) * NG, NG), :].astype(F32)


def vmem():
    return pl.BlockSpec(memory_space=pltpu.VMEM)


def smem():
    return pl.BlockSpec(memory_space=pltpu.SMEM)


def call(kernel, in_specs, out_shape, scratch, name, micros):
    many = isinstance(out_shape, (list, tuple))
    return pl.pallas_call(
        kernel,
        in_specs=in_specs,
        out_specs=[vmem() for _ in out_shape] if many else vmem(),
        out_shape=out_shape,
        scratch_shapes=scratch,
        name=name,
        cost_estimate=pl.CostEstimate(
            flops=int(micros * 1e8), bytes_accessed=int(micros * 3.5e6), transcendentals=0
        ),
        compiler_params=pltpu.CompilerParams(vmem_limit_bytes=VMEM_LIMIT),
    )


def mark(array):
    whole = [pl.BlockSpec(memory_space=pl.ANY)]
    return call(mark_kernel, whole, jax.ShapeDtypeStruct((8, NG), F32), [], "mark", 30)(array)


def from_behind(block, axis, distance):
    count = lax.axis_size(axis)
    return lax.ppermute(block, axis, [((i - distance) % count, i) for i in range(count)])


def per_device(orbitals, projections, aug_blocks, atom_home):
    n_band = lax.axis_size("band")
    n_slab = lax.axis_size("slab")
    owners = n_band * n_slab
    atom_dev = aug_blocks.shape[0]
    channels = projections.shape[1]
    slab_bricks = PLANES // 2
    my_slab = lax.axis_index("slab")
    right, left, left_y, left_y_back = (jnp.asarray(t) for t in tables())
    squares = fold_square_host()
    fold_rows = jnp.asarray(squares[row_order()])

    own = orbitals[0]
    own_proj = projections[0]

    messages = call(
        message_kernel,
        [vmem()],
        jax.ShapeDtypeStruct((n_band, CHANNEL_ROWS, NG), BF),
        [pltpu.VMEM((CHANNEL_ROWS, projections.shape[2]), F32)],
        "messages",
        1,
    )(projections)
    messages, late_blocks = lax.optimization_barrier((messages, aug_blocks))
    all_proj = lax.all_to_all(messages, "band", split_axis=0, concat_axis=0, tiled=True)

    slab_of = (atom_home[0] // slab_bricks).reshape(owners, atom_dev)
    here = slab_of == my_slab
    home = atom_home.reshape(3, owners, atom_dev)
    home = home - jnp.array([1, 0, 0], jnp.int32)[:, None, None] * (my_slab * slab_bricks)
    home = jnp.sum(jnp.where(here[None], home, 0), axis=2) * jnp.array([2, 1, 1], jnp.int32)[:, None]

    blocks = call(
        block_kernel,
        [vmem()],
        jax.ShapeDtypeStruct((8, atom_dev * CHANNEL_ROWS, NG), BF),
        [pltpu.VMEM((8, atom_dev * CHANNEL_ROWS, NG), F32)] * 2,
        "blocks",
        1,
    )(late_blocks)
    wide_proj = own_proj.reshape(-1, NG)
    fill = jnp.zeros((-wide_proj.shape[0] % 16, NG), BF)
    both = jnp.concatenate([own.reshape(-1, NG), wide_proj, fill], axis=0)
    here = here.astype(F32).reshape(-1, NG)
    both, home, here, blocks = lax.optimization_barrier((both, home, here, blocks))
    nxt = from_behind(both, "band", -1)

    charges = call(
        charge_kernel,
        [smem()] + [vmem()] * 2,
        jax.ShapeDtypeStruct((owners, 16, NG), jnp.int16),
        [pltpu.VMEM((2 * owners, 8, NG), F32)],
        "charges",
        2,
    )(atom_home, all_proj, blocks)
    charges = lax.all_to_all(charges, ("band", "slab"), split_axis=0, concat_axis=0, tiled=True)

    fold_y = lax.dynamic_index_in_dim(fold_rows, my_slab, 0, keepdims=False)
    fold_x = jnp.asarray(np.broadcast_to(squares[:, None], (NG, NG)).copy())
    fold_z = jnp.asarray(squares[None, :])

    def density(p, other):
        return call(
            functools.partial(density_kernel, p),
            [smem()] + [vmem()] * 6,
            jax.ShapeDtypeStruct((n_slab, FWD_TILES, 16, NG), jnp.int16),
            [pltpu.VMEM((PLANES, NG, NG), F32), pltpu.VMEM((owners, NG), F32)],
            "density" + str(p),
            6,
        )(home, here, charges, both, other, right, left_y)

    def solve(p, spectrum):
        return call(
            solve_kernel,
            [smem()] + [vmem()] * 4,
            jax.ShapeDtypeStruct((n_slab, BACK_TILES, 16, NG), jnp.int16),
            [pltpu.VMEM((NG, ROWS, NG), F32)],
            "solve" + str(p),
            3,
        )(fold_y, spectrum, fold_x, fold_z, left)

    def swap(block):
        return lax.all_to_all(block, "slab", split_axis=0, concat_axis=0, tiled=True)

    cross = swap(density(1, nxt))
    mine = density(0, both)
    cross, mine = lax.optimization_barrier((cross, mine))
    mine = swap(mine)
    cross = solve(1, cross)
    cross, mine = lax.optimization_barrier((cross, mine))
    cross = swap(cross)
    mine = solve(0, mine)
    cross, mine = lax.optimization_barrier((cross, mine))
    mine = swap(mine)

    kept, sent = call(
        back_cross_kernel,
        [vmem()] * 5,
        [
            jax.ShapeDtypeStruct((PLANES, NG, NG), F32),
            jax.ShapeDtypeStruct((PLANES * NG + PLANES, NG), jnp.int16),
        ],
        [pltpu.VMEM((PLANES, NG), F32)],
        "back_cross",
        2,
    )(cross, both, nxt, left_y_back, right)
    got = from_behind(sent, "band", 1)
    got, _ = lax.optimization_barrier((got, mark(mine)))
    return call(
        back_own_kernel,
        [vmem()] * 6,
        jax.ShapeDtypeStruct((1, PLANES, NG, NG), F32),
        [],
        "back_own",
        2,
    )(mine, both, kept, got, left_y_back, right)


def solution(mesh):
    in_specs = (
        P("band", "slab", None, None),
        P("band", None, None),
        P(("band", "slab"), None, None, None),
        P(),
    )
    out_specs = P("band", "slab", None, None)
    return jax.shard_map(
        per_device, mesh=mesh, in_specs=in_specs, out_specs=out_specs, check_vma=False
    )
```

time: 127 us -> 105 us (0.83)
  blocking collectives: 16.9 us -> 0 us
  waiting for transfers between devices: 33.2 us -> 42.1 us
  local copies, waits for them, and re-layouts: 10.9 us -> 2.7 us
  Pallas kernels: 30.6 us -> 22.8 us
  starting transfers between devices: 31.7 us -> 35.9 us
  other arithmetic: 2.6 us -> 0.36 us
    all_to_all x1 -> x0, blocking collectives: 16.9 us -> none  [per_device(): lax.all_to_all(columns, 'slab', split_axis=0, concat_axis=0, tiled=True)]
    all_to_all x2 -> x5, starting transfers between devices: 12.6 us -> 24.6 us  [the longest x4 15.3 us: swap(): lax.all_to_all(block, 'slab', split_axis=0, concat_axis=0, tiled=True)]
    pallas_call x5 -> x8, Pallas kernels: 28.5 us -> 21.8 us  [the longest x2 8.79 us: density(): call(functools.partial(density_kernel, p), [smem()] + [vmem()] * 6, jax.S...]
    reshape x4 -> x0, local copies, waits for them, and re-layouts: 6.68 us -> none  [the longest x2 3.44 us: per_device(): blocks.transpose(6, 0, 4, 1, 5, 2, 3, 7).reshape(8, atom_dev * channels, NG)]
    all_to_all x2 -> x5, waiting for transfers between devices: 16 us -> 20.8 us  [the longest x4 15.8 us: swap(): lax.all_to_all(block, 'slab', split_axis=0, concat_axis=0, tiled=True)]
    all_to_all x1, starting transfers between devices: 9.97 us -> 5.56 us  [per_device(): lax.all_to_all(charges, ('band', 'slab'), split_axis=0, concat_axis=0, ti...]
    ppermute x3 -> x2, waiting for transfers between devices: 4.16 us -> 7.85 us  [from_behind(): lax.ppermute(block, axis, [((i - distance) % count, i) for i in range(cou...]
    ppermute x3 -> x2, starting transfers between devices: 9.11 us -> 5.8 us  [from_behind(): lax.ppermute(block, axis, [((i - distance) % count, i) for i in range(cou...]
  transfers between devices with their start and end apart: 6 -> 8, of which waited for: 3 -> 7; matrix products, arithmetic and copies ran while one was open for 10% -> 2% of each run, Pallas kernels for 3% -> 14%
where the time goes in v1:
time: 105 us; the launch traced here: 104 us
  waiting for transfers between devices  42.1 us (40%)
  starting transfers between devices  35.9 us (34%)
  Pallas kernels  22.8 us (22%)
  local copies, waits for them, and re-layouts  2.7 us (3%)
    all_to_all x4, waiting for transfers between devices, swap(): lax.all_to_all(block, 'slab', split_axis=0, concat_axis=0, tiled=True)  15.8 us
    all_to_all x4, starting transfers between devices, swap(): lax.all_to_all(block, 'slab', split_axis=0, concat_axis=0, tiled=True)  15.3 us
    all_to_all x1, waiting for transfers between devices, per_device(): lax.all_to_all(charges, ('band', 'slab'), split_axis=0, concat_axis=0, ti...  13.4 us
    all_to_all x1, starting transfers between devices, per_device(): lax.all_to_all(messages, 'band', split_axis=0, concat_axis=0, tiled=True)  9.26 us
    pallas_call x2, Pallas kernels, density(): call(functools.partial(density_kernel, p), [smem()] + [vmem()] * 6, jax.S...  8.79 us
    ppermute x2, waiting for transfers between devices, from_behind(): lax.ppermute(block, axis, [((i - distance) % count, i) for i in range(cou...  7.85 us
    pallas_call x2, Pallas kernels, solve(): call(solve_kernel, [smem()] + [vmem()] * 4, jax.ShapeDtypeStruct((n_slab,...  7.04 us
    ppermute x2, starting transfers between devices, from_behind(): lax.ppermute(block, axis, [((i - distance) % count, i) for i in range(cou...  5.8 us
  transfers between devices with their start and end apart: 8, of which 7 were waited for; matrix products, arithmetic and copies ran while one was open for 2% of the time, Pallas kernels for 14%

profile of v1, /device:TPU:1, one launch (start us, length us, event | category | flops | bytes accessed | tf_op | source)
XLA Modules:
  0.0 104.1 jit_solution(11846524094811748658)
XLA Ops:
  0.0 0.7 copy-done.5
  0.7 0.7 messages.1
  1.5 9.3 %all-to-all-start = ((bf16[16,16,128]{2,1,0:T(8,128)(2,1)}), bf16[16,16,128]{2,1,0:T(8,128)(2,1)S(1)}, u32[]{:S(2)}, u32[]{:S(2)}) async-start(bf16[16,16,128]{2,1,0:T(8,128)(2,1)} %messages.1), calls=%async_computation | async-start | bytes 131072 | tf_op jit(solution)/shard_map/all_to_all | solution.py:357
  10.7 0.2 reshape.39
  11.0 0.1 squeeze.10
  11.2 0.2 select_reduce_fusion
  11.4 0.4 copy-done.11
  11.9 0.1 copy-done.10
  12.1 0.3 concatenate.3.own_ref.next_ref
  12.4 0.5 blocks.1.block_ref
  12.9 0.2 collective-permute-start
  13.1 5.0 %all-to-all-done.proj_ref = bf16[16,16,128]{2,1,0:T(8,128)(2,1)S(1)} async-done(((bf16[16,16,128]{2,1,0:T(8,128)(2,1)}), bf16[16,16,128]{2,1,0:T(8,128)(2,1)S(1)}, u32[]{:S(2)}, u32[]{:S(2)}) %all-to-all-start) | async-done | bytes 65568 | tf_op jit(solution)/shard_map/all_to_all | solution.py:357
  18.1 2.8 %charges.1 = s16[128,16,128]{2,1,0:T(8,128)(2,1)} custom-call(s32[3,512]{1,0:T(4,128)S(1)} %copy-done.7, bf16[16,16,128]{2,1,0:T(8,128)(2,1)S(1)} %all-to-all-done.proj_ref, bf16[8,64,128]{2,1,0:T(8,128)(2,1)S(1)} %blocks.1.block_ref), custom_call_target="tpu_custom_call" | custom-call | flops 200000000 | bytes 7000000 | tf_op jit(solution)/shard_map/charges/pallas_call | solution.py:380
  20.9 5.6 %all-to-all-start.1 = ((s16[128,16,128]{2,1,0:T(8,128)(2,1)}), s16[128,16,128]{2,1,0:T(8,128)(2,1)S(1)}, u32[]{:S(2)}, u32[]{:S(2)}) async-start(s16[128,16,128]{2,1,0:T(8,128)(2,1)} %charges.1), calls=%async_computation.1 | async-start | bytes 1048576 | tf_op jit(solution)/shard_map/all_to_all | solution.py:388
  26.5 13.4 %all-to-all-done.1.charge_ref = s16[128,16,128]{2,1,0:T(8,128)(2,1)S(1)} async-done(((s16[128,16,128]{2,1,0:T(8,128)(2,1)}), s16[128,16,128]{2,1,0:T(8,128)(2,1)S(1)}, u32[]{:S(2)}, u32[]{:S(2)}) %all-to-all-start.1) | async-done | bytes 524320 | tf_op jit(solution)/shard_map/all_to_all | solution.py:388
  39.9 4.4 %density1.1 = s16[8,18,16,128]{3,2,1,0:T(8,128)(2,1)} custom-call(s32[3,128]{1,0:T(4,128)S(1)} %broadcast_multiply_fusion.home_ref, f32[4,128]{1,0:T(4,128)S(1)} %fusion.6.here_ref, s16[128,16,128]{2,1,0:T(8,128)(2,1)S(1)} %all-to-all-done.1.charge_ref, bf16[2096,128]{1,0:T(8,128)(2,1)S(1)} %concatenate.3.own_ref.next_ref, ...), custom_call_target="tpu_custom_call" | custom-call | flops 600000000 | bytes 21000000 | tf_op jit(solution)/shard_map/density1/pallas_call | solution.py:395
  44.3 3.5 %all-to-all-start.2 = ((s16[8,18,16,128]{3,2,1,0:T(8,128)(2,1)}), s16[8,18,16,128]{3,2,1,0:T(8,128)(2,1)S(1)}, u32[]{:S(2)}, u32[]{:S(2)}) async-start(s16[8,18,16,128]{3,2,1,0:T(8,128)(2,1)} %density1.1), calls=%async_computation.2 | async-start | bytes 1179648 | tf_op jit(solution)/shard_map/all_to_all | solution.py:415
  47.8 4.4 %density0.1 = s16[8,18,16,128]{3,2,1,0:T(8,128)(2,1)} custom-call(s32[3,128]{1,0:T(4,128)S(1)} %broadcast_multiply_fusion.home_ref, f32[4,128]{1,0:T(4,128)S(1)} %fusion.6.here_ref, s16[128,16,128]{2,1,0:T(8,128)(2,1)S(1)} %all-to-all-done.1.charge_ref, bf16[2096,128]{1,0:T(8,128)(2,1)S(1)} %concatenate.3.own_ref.next_ref, ...), custom_call_target="tpu_custom_call" | custom-call | flops 600000000 | bytes 21000000 | tf_op jit(solution)/shard_map/density0/pallas_call | solution.py:395
  52.2 4.8 %all-to-all-done.2.in_ref = s16[8,18,16,128]{3,2,1,0:T(8,128)(2,1)S(1)} async-done(((s16[8,18,16,128]{3,2,1,0:T(8,128)(2,1)}), s16[8,18,16,128]{3,2,1,0:T(8,128)(2,1)S(1)}, u32[]{:S(2)}, u32[]{:S(2)}) %all-to-all-start.2) | async-done | bytes 589856 | tf_op jit(solution)/shard_map/all_to_all | solution.py:415
  57.0 3.8 %all-to-all-start.3 = ((s16[8,18,16,128]{3,2,1,0:T(8,128)(2,1)}), s16[8,18,16,128]{3,2,1,0:T(8,128)(2,1)S(1)}, u32[]{:S(2)}, u32[]{:S(2)}) async-start(s16[8,18,16,128]{3,2,1,0:T(8,128)(2,1)} %density0.1), calls=%async_computation.3 | async-start | bytes 1179648 | tf_op jit(solution)/shard_map/all_to_all | solution.py:415
  60.8 0.7 dynamic-slice_bitcast_fusion.square_ref
  61.5 3.5 %solve1.1 = s16[8,17,16,128]{3,2,1,0:T(8,128)(2,1)} custom-call(f32[16]{0:T(128)S(1)} %dynamic-slice_bitcast_fusion.square_ref, s16[8,18,16,128]{3,2,1,0:T(8,128)(2,1)S(1)} %all-to-all-done.2.in_ref, f32[128,128]{1,0:T(8,128)S(1)} %copy-done.4, f32[1,128]{1,0:T(1,128)S(1)} %copy-done.8, bf16[128,384]{1,0:T(8,128)(2,1)S(1)} %copy-done.3), custom_call_target="tpu_custom_call" | custom-call | flops 300000000 | bytes 10500000 | tf_op jit(solution)/shard_map/solve1/pallas_call | solution.py:405
  65.1 4.5 %all-to-all-done.3.in_ref = s16[8,18,16,128]{3,2,1,0:T(8,128)(2,1)S(1)} async-done(((s16[8,18,16,128]{3,2,1,0:T(8,128)(2,1)}), s16[8,18,16,128]{3,2,1,0:T(8,128)(2,1)S(1)}, u32[]{:S(2)}, u32[]{:S(2)}) %all-to-all-start.3) | async-done | bytes 589856 | tf_op jit(solution)/shard_map/all_to_all | solution.py:415
  69.5 4.4 %all-to-all-start.4 = ((s16[8,17,16,128]{3,2,1,0:T(8,128)(2,1)}), s16[8,17,16,128]{3,2,1,0:T(8,128)(2,1)S(1)}, u32[]{:S(2)}, u32[]{:S(2)}) async-start(s16[8,17,16,128]{3,2,1,0:T(8,128)(2,1)} %solve1.1), calls=%async_computation.4 | async-start | bytes 1114112 | tf_op jit(solution)/shard_map/all_to_all | solution.py:415
  73.9 3.5 %solve0.1 = s16[8,17,16,128]{3,2,1,0:T(8,128)(2,1)} custom-call(f32[16]{0:T(128)S(1)} %dynamic-slice_bitcast_fusion.square_ref, s16[8,18,16,128]{3,2,1,0:T(8,128)(2,1)S(1)} %all-to-all-done.3.in_ref, f32[128,128]{1,0:T(8,128)S(1)} %copy-done.4, f32[1,128]{1,0:T(1,128)S(1)} %copy-done.8, bf16[128,384]{1,0:T(8,128)(2,1)S(1)} %copy-done.3), custom_call_target="tpu_custom_call" | custom-call | flops 300000000 | bytes 10500000 | tf_op jit(solution)/shard_map/solve0/pallas_call | solution.py:405
  77.4 4.8 %all-to-all-done.4.in_ref = s16[8,17,16,128]{3,2,1,0:T(8,128)(2,1)S(1)} async-done(((s16[8,17,16,128]{3,2,1,0:T(8,128)(2,1)}), s16[8,17,16,128]{3,2,1,0:T(8,128)(2,1)S(1)}, u32[]{:S(2)}, u32[]{:S(2)}) %all-to-all-start.4) | async-done | bytes 557088 | tf_op jit(solution)/shard_map/all_to_all | solution.py:415
  82.3 1.0 %back_cross.1 = (f32[16,128,128]{2,1,0:T(8,128)S(1)}, s16[2064,128]{1,0:T(8,128)(2,1)S(1)}) custom-call(s16[8,17,16,128]{3,2,1,0:T(8,128)(2,1)S(1)} %all-to-all-done.4.in_ref, bf16[2096,128]{1,0:T(8,128)(2,1)S(1)} %concatenate.3.own_ref.next_ref, bf16[2096,128]{1,0:T(8,128)(2,1)S(1)} %collective-permute-done.next_ref, bf16[128,384]{1,0:T(8,128)(2,1)S(1)} %copy-done.2, ...), custom_call_target="tpu_custom_call" | custom-call | flops 200000000 | bytes 7000000 | tf_op jit(solution)/shard_map/back_cross/pallas_call | solution.py:428
  83.3 5.6 %collective-permute-start.1 = (s16[2064,128]{1,0:T(8,128)(2,1)S(1)}, s16[2064,128]{1,0:T(8,128)(2,1)S(1)}, u32[]{:S(2)}, u32[]{:S(2)}) collective-permute-start(s16[2064,128]{1,0:T(8,128)(2,1)S(1)} %get-tuple-element.32), channel_id=1, source_target_pairs={{120,0},{0,8},{8,16},{16,24},{24,32},{32,40},{40,48},{48,56},{56,6... | collective-permute-start | bytes 1585160 | tf_op jit(solution)/shard_map/ppermute | solution.py:330
  89.0 3.5 %all-to-all-start.5 = ((s16[8,17,16,128]{3,2,1,0:T(8,128)(2,1)}), s16[8,17,16,128]{3,2,1,0:T(8,128)(2,1)S(1)}, u32[]{:S(2)}, u32[]{:S(2)}) async-start(s16[8,17,16,128]{3,2,1,0:T(8,128)(2,1)} %solve0.1), calls=%async_computation.5 | async-start | bytes 1114112 | tf_op jit(solution)/shard_map/all_to_all | solution.py:415
  92.5 7.8 %collective-permute-done.1.sent_ref = s16[2064,128]{1,0:T(8,128)(2,1)S(1)} collective-permute-done((s16[2064,128]{1,0:T(8,128)(2,1)S(1)}, s16[2064,128]{1,0:T(8,128)(2,1)S(1)}, u32[]{:S(2)}, u32[]{:S(2)}) %collective-permute-start.1) | collective-permute-done | bytes 528416 | tf_op jit(solution)/shard_map/ppermute | solution.py:330
  100.4 1.8 %all-to-all-done.5.in_ref = s16[8,17,16,128]{3,2,1,0:T(8,128)(2,1)S(1)} async-done(((s16[8,17,16,128]{3,2,1,0:T(8,128)(2,1)}), s16[8,17,16,128]{3,2,1,0:T(8,128)(2,1)S(1)}, u32[]{:S(2)}, u32[]{:S(2)}) %all-to-all-start.5) | async-done | bytes 557088 | tf_op jit(solution)/shard_map/all_to_all | solution.py:415
  102.1 1.9 %back_own.1 = f32[1,16,128,128]{3,2,1,0:T(8,128)} custom-call(s16[8,17,16,128]{3,2,1,0:T(8,128)(2,1)S(1)} %all-to-all-done.5.in_ref, bf16[2096,128]{1,0:T(8,128)(2,1)S(1)} %concatenate.3.own_ref.next_ref, f32[16,128,128]{2,1,0:T(8,128)S(1)} %get-tuple-element.31.kept_ref, s16[2064,128]{1,0:T(8,128)(2,1)S(1)} %collective-permute-done.1.sent_ref, ...), custom_call_target="tpu_custom_call" | custom-call | flops 200000000 | bytes 7000000 | tf_op jit(solution)/shard_map/back_own/pallas_call | solution.py:441
  (32 shorter events, 0.3 us)
Async XLA Ops:
  0.0 0.7 copy-start.5
  0.7 10.4 %copy-start.12 = (s32[3]{0:T(128)S(1)}, s32[3]{0:T(128)}, u32[]{:S(2)}) copy-start(s32[3]{0:T(128)} %constant.51.clone) | copy-start | bytes 40
  1.5 9.3 %copy-start.7 = (s32[3,512]{1,0:T(4,128)S(1)}, s32[3,512]{1,0:T(4,128)}, u32[]{:S(2)}) copy-start(s32[3,512]{1,0:T(4,128)} %home_ref.1) | copy-start | bytes 18436
  1.5 10.7 %copy-start.9 = (bf16[1,16,128,128]{3,2,1,0:T(8,128)(2,1)S(1)}, bf16[1,16,128,128]{3,2,1,0:T(8,128)(2,1)}, u32[]{:S(2)}) copy-start(bf16[1,16,128,128]{3,2,1,0:T(8,128)(2,1)} %param.13) | copy-start | bytes 1572868
  1.5 16.6 %all-to-all-start = ((bf16[16,16,128]{2,1,0:T(8,128)(2,1)}), bf16[16,16,128]{2,1,0:T(8,128)(2,1)S(1)}, u32[]{:S(2)}, u32[]{:S(2)}) async-start(bf16[16,16,128]{2,1,0:T(8,128)(2,1)} %messages.1), calls=%async_computation | async-start | bytes 131072 | tf_op jit(solution)/shard_map/all_to_all | solution.py:357
  11.1 0.7 copy-start.11
  11.2 0.7 copy-start.6
  11.2 0.9 copy-start.10
  12.9 13.5 %collective-permute-start = (bf16[2096,128]{1,0:T(8,128)(2,1)S(1)}, bf16[2096,128]{1,0:T(8,128)(2,1)S(1)}, u32[]{:S(2)}, u32[]{:S(2)}) collective-permute-start(bf16[2096,128]{1,0:T(8,128)(2,1)S(1)} %concatenate.3.own_ref.next_ref), channel_id=1, source_target_pairs={{8,0},{16,8},{24,16},{32,24},{40,32},{48,40},{56,48},{64,56},{72,6... | collective-permute-start | bytes 1609736 | tf_op jit(solution)/shard_map/ppermute | solution.py:330
  20.9 19.0 %copy-start = (bf16[256,256]{1,0:T(8,128)(2,1)S(1)}, bf16[256,256]{1,0:T(8,128)(2,1)}, u32[]{:S(2)}) copy-start(bf16[256,256]{1,0:T(8,128)(2,1)} %constant.46.clone.right_ref) | copy-start | bytes 393220
  20.9 19.0 %copy-start.1 = (bf16[128,384]{1,0:T(8,128)(2,1)S(1)}, bf16[128,384]{1,0:T(8,128)(2,1)}, u32[]{:S(2)}) copy-start(bf16[128,384]{1,0:T(8,128)(2,1)} %constant.48.clone.left_ref) | copy-start | bytes 294916
  20.9 19.0 %all-to-all-start.1 = ((s16[128,16,128]{2,1,0:T(8,128)(2,1)}), s16[128,16,128]{2,1,0:T(8,128)(2,1)S(1)}, u32[]{:S(2)}, u32[]{:S(2)}) async-start(s16[128,16,128]{2,1,0:T(8,128)(2,1)} %charges.1), calls=%async_computation.1 | async-start | bytes 1048576 | tf_op jit(solution)/shard_map/all_to_all | solution.py:388
  44.3 12.7 %all-to-all-start.2 = ((s16[8,18,16,128]{3,2,1,0:T(8,128)(2,1)}), s16[8,18,16,128]{3,2,1,0:T(8,128)(2,1)S(1)}, u32[]{:S(2)}, u32[]{:S(2)}) async-start(s16[8,18,16,128]{3,2,1,0:T(8,128)(2,1)} %density1.1), calls=%async_computation.2 | async-start | bytes 1179648 | tf_op jit(solution)/shard_map/all_to_all | solution.py:415
  52.2 9.3 %copy-start.3 = (bf16[128,384]{1,0:T(8,128)(2,1)S(1)}, bf16[128,384]{1,0:T(8,128)(2,1)}, u32[]{:S(2)}) copy-start(bf16[128,384]{1,0:T(8,128)(2,1)} %constant.47.clone.left_ref) | copy-start | bytes 294916
  52.2 9.3 %copy-start.4 = (f32[128,128]{1,0:T(8,128)S(1)}, f32[128,128]{1,0:T(8,128)}, u32[]{:S(2)}) copy-start(f32[128,128]{1,0:T(8,128)} %constant.53.clone.fold_x_ref) | copy-start | bytes 196612
  57.0 12.5 %all-to-all-start.3 = ((s16[8,18,16,128]{3,2,1,0:T(8,128)(2,1)}), s16[8,18,16,128]{3,2,1,0:T(8,128)(2,1)S(1)}, u32[]{:S(2)}, u32[]{:S(2)}) async-start(s16[8,18,16,128]{3,2,1,0:T(8,128)(2,1)} %density0.1), calls=%async_computation.3 | async-start | bytes 1179648 | tf_op jit(solution)/shard_map/all_to_all | solution.py:415
  60.8 0.7 copy-start.8
  69.5 12.8 %all-to-all-start.4 = ((s16[8,17,16,128]{3,2,1,0:T(8,128)(2,1)}), s16[8,17,16,128]{3,2,1,0:T(8,128)(2,1)S(1)}, u32[]{:S(2)}, u32[]{:S(2)}) async-start(s16[8,17,16,128]{3,2,1,0:T(8,128)(2,1)} %solve1.1), calls=%async_computation.4 | async-start | bytes 1114112 | tf_op jit(solution)/shard_map/all_to_all | solution.py:415
  73.9 8.4 %copy-start.2 = (bf16[128,384]{1,0:T(8,128)(2,1)S(1)}, bf16[128,384]{1,0:T(8,128)(2,1)}, u32[]{:S(2)}) copy-start(bf16[128,384]{1,0:T(8,128)(2,1)} %constant.49.clone.left_ref) | copy-start | bytes 294916
  83.3 17.0 %collective-permute-start.1 = (s16[2064,128]{1,0:T(8,128)(2,1)S(1)}, s16[2064,128]{1,0:T(8,128)(2,1)S(1)}, u32[]{:S(2)}, u32[]{:S(2)}) collective-permute-start(s16[2064,128]{1,0:T(8,128)(2,1)S(1)} %get-tuple-element.32), channel_id=1, source_target_pairs={{120,0},{0,8},{8,16},{16,24},{24,32},{32,40},{40,48},{48,56},{56,6... | collective-permute-start | bytes 1585160 | tf_op jit(solution)/shard_map/ppermute | solution.py:330
  89.0 13.2 %all-to-all-start.5 = ((s16[8,17,16,128]{3,2,1,0:T(8,128)(2,1)}), s16[8,17,16,128]{3,2,1,0:T(8,128)(2,1)S(1)}, u32[]{:S(2)}, u32[]{:S(2)}) async-start(s16[8,17,16,128]{3,2,1,0:T(8,128)(2,1)} %solve0.1), calls=%async_computation.5 | async-start | bytes 1114112 | tf_op jit(solution)/shard_map/all_to_all | solution.py:415

commit v2 on v1

--- a/solution.py
+++ b/solution.py
@@ -18,7 +18,6 @@
 BLOCK_LIMIT = 3.0
 QMAX = 32760.0
 STEPS = 8.0
-CHANNELS = 9
 CHANNEL_ROWS = 16
 FWD_TILES = PLANES + 2
 BACK_TILES = PLANES + 1
@@ -100,13 +99,14 @@
     return value.astype(jnp.int32).astype(F32)
 
 
-def block_kernel(block_ref, out_ref, rows, turned):
+def local_kernel(after_ref, home_any, block_ref, out_ref, place_ref, here_ref, rows, turned, home_ref, sem):
+    fetch = pltpu.make_async_copy(home_any, home_ref, sem)
+    fetch.start()
     lane = lax.broadcasted_iota(jnp.int32, (1, NG), 1) // 8
-    atoms, bricks, channels = block_ref.shape[:3]
+    atoms, channels, bricks = block_ref.shape[:3]
     rows[...] = jnp.zeros_like(rows)
-    for k in range(bricks):
-        for t in range(atoms):
-            rows[k, pl.ds(CHANNEL_ROWS * t, channels), :] = block_ref[t, k].astype(F32)
+    for t in range(atoms):
+        rows[:, pl.ds(CHANNEL_ROWS * t, channels), :] = jnp.swapaxes(block_ref[t].astype(F32), 0, 1)
     for k in range(bricks):
         values = rows[k]
         first = (k // 4) * 8 + (k // 2 % 2) * 2 + k % 2
@@ -118,6 +118,20 @@
                     inside = lane == first + 4 * x
                     turned[y] = moved if k == 0 and x == 0 else jnp.where(inside, moved, turned[y])
     out_ref[...] = turned[...].astype(BF)
+    fetch.wait()
+    half = PLANES // 2
+    slab = lax.axis_index("slab")
+    here = home_ref[0:1, :] // half == slab
+    place = (home_ref[0:1, :] - slab * half) * 2 + 16 * home_ref[1:2, :] + 256 * home_ref[2:3, :]
+    place = jnp.where(here, place, 0)
+    here = jnp.where(here, BLOCK_LIMIT / QMAX, 0.0)
+    for r in range(place_ref.shape[0]):
+        part = place[:, r * NG : (r + 1) * NG]
+        total = part
+        for t in range(1, atoms):
+            total = total + pltpu.roll(part, NG - t, 1)
+        place_ref[r : r + 1, :] = total
+        here_ref[r : r + 1, :] = here[:, r * NG : (r + 1) * NG]
 
 
 def message_kernel(proj_ref, out_ref, rows):
@@ -130,7 +144,9 @@
         out_ref[b] = moved[:, :NG].astype(BF)
 
 
-def charge_kernel(home_ref, proj_ref, block_ref, out_ref, held):
+def charge_kernel(home_hbm, proj_ref, block_ref, out_ref, home_ref, sem):
+    fetch = pltpu.make_async_copy(home_hbm, home_ref, sem)
+    fetch.start()
     slab = lax.axis_index("slab")
     owner = lax.axis_index("band") * SLABS + slab
     groups = proj_ref.shape[0]
@@ -142,6 +158,7 @@
         for t in range(atoms):
             weights[t] = jnp.where(lane // SLABS == b, mine[:, t : t + 1], weights[t])
     pieces = []
+    fetch.wait()
     for t in range(atoms):
         goes = (lane & (SLABS - 1)) == home_ref[0, owner * atoms + t] // (PLANES // 2)
         behind = pltpu.roll(weights[t], NG - SLABS, 1)
@@ -151,41 +168,39 @@
     bound = jnp.sum(jnp.abs(weight), axis=0, keepdims=True) * BLOCK_LIMIT
     weight = jnp.transpose(weight * (QMAX / jnp.maximum(bound, 1e-30)))
     both = jnp.concatenate(split(weight), axis=1)
-    for y in range(8):
-        held[:, y, :] = dot(both, jnp.concatenate([block_ref[y], block_ref[y]], axis=0))
+    values = [dot(both, jnp.concatenate([block_ref[y], block_ref[y]], axis=0)) for y in range(8)]
+    values = jnp.swapaxes(jnp.round(jnp.stack(values)), 0, 1)
     half = weight.shape[0] // 2
-    both_pairs = jnp.concatenate([held[:half], held[half:]], axis=1)
-    out_ref[...] = to_int16(jnp.round(both_pairs))
+    out_ref[...] = to_int16(jnp.concatenate([values[:half], values[half:]], axis=1))
 
 
 def mark_kernel(in_ref, out_ref):
     out_ref[...] = jnp.zeros_like(out_ref)
 
 
-def density_kernel(p, home_ref, here_ref, charge_ref, own_ref, next_ref, right_ref, left_ref, out_ref, field, scales):
+def density_kernel(p, place_ref, here_ref, charge_ref, own_ref, next_ref, proj_ref, next_proj_ref, right_ref, left_ref, out_ref, field, scales):
     rows, owners = here_ref.shape[0], charge_ref.shape[0]
-    proj = pl.ds(PLANES * NG, own_ref.shape[0] - PLANES * NG)
-    sizes = jnp.abs(own_ref[proj, :].astype(F32) * next_ref[proj, :].astype(F32))
-    bound = sizes[:rows]
-    for c in range(1, CHANNELS):
-        bound = bound + sizes[c * rows : (c + 1) * rows]
-    bound = bound * here_ref[...] * (BLOCK_LIMIT / QMAX)
     count = owners // rows
-    wide = lax.broadcasted_iota(jnp.int32, (count, NG), 1) // (NG // count)
-    own_lane = wide == lax.broadcasted_iota(jnp.int32, (count, NG), 0)
+    atoms = NG // count
+    own_lane = lax.broadcasted_iota(jnp.int32, (count, NG), 1) // atoms == lax.broadcasted_iota(jnp.int32, (count, NG), 0)
+    sizes = jnp.sum(jnp.abs(proj_ref[0].astype(F32) * next_proj_ref[0].astype(F32)), axis=0, keepdims=True)
     for r in range(rows):
-        picked = jnp.where(own_lane, bound[r : r + 1], 0.0)
-        total = jnp.sum(picked, axis=1, keepdims=True)
+        bound = sizes[:, r * NG : (r + 1) * NG] * here_ref[r : r + 1, :]
+        total = jnp.sum(jnp.where(own_lane, bound, 0.0), axis=1, keepdims=True)
         scales[pl.ds(r * count, count), :] = jnp.broadcast_to(total, (count, NG))
     for x in range(PLANES):
-        plane = pl.ds(x * NG, NG)
-        field[x] = own_ref[plane, :].astype(F32) * next_ref[plane, :].astype(F32)
+        field[x] = own_ref[0, x].astype(F32) * next_ref[0, x].astype(F32)
     lane = lax.broadcasted_iota(jnp.int32, (8, NG), 1)
 
-    def add_atom(d, carry):
-        plane = home_ref[0, d]
-        brick_y = home_ref[1, d]
-        shift = home_ref[2, d] * 8
+    def add_row(r, carry):
+        for i in range(count):
+            add_atom(r * count + i, place_ref[r, i * atoms])
+        return carry
+
+    def add_atom(d, place):
+        plane = place & 15
+        brick_y = (place >> 4) & 15
+        shift = (place >> 8) * 8
         inside = ((lane - shift) & (NG - 1)) < 16
         places = []
         tile = from_int16(charge_ref[d])[8 * p : 8 * p + 8] * scales[pl.ds(d, 1), :]
@@ -196,9 +211,8 @@
             places.append((at, field[at] + jnp.where(inside, turned, 0.0)))
         for at, total in places:
             field[at] = total
-        return carry
-
-    lax.fori_loop(0, charge_ref.shape[0], add_atom, 0, unroll=32)
+
+    lax.fori_loop(0, rows, add_row, 0)
     for x in range(0, PLANES, 2):
         both = times_right(jnp.concatenate([field[x], field[x + 1]], axis=0), right_ref)
         both = times_left(left_ref, jnp.concatenate([both[:NG], both[NG:]], axis=1))
@@ -226,41 +240,35 @@
     lax.fori_loop(0, SLABS, pack, 0, unroll=True)
 
 
-def solve_kernel(square_ref, in_ref, fold_x_ref, fold_z_ref, left_ref, out_ref, field):
-    def unpack(s, carry):
-        step = step_size(from_int16(in_ref[s, PLANES]))
-        for x in range(PLANES):
-            field[s * PLANES + x] = from_int16(in_ref[s, x]) * step
-        low = from_int16(in_ref[s, PLANES + 1]) * (step[0:1] * (0.5 / QMAX))
-        planes = pl.ds(s * PLANES, PLANES)
-        field[planes, 0, :] = field[planes, 0, :] + low
-        return carry
-
-    lax.fori_loop(0, SLABS, unpack, 0, unroll=True)
+def solve_kernel(base, squares_ref, in_ref, fold_x_ref, fold_z_ref, left_ref, *rest):
+    *more, out_ref, field = rest
+
+    for s in range(SLABS):
+        step = step_size(from_int16(in_ref[s, base + PLANES]))
+        planes = from_int16(in_ref[s, pl.ds(base, PLANES)]) * step[None]
+        low = from_int16(in_ref[s, base + PLANES + 1]) * (step[0:1] * (0.5 / QMAX))
+        rows = pl.ds(s * PLANES, PLANES)
+        field[:, rows, :] = jnp.swapaxes(planes, 0, 1)
+        field[0, rows, :] = field[0, rows, :] + low
     fold = fold_x_ref[...] + fold_z_ref[...]
+    slab = lax.axis_index("slab")
     for r in range(0, ROWS, 2):
         halves = []
         for k in range(2):
-            total = fold + square_ref[r + k]
+            total = fold + squares_ref[slab, r + k]
             halves.append(jnp.where(total > 0, KERNEL_SCALE / (total + SCREENING_RANGE), 0.0) * (1.0 / NG**3))
-        columns = jnp.concatenate([field[:, r, :], field[:, r + 1, :]], axis=1)
+        columns = jnp.concatenate([field[r], field[r + 1]], axis=1)
         spectrum = times_left(left_ref, columns) * jnp.concatenate(halves, axis=1)
         columns = times_left(left_ref, spectrum)
-        field[:, r, :] = columns[:, :NG]
-        field[:, r + 1, :] = columns[:, NG:]
-
-    def pack(s, carry):
-        largest = jnp.abs(field[s * PLANES])
-        for x in range(1, PLANES):
-            largest = jnp.maximum(largest, jnp.abs(field[s * PLANES + x]))
-        code = step_code(largest)
-        factor = 1.0 / step_size(code)
-        for x in range(PLANES):
-            out_ref[s, x] = to_int16(jnp.round(field[s * PLANES + x] * factor))
+        field[r] = columns[:, :NG]
+        field[r + 1] = columns[:, NG:]
+    for s in range(SLABS):
+        planes = jnp.swapaxes(field[:, pl.ds(s * PLANES, PLANES), :], 0, 1)
+        code = step_code(jnp.max(jnp.abs(planes), axis=0))
+        out_ref[s, pl.ds(0, PLANES)] = to_int16(jnp.round(planes * (1.0 / step_size(code))[None]))
         out_ref[s, PLANES] = to_int16(code)
-        return carry
-
-    lax.fori_loop(0, SLABS, pack, 0, unroll=True)
+        for more_ref in more:
+            out_ref[s, pl.ds(BACK_TILES, FWD_TILES)] = more_ref[s]
 
 
 def potential_pair(in_ref, steps, x, left_ref, right_ref):
@@ -278,8 +286,8 @@
         pair = potential_pair(in_ref, steps, x, left_ref, right_ref)
         for k in range(2):
             potential = pair[k]
-            kept_ref[x + k] = potential * next_ref[pl.ds((x + k) * NG, NG), :].astype(F32)
-            product = potential * own_ref[pl.ds((x + k) * NG, NG), :].astype(F32)
+            kept_ref[x + k] = potential * next_ref[0, x + k].astype(F32)
+            product = potential * own_ref[0, x + k].astype(F32)
             code = step_code(jnp.max(jnp.abs(product), axis=0, keepdims=True))
             codes[x + k : x + k + 1, :] = code
             sent_ref[pl.ds((x + k) * NG, NG), :] = to_int16(jnp.round(product * (1.0 / step_size(code))))
@@ -293,7 +301,11 @@
         pair = potential_pair(in_ref, steps, x, left_ref, right_ref)
         for k in range(2):
             sent = from_int16(sent_ref[pl.ds((x + k) * NG, NG), :]) * sent_steps[x + k : x + k + 1]
-            out_ref[0, x + k] = kept_ref[x + k] + sent + pair[k] * own_ref[pl.ds((x + k) * NG, NG), :].astype(F32)
+            out_ref[0, x + k] = kept_ref[x + k] + sent + pair[k] * own_ref[0, x + k].astype(F32)
+
+
+def hbm():
+    return pl.BlockSpec(memory_space=pltpu.HBM)
 
 
 def vmem():
@@ -335,15 +347,9 @@
     n_slab = lax.axis_size("slab")
     owners = n_band * n_slab
     atom_dev = aug_blocks.shape[0]
-    channels = projections.shape[1]
-    slab_bricks = PLANES // 2
-    my_slab = lax.axis_index("slab")
     right, left, left_y, left_y_back = (jnp.asarray(t) for t in tables())
     squares = fold_square_host()
-    fold_rows = jnp.asarray(squares[row_order()])
-
-    own = orbitals[0]
-    own_proj = projections[0]
+
 
     messages = call(
         message_kernel,
@@ -353,77 +359,67 @@
         "messages",
         1,
     )(projections)
-    messages, late_blocks = lax.optimization_barrier((messages, aug_blocks))
     all_proj = lax.all_to_all(messages, "band", split_axis=0, concat_axis=0, tiled=True)
 
-    slab_of = (atom_home[0] // slab_bricks).reshape(owners, atom_dev)
-    here = slab_of == my_slab
-    home = atom_home.reshape(3, owners, atom_dev)
-    home = home - jnp.array([1, 0, 0], jnp.int32)[:, None, None] * (my_slab * slab_bricks)
-    home = jnp.sum(jnp.where(here[None], home, 0), axis=2) * jnp.array([2, 1, 1], jnp.int32)[:, None]
-
-    blocks = call(
-        block_kernel,
-        [vmem()],
-        jax.ShapeDtypeStruct((8, atom_dev * CHANNEL_ROWS, NG), BF),
-        [pltpu.VMEM((8, atom_dev * CHANNEL_ROWS, NG), F32)] * 2,
-        "blocks",
+    home_rows = atom_home.shape[1] // NG
+    blocks, places, here = call(
+        local_kernel,
+        [pl.BlockSpec(memory_space=pl.ANY), hbm(), vmem()],
+        [
+            jax.ShapeDtypeStruct((8, atom_dev * CHANNEL_ROWS, NG), BF),
+            jax.ShapeDtypeStruct((home_rows, NG), jnp.int32),
+            jax.ShapeDtypeStruct((home_rows, NG), F32),
+        ],
+        [pltpu.VMEM((8, atom_dev * CHANNEL_ROWS, NG), F32)] * 2
+        + [pltpu.VMEM(atom_home.shape, jnp.int32), pltpu.SemaphoreType.DMA],
+        "local",
         1,
-    )(late_blocks)
-    wide_proj = own_proj.reshape(-1, NG)
-    fill = jnp.zeros((-wide_proj.shape[0] % 16, NG), BF)
-    both = jnp.concatenate([own.reshape(-1, NG), wide_proj, fill], axis=0)
-    here = here.astype(F32).reshape(-1, NG)
-    both, home, here, blocks = lax.optimization_barrier((both, home, here, blocks))
-    nxt = from_behind(both, "band", -1)
+    )(messages, atom_home, aug_blocks.transpose(0, 2, 1, 3))
+    own, proj, blocks = lax.optimization_barrier((orbitals, projections, blocks))
+    next_proj = from_behind(proj, "band", -1)
+    nxt = from_behind(own, "band", -1)
 
     charges = call(
         charge_kernel,
-        [smem()] + [vmem()] * 2,
+        [hbm()] + [vmem()] * 2,
         jax.ShapeDtypeStruct((owners, 16, NG), jnp.int16),
-        [pltpu.VMEM((2 * owners, 8, NG), F32)],
+        [pltpu.SMEM(atom_home.shape, jnp.int32), pltpu.SemaphoreType.DMA],
         "charges",
         2,
     )(atom_home, all_proj, blocks)
     charges = lax.all_to_all(charges, ("band", "slab"), split_axis=0, concat_axis=0, tiled=True)
 
-    fold_y = lax.dynamic_index_in_dim(fold_rows, my_slab, 0, keepdims=False)
+    fold_y = jnp.asarray(squares[row_order()])
     fold_x = jnp.asarray(np.broadcast_to(squares[:, None], (NG, NG)).copy())
     fold_z = jnp.asarray(squares[None, :])
 
-    def density(p, other):
+    def density(p, other, other_proj):
         return call(
             functools.partial(density_kernel, p),
-            [smem()] + [vmem()] * 6,
+            [smem()] + [vmem()] * 8,
             jax.ShapeDtypeStruct((n_slab, FWD_TILES, 16, NG), jnp.int16),
             [pltpu.VMEM((PLANES, NG, NG), F32), pltpu.VMEM((owners, NG), F32)],
             "density" + str(p),
             6,
-        )(home, here, charges, both, other, right, left_y)
-
-    def solve(p, spectrum):
+        )(places, here, charges, own, other, proj, other_proj, right, left_y)
+
+    def solve(name, base, spectrum, *more):
+        tiles = BACK_TILES + FWD_TILES * len(more)
         return call(
-            solve_kernel,
-            [smem()] + [vmem()] * 4,
-            jax.ShapeDtypeStruct((n_slab, BACK_TILES, 16, NG), jnp.int16),
-            [pltpu.VMEM((NG, ROWS, NG), F32)],
-            "solve" + str(p),
+            functools.partial(solve_kernel, base),
+            [smem()] + [vmem()] * (4 + len(more)),
+            jax.ShapeDtypeStruct((n_slab, tiles, 16, NG), jnp.int16),
+            [pltpu.VMEM((ROWS, NG, NG), F32)],
+            name,
             3,
-        )(fold_y, spectrum, fold_x, fold_z, left)
+        )(fold_y, spectrum, fold_x, fold_z, left, *more)
 
     def swap(block):
         return lax.all_to_all(block, "slab", split_axis=0, concat_axis=0, tiled=True)
 
-    cross = swap(density(1, nxt))
-    mine = density(0, both)
-    cross, mine = lax.optimization_barrier((cross, mine))
-    mine = swap(mine)
-    cross = solve(1, cross)
-    cross, mine = lax.optimization_barrier((cross, mine))
-    cross = swap(cross)
-    mine = solve(0, mine)
-    cross, mine = lax.optimization_barrier((cross, mine))
-    mine = swap(mine)
+    cross = swap(density(1, nxt, next_proj))
+    cross = swap(solve("solve1", 0, cross, density(0, own, proj)))
+    mine = swap(solve("solve0", BACK_TILES, cross))
 
     kept, sent = call(
         back_cross_kernel,
@@ -435,7 +431,7 @@
         [pltpu.VMEM((PLANES, NG), F32)],
         "back_cross",
         2,
-    )(cross, both, nxt, left_y_back, right)
+    )(cross, own, nxt, left_y_back, right)
     got = from_behind(sent, "band", 1)
     got, _ = lax.optimization_barrier((got, mark(mine)))
     return call(
@@ -445,7 +441,7 @@
         [],
         "back_own",
         2,
-    )(mine, both, kept, got, left_y_back, right)
+    )(mine, own, kept, got, left_y_back, right)
 
 
 def solution(mesh):

time: 105 us -> 102 us (0.971)
  blocking collectives: 0 us -> 18.5 us
  waiting for transfers between devices: 42.1 us -> 31.1 us
  starting transfers between devices: 35.9 us -> 28.3 us
  Pallas kernels: 22.8 us -> 20 us
    all_to_all x0 -> x1, blocking collectives: none -> 18.5 us  [swap(): lax.all_to_all(block, 'slab', split_axis=0, concat_axis=0, tiled=True)]
    all_to_all x4 -> x2, starting transfers between devices: 15.3 us -> 7.08 us  [swap(): lax.all_to_all(block, 'slab', split_axis=0, concat_axis=0, tiled=True)]
    all_to_all x1, waiting for transfers between devices: 13.4 us -> 8.08 us  [per_device(): lax.all_to_all(charges, ('band', 'slab'), split_axis=0, concat_axis=0, ti...]
    all_to_all x4 -> x2, waiting for transfers between devices: 15.8 us -> 11.3 us  [swap(): lax.all_to_all(block, 'slab', split_axis=0, concat_axis=0, tiled=True)]
    pallas_call x6, Pallas kernels: 19.1 us -> 15.6 us  [the longest x2 7.86 us: density(): call(functools.partial(density_kernel, p), [smem()] + [vmem()] * 8, jax.S...]
    unnamed x26, local copies, waits for them, and re-layouts: 1.31 us -> 3.04 us
    ppermute x2 -> x3, waiting for transfers between devices: 7.85 us -> 6.75 us  [from_behind(): lax.ppermute(block, axis, [((i - distance) % count, i) for i in range(cou...]
    ppermute x2 -> x3, starting transfers between devices: 5.8 us -> 6.37 us  [from_behind(): lax.ppermute(block, axis, [((i - distance) % count, i) for i in range(cou...]
  transfers between devices with their start and end apart: 8 -> 7, of which waited for: 7 -> 6; matrix products, arithmetic and copies ran while one was open for 2% -> 0% of each run, Pallas kernels for 14% -> 9%
where the time goes in v2:
time: 102 us; the launch traced here: 101 us
  waiting for transfers between devices  31.1 us (30%)
  starting transfers between devices  28.3 us (28%)
  Pallas kernels  20 us (20%)
  blocking collectives  18.5 us (18%)
  local copies, waits for them, and re-layouts  3.04 us (3%)
    all_to_all x1, blocking collectives, swap(): lax.all_to_all(block, 'slab', split_axis=0, concat_axis=0, tiled=True)  18.5 us
    all_to_all x2, waiting for transfers between devices, swap(): lax.all_to_all(block, 'slab', split_axis=0, concat_axis=0, tiled=True)  11.3 us
    all_to_all x1, starting transfers between devices, per_device(): lax.all_to_all(messages, 'band', split_axis=0, concat_axis=0, tiled=True)  9.27 us
    all_to_all x1, waiting for transfers between devices, per_device(): lax.all_to_all(charges, ('band', 'slab'), split_axis=0, concat_axis=0, ti...  8.08 us
    pallas_call x2, Pallas kernels, density(): call(functools.partial(density_kernel, p), [smem()] + [vmem()] * 8, jax.S...  7.86 us
    all_to_all x2, starting transfers between devices, swap(): lax.all_to_all(block, 'slab', split_axis=0, concat_axis=0, tiled=True)  7.08 us
    ppermute x3, waiting for transfers between devices, from_behind(): lax.ppermute(block, axis, [((i - distance) % count, i) for i in range(cou...  6.75 us
    ppermute x3, starting transfers between devices, from_behind(): lax.ppermute(block, axis, [((i - distance) % count, i) for i in range(cou...  6.37 us
  transfers between devices with their start and end apart: 7, of which 6 were waited for; matrix products, arithmetic and copies ran while one was open for 0% of the time, Pallas kernels for 9%

profile of v2, /device:TPU:1, one launch (start us, length us, event | category | flops | bytes accessed | tf_op | source)
XLA Modules:
  0.0 101.1 jit_solution(6189498190992753884)
XLA Ops:
  0.0 0.7 copy-done.6
  0.7 0.7 messages.1.after_ref
  1.5 9.3 %all-to-all-start = ((bf16[16,16,128]{2,1,0:T(8,128)(2,1)}), bf16[16,16,128]{2,1,0:T(8,128)(2,1)S(1)}, u32[]{:S(2)}, u32[]{:S(2)}) async-start(bf16[16,16,128]{2,1,0:T(8,128)(2,1)} %messages.1.after_ref), calls=%async_computation | async-start | bytes 131072 | tf_op jit(solution)/shard_map/all_to_all | solution.py:362
  10.7 0.9 copy-done.10
  11.6 0.7 copy-done.11
  12.3 0.6 local.1
  12.9 0.2 collective-permute-start
  13.1 5.0 %all-to-all-done.proj_ref = bf16[16,16,128]{2,1,0:T(8,128)(2,1)S(1)} async-done(((bf16[16,16,128]{2,1,0:T(8,128)(2,1)}), bf16[16,16,128]{2,1,0:T(8,128)(2,1)S(1)}, u32[]{:S(2)}, u32[]{:S(2)}) %all-to-all-start) | async-done | bytes 65568 | tf_op jit(solution)/shard_map/all_to_all | solution.py:362
  18.1 0.7 copy-done.12
  18.8 2.3 %charges.1 = s16[128,16,128]{2,1,0:T(8,128)(2,1)} custom-call(s32[3,512]{1,0:T(4,128)S(1)} %copy-done.12, bf16[16,16,128]{2,1,0:T(8,128)(2,1)S(1)} %all-to-all-done.proj_ref, bf16[8,64,128]{2,1,0:T(8,128)(2,1)S(1)} %get-tuple-element.16.block_ref), custom_call_target="tpu_custom_call" | custom-call | flops 200000000 | bytes 7000000 | tf_op jit(solution)/shard_map/charges/pallas_call | solution.py:382
  21.1 5.6 %all-to-all-start.1 = ((s16[128,16,128]{2,1,0:T(8,128)(2,1)}), s16[128,16,128]{2,1,0:T(8,128)(2,1)S(1)}, u32[]{:S(2)}, u32[]{:S(2)}) async-start(s16[128,16,128]{2,1,0:T(8,128)(2,1)} %charges.1), calls=%async_computation.1 | async-start | bytes 1048576 | tf_op jit(solution)/shard_map/all_to_all | solution.py:390
  26.7 1.1 %collective-permute-start.1 = (bf16[1,9,512]{2,1,0:T(8,128)(2,1)S(1)}, bf16[1,9,512]{2,1,0:T(8,128)(2,1)S(1)}, u32[]{:S(2)}, u32[]{:S(2)}) collective-permute-start(bf16[1,9,512]{2,1,0:T(8,128)(2,1)S(1)} %copy-done.7), channel_id=1, source_target_pairs={{8,0},{16,8},{24,16},{32,24},{40,32},{48,40},{56,48},{64,56},{72,6... | collective-permute-start | bytes 27656 | tf_op jit(solution)/shard_map/ppermute | solution.py:342
  27.8 4.2 %collective-permute-done.1.next_proj_ref = bf16[1,9,512]{2,1,0:T(8,128)(2,1)S(1)} collective-permute-done((bf16[1,9,512]{2,1,0:T(8,128)(2,1)S(1)}, bf16[1,9,512]{2,1,0:T(8,128)(2,1)S(1)}, u32[]{:S(2)}, u32[]{:S(2)}) %collective-permute-start.1) | collective-permute-done | bytes 9248 | tf_op jit(solution)/shard_map/ppermute | solution.py:342
  32.0 8.1 %all-to-all-done.1.charge_ref = s16[128,16,128]{2,1,0:T(8,128)(2,1)S(1)} async-done(((s16[128,16,128]{2,1,0:T(8,128)(2,1)}), s16[128,16,128]{2,1,0:T(8,128)(2,1)S(1)}, u32[]{:S(2)}, u32[]{:S(2)}) %all-to-all-start.1) | async-done | bytes 524320 | tf_op jit(solution)/shard_map/all_to_all | solution.py:390
  40.1 4.3 %density1.1 = s16[8,18,16,128]{3,2,1,0:T(8,128)(2,1)} custom-call(s32[4,128]{1,0:T(4,128)S(1)} %get-tuple-element.13.place_ref, f32[4,128]{1,0:T(4,128)S(1)} %get-tuple-element.14.here_ref, s16[128,16,128]{2,1,0:T(8,128)(2,1)S(1)} %all-to-all-done.1.charge_ref, bf16[1,16,128,128]{3,2,1,0:T(8,128)(2,1)S(1)} %copy-done, ...), custom_call_target="tpu_custom_call" | custom-call | flops 600000000 | bytes 21000000 | tf_op jit(solution)/shard_map/density1/pallas_call | solution.py:397
  44.4 3.5 %all-to-all-start.2 = ((s16[8,18,16,128]{3,2,1,0:T(8,128)(2,1)}), s16[8,18,16,128]{3,2,1,0:T(8,128)(2,1)S(1)}, u32[]{:S(2)}, u32[]{:S(2)}) async-start(s16[8,18,16,128]{3,2,1,0:T(8,128)(2,1)} %density1.1), calls=%async_computation.2 | async-start | bytes 1179648 | tf_op jit(solution)/shard_map/all_to_all | solution.py:418
  48.0 0.0 copy-start.2
  48.0 0.0 copy-start.5
  48.0 0.0 copy-start.8
  48.0 0.0 copy-start.9
  48.0 3.5 %density0.1.rest_0_ = s16[8,18,16,128]{3,2,1,0:T(8,128)(2,1)S(1)} custom-call(s32[4,128]{1,0:T(4,128)S(1)} %get-tuple-element.13.place_ref, f32[4,128]{1,0:T(4,128)S(1)} %get-tuple-element.14.here_ref, s16[128,16,128]{2,1,0:T(8,128)(2,1)S(1)} %all-to-all-done.1.charge_ref, bf16[1,16,128,128]{3,2,1,0:T(8,128)(2,1)S(1)} %copy-done, ...), custom_call_target="tpu_custom_call" | custom-call | flops 600000000 | bytes 21000000 | tf_op jit(solution)/shard_map/density0/pallas_call | solution.py:397
  51.6 5.6 %all-to-all-done.2.in_ref = s16[8,18,16,128]{3,2,1,0:T(8,128)(2,1)S(1)} async-done(((s16[8,18,16,128]{3,2,1,0:T(8,128)(2,1)}), s16[8,18,16,128]{3,2,1,0:T(8,128)(2,1)S(1)}, u32[]{:S(2)}, u32[]{:S(2)}) %all-to-all-start.2) | async-done | bytes 589856 | tf_op jit(solution)/shard_map/all_to_all | solution.py:418
  57.2 2.0 %solve1.1 = s16[8,35,16,128]{3,2,1,0:T(8,128)(2,1)S(1)} custom-call(f32[8,16]{1,0:T(8,128)S(1)} %copy-done.8, s16[8,18,16,128]{3,2,1,0:T(8,128)(2,1)S(1)} %all-to-all-done.2.in_ref, f32[128,128]{1,0:T(8,128)S(1)} %copy-done.5, f32[1,128]{1,0:T(1,128)S(1)} %copy-done.9, bf16[128,384]{1,0:T(8,128)(2,1)S(1)} %copy-done.2, ...), custom_call_target="tpu_custom_call" | custom-call | flops 300000000 | bytes 10500000 | tf_op jit(solution)/shard_map/solve1/pallas_call | solution.py:408
  59.2 0.0 copy-start.4
  59.2 18.5 %all_to_all.25.in_ref = s16[8,35,16,128]{3,2,1,0:T(8,128)(2,1)S(1)} all-to-all(s16[8,35,16,128]{3,2,1,0:T(8,128)(2,1)S(1)} %solve1.1), channel_id=1, replica_groups=mesh['band'=16,'slab'=8] {'slab'}, dimensions={0} | all-to-all | bytes 2293760 | tf_op jit(solution)/shard_map/all_to_all | solution.py:418
  77.8 1.8 %back_cross.1 = (f32[16,128,128]{2,1,0:T(8,128)S(1)}, s16[2064,128]{1,0:T(8,128)(2,1)}) custom-call(s16[8,35,16,128]{3,2,1,0:T(8,128)(2,1)S(1)} %all_to_all.25.in_ref, bf16[1,16,128,128]{3,2,1,0:T(8,128)(2,1)S(1)} %copy-done, bf16[1,16,128,128]{3,2,1,0:T(8,128)(2,1)S(1)} %collective-permute-done.next_ref, bf16[128,384]{1,0:T(8,128)(2,1)S(1)} %copy-done.4, ...), custom_call_target="tpu_custom_call" | custom-call | flops 200000000 | bytes 7000000 | tf_op jit(solution)/shard_map/back_cross/pallas_call | solution.py:424
  79.6 5.1 %collective-permute-start.2 = (s16[2064,128]{1,0:T(8,128)(2,1)}, s16[2064,128]{1,0:T(8,128)(2,1)S(1)}, u32[]{:S(2)}, u32[]{:S(2)}) collective-permute-start(s16[2064,128]{1,0:T(8,128)(2,1)} %get-tuple-element.20), channel_id=1, source_target_pairs={{120,0},{0,8},{8,16},{16,24},{24,32},{32,40},{40,48},{48,56},{56,6... | collective-permute-start | bytes 1585160 | tf_op jit(solution)/shard_map/ppermute | solution.py:342
  84.7 2.8 %solve0.1 = s16[8,17,16,128]{3,2,1,0:T(8,128)(2,1)} custom-call(f32[8,16]{1,0:T(8,128)S(1)} %copy-done.8, s16[8,35,16,128]{3,2,1,0:T(8,128)(2,1)S(1)} %all_to_all.25.in_ref, f32[128,128]{1,0:T(8,128)S(1)} %copy-done.5, f32[1,128]{1,0:T(1,128)S(1)} %copy-done.9, bf16[128,384]{1,0:T(8,128)(2,1)S(1)} %copy-done.2), custom_call_target="tpu_custom_call" | custom-call | flops 300000000 | bytes 10500000 | tf_op jit(solution)/shard_map/solve0/pallas_call | solution.py:408
  87.5 3.5 %all-to-all-start.4 = ((s16[8,17,16,128]{3,2,1,0:T(8,128)(2,1)}), s16[8,17,16,128]{3,2,1,0:T(8,128)(2,1)S(1)}, u32[]{:S(2)}, u32[]{:S(2)}) async-start(s16[8,17,16,128]{3,2,1,0:T(8,128)(2,1)} %solve0.1), calls=%async_computation.4 | async-start | bytes 1114112 | tf_op jit(solution)/shard_map/all_to_all | solution.py:418
  91.0 2.6 %collective-permute-done.2.sent_ref = s16[2064,128]{1,0:T(8,128)(2,1)S(1)} collective-permute-done((s16[2064,128]{1,0:T(8,128)(2,1)}, s16[2064,128]{1,0:T(8,128)(2,1)S(1)}, u32[]{:S(2)}, u32[]{:S(2)}) %collective-permute-start.2) | collective-permute-done | bytes 528416 | tf_op jit(solution)/shard_map/ppermute | solution.py:342
  93.6 5.7 %all-to-all-done.4.in_ref = s16[8,17,16,128]{3,2,1,0:T(8,128)(2,1)S(1)} async-done(((s16[8,17,16,128]{3,2,1,0:T(8,128)(2,1)}), s16[8,17,16,128]{3,2,1,0:T(8,128)(2,1)S(1)}, u32[]{:S(2)}, u32[]{:S(2)}) %all-to-all-start.4) | async-done | bytes 557088 | tf_op jit(solution)/shard_map/all_to_all | solution.py:418
  99.3 1.9 %back_own.1 = f32[1,16,128,128]{3,2,1,0:T(8,128)} custom-call(s16[8,17,16,128]{3,2,1,0:T(8,128)(2,1)S(1)} %all-to-all-done.4.in_ref, bf16[1,16,128,128]{3,2,1,0:T(8,128)(2,1)S(1)} %copy-done, f32[16,128,128]{2,1,0:T(8,128)S(1)} %get-tuple-element.19.kept_ref, s16[2064,128]{1,0:T(8,128)(2,1)S(1)} %collective-permute-done.2.sent_ref, ...), custom_call_target="tpu_custom_call" | custom-call | flops 200000000 | bytes 7000000 | tf_op jit(solution)/shard_map/back_own/pallas_call | solution.py:437
  (18 shorter events, 0.0 us)
Async XLA Ops:
  0.0 0.7 copy-start.6
  1.4 25.2 %copy-start.7 = (bf16[1,9,512]{2,1,0:T(8,128)(2,1)S(1)}, bf16[1,9,512]{2,1,0:T(8,128)(2,1)}, u32[]{:S(2)}) copy-start(bf16[1,9,512]{2,1,0:T(8,128)(2,1)} %next_proj_ref) | copy-start | bytes 27652
  1.5 38.6 %copy-start = (bf16[1,16,128,128]{3,2,1,0:T(8,128)(2,1)S(1)}, bf16[1,16,128,128]{3,2,1,0:T(8,128)(2,1)}, u32[]{:S(2)}) copy-start(bf16[1,16,128,128]{3,2,1,0:T(8,128)(2,1)} %own_ref.3) | copy-start | bytes 1572868
  1.5 38.6 %copy-start.1 = (bf16[256,256]{1,0:T(8,128)(2,1)S(1)}, bf16[256,256]{1,0:T(8,128)(2,1)}, u32[]{:S(2)}) copy-start(bf16[256,256]{1,0:T(8,128)(2,1)} %constant.14.clone.right_ref) | copy-start | bytes 393220
  1.5 38.6 %copy-start.3 = (bf16[128,384]{1,0:T(8,128)(2,1)S(1)}, bf16[128,384]{1,0:T(8,128)(2,1)}, u32[]{:S(2)}) copy-start(bf16[128,384]{1,0:T(8,128)(2,1)} %constant.16.clone.left_ref) | copy-start | bytes 294916
  1.5 16.6 %all-to-all-start = ((bf16[16,16,128]{2,1,0:T(8,128)(2,1)}), bf16[16,16,128]{2,1,0:T(8,128)(2,1)S(1)}, u32[]{:S(2)}, u32[]{:S(2)}) async-start(bf16[16,16,128]{2,1,0:T(8,128)(2,1)} %messages.1.after_ref), calls=%async_computation | async-start | bytes 131072 | tf_op jit(solution)/shard_map/all_to_all | solution.py:362
  10.7 0.9 copy-start.10
  11.6 0.7 copy-start.11
  12.9 19.1 %collective-permute-start = (bf16[1,16,128,128]{3,2,1,0:T(8,128)(2,1)}, bf16[1,16,128,128]{3,2,1,0:T(8,128)(2,1)S(1)}, u32[]{:S(2)}, u32[]{:S(2)}) collective-permute-start(bf16[1,16,128,128]{3,2,1,0:T(8,128)(2,1)} %own_ref.3), channel_id=1, source_target_pairs={{8,0},{16,8},{24,16},{32,24},{40,32},{48,40},{56,48},{64,56},{72,6... | collective-permute-start | bytes 1572872 | tf_op jit(solution)/shard_map/ppermute | solution.py:342
  18.1 0.7 copy-start.12
  21.1 19.0 %all-to-all-start.1 = ((s16[128,16,128]{2,1,0:T(8,128)(2,1)}), s16[128,16,128]{2,1,0:T(8,128)(2,1)S(1)}, u32[]{:S(2)}, u32[]{:S(2)}) async-start(s16[128,16,128]{2,1,0:T(8,128)(2,1)} %charges.1), calls=%async_computation.1 | async-start | bytes 1048576 | tf_op jit(solution)/shard_map/all_to_all | solution.py:390
  26.7 5.3 %collective-permute-start.1 = (bf16[1,9,512]{2,1,0:T(8,128)(2,1)S(1)}, bf16[1,9,512]{2,1,0:T(8,128)(2,1)S(1)}, u32[]{:S(2)}, u32[]{:S(2)}) collective-permute-start(bf16[1,9,512]{2,1,0:T(8,128)(2,1)S(1)} %copy-done.7), channel_id=1, source_target_pairs={{8,0},{16,8},{24,16},{32,24},{40,32},{48,40},{56,48},{64,56},{72,6... | collective-permute-start | bytes 27656 | tf_op jit(solution)/shard_map/ppermute | solution.py:342
  44.4 12.7 %all-to-all-start.2 = ((s16[8,18,16,128]{3,2,1,0:T(8,128)(2,1)}), s16[8,18,16,128]{3,2,1,0:T(8,128)(2,1)S(1)}, u32[]{:S(2)}, u32[]{:S(2)}) async-start(s16[8,18,16,128]{3,2,1,0:T(8,128)(2,1)} %density1.1), calls=%async_computation.2 | async-start | bytes 1179648 | tf_op jit(solution)/shard_map/all_to_all | solution.py:418
  48.0 9.2 %copy-start.2 = (bf16[128,384]{1,0:T(8,128)(2,1)S(1)}, bf16[128,384]{1,0:T(8,128)(2,1)}, u32[]{:S(2)}) copy-start(bf16[128,384]{1,0:T(8,128)(2,1)} %constant.15.clone.left_ref) | copy-start | bytes 294916
  48.0 9.2 %copy-start.5 = (f32[128,128]{1,0:T(8,128)S(1)}, f32[128,128]{1,0:T(8,128)}, u32[]{:S(2)}) copy-start(f32[128,128]{1,0:T(8,128)} %constant.19.clone.fold_x_ref) | copy-start | bytes 196612
  48.0 9.2 %copy-start.8 = (f32[8,16]{1,0:T(8,128)S(1)}, f32[8,16]{1,0:T(8,128)}, u32[]{:S(2)}) copy-start(f32[8,16]{1,0:T(8,128)} %constant.18.clone.squares_ref) | copy-start | bytes 1540
  48.0 9.2 %copy-start.9 = (f32[1,128]{1,0:T(1,128)S(1)}, f32[1,128]{1,0:T(1,128)}, u32[]{:S(2)}) copy-start(f32[1,128]{1,0:T(1,128)} %constant.20.clone.fold_z_ref) | copy-start | bytes 1540
  59.2 18.6 %copy-start.4 = (bf16[128,384]{1,0:T(8,128)(2,1)S(1)}, bf16[128,384]{1,0:T(8,128)(2,1)}, u32[]{:S(2)}) copy-start(bf16[128,384]{1,0:T(8,128)(2,1)} %constant.17.clone.left_ref) | copy-start | bytes 294916
  79.6 14.0 %collective-permute-start.2 = (s16[2064,128]{1,0:T(8,128)(2,1)}, s16[2064,128]{1,0:T(8,128)(2,1)S(1)}, u32[]{:S(2)}, u32[]{:S(2)}) collective-permute-start(s16[2064,128]{1,0:T(8,128)(2,1)} %get-tuple-element.20), channel_id=1, source_target_pairs={{120,0},{0,8},{8,16},{16,24},{24,32},{32,40},{40,48},{48,56},{56,6... | collective-permute-start | bytes 1585160 | tf_op jit(solution)/shard_map/ppermute | solution.py:342
  87.5 11.8 %all-to-all-start.4 = ((s16[8,17,16,128]{3,2,1,0:T(8,128)(2,1)}), s16[8,17,16,128]{3,2,1,0:T(8,128)(2,1)S(1)}, u32[]{:S(2)}, u32[]{:S(2)}) async-start(s16[8,17,16,128]{3,2,1,0:T(8,128)(2,1)} %solve0.1), calls=%async_computation.4 | async-start | bytes 1114112 | tf_op jit(solution)/shard_map/all_to_all | solution.py:418

commit v3 on v2

--- a/solution.py
+++ b/solution.py
@@ -99,7 +99,7 @@
     return value.astype(jnp.int32).astype(F32)
 
 
-def local_kernel(after_ref, home_any, block_ref, out_ref, place_ref, here_ref, rows, turned, home_ref, sem):
+def local_kernel(after_ref, home_any, block_ref, out_ref, place_ref, here_ref, goes_ref, rows, turned, home_ref, sem):
     fetch = pltpu.make_async_copy(home_any, home_ref, sem)
     fetch.start()
     lane = lax.broadcasted_iota(jnp.int32, (1, NG), 1) // 8
@@ -132,6 +132,12 @@
             total = total + pltpu.roll(part, NG - t, 1)
         place_ref[r : r + 1, :] = total
         here_ref[r : r + 1, :] = here[:, r * NG : (r + 1) * NG]
+    owner = lax.axis_index("band") * SLABS + slab
+    wide = home_ref.shape[1]
+    mine = pltpu.roll(home_ref[0:1, :] // half, wide - owner * atoms, 1)[:, :NG]
+    slab_lane = lax.broadcasted_iota(jnp.int32, (1, NG), 1) & (SLABS - 1)
+    for t in range(atoms):
+        goes_ref[t : t + 1, :] = jnp.where(mine[:, t : t + 1] == slab_lane, 1.0, 0.0)
 
 
 def message_kernel(proj_ref, out_ref, rows):
@@ -144,11 +150,15 @@
         out_ref[b] = moved[:, :NG].astype(BF)
 
 
-def charge_kernel(home_hbm, proj_ref, block_ref, out_ref, home_ref, sem):
-    fetch = pltpu.make_async_copy(home_hbm, home_ref, sem)
-    fetch.start()
+def streamed(out_ref, held, sems, chunk, start, size):
+    part = pl.ds(start, size)
+    copy = pltpu.make_async_copy(held.at[part], out_ref.at[part], sems.at[chunk])
+    copy.start()
+    return copy
+
+
+def charge_kernel(goes_ref, proj_ref, block_ref, out_ref, held, sems):
     slab = lax.axis_index("slab")
-    owner = lax.axis_index("band") * SLABS + slab
     groups = proj_ref.shape[0]
     atoms = block_ref.shape[1] // CHANNEL_ROWS
     lane = lax.broadcasted_iota(jnp.int32, (CHANNEL_ROWS, NG), 1)
@@ -158,27 +168,33 @@
         for t in range(atoms):
             weights[t] = jnp.where(lane // SLABS == b, mine[:, t : t + 1], weights[t])
     pieces = []
-    fetch.wait()
     for t in range(atoms):
-        goes = (lane & (SLABS - 1)) == home_ref[0, owner * atoms + t] // (PLANES // 2)
         behind = pltpu.roll(weights[t], NG - SLABS, 1)
-        pairs = [jnp.where(goes, weights[t] * other, 0.0) for other in (weights[t], behind)]
-        pieces.append(jnp.concatenate(pairs, axis=1))
+        picked = weights[t] * goes_ref[t : t + 1, :]
+        pieces.append(jnp.concatenate([picked * weights[t], picked * behind], axis=1))
     weight = jnp.concatenate(pieces, axis=0)
     bound = jnp.sum(jnp.abs(weight), axis=0, keepdims=True) * BLOCK_LIMIT
     weight = jnp.transpose(weight * (QMAX / jnp.maximum(bound, 1e-30)))
     both = jnp.concatenate(split(weight), axis=1)
-    values = [dot(both, jnp.concatenate([block_ref[y], block_ref[y]], axis=0)) for y in range(8)]
-    values = jnp.swapaxes(jnp.round(jnp.stack(values)), 0, 1)
     half = weight.shape[0] // 2
-    out_ref[...] = to_int16(jnp.concatenate([values[:half], values[half:]], axis=1))
-
-
-def mark_kernel(in_ref, out_ref):
-    out_ref[...] = jnp.zeros_like(out_ref)
-
-
-def density_kernel(p, place_ref, here_ref, charge_ref, own_ref, next_ref, proj_ref, next_proj_ref, right_ref, left_ref, out_ref, field, scales):
+    size = half // 4
+    copies = []
+    blocks = [jnp.concatenate([block_ref[y], block_ref[y]], axis=0) for y in range(8)]
+    for n in range(4):
+        pairs = []
+        for p in range(2):
+            rows = both[p * half + n * size : p * half + (n + 1) * size]
+            values = jnp.round(jnp.stack([dot(rows, block) for block in blocks]))
+            pairs.append(jnp.swapaxes(values, 0, 1))
+        held[pl.ds(n * size, size)] = to_int16(jnp.concatenate(pairs, axis=1))
+        copies.append(streamed(out_ref, held, sems, n, n * size, size))
+    for copy in copies:
+        copy.wait()
+
+
+def density_kernel(p, place_vmem, here_ref, charge_ref, own_ref, next_ref, proj_ref, next_proj_ref, right_ref, left_ref, out_ref, field, scales, place_ref, sem):
+    fetch = pltpu.make_async_copy(place_vmem, place_ref, sem)
+    fetch.start()
     rows, owners = here_ref.shape[0], charge_ref.shape[0]
     count = owners // rows
     atoms = NG // count
@@ -191,6 +207,7 @@
     for x in range(PLANES):
         field[x] = own_ref[0, x].astype(F32) * next_ref[0, x].astype(F32)
     lane = lax.broadcasted_iota(jnp.int32, (8, NG), 1)
+    fetch.wait()
 
     def add_row(r, carry):
         for i in range(count):
@@ -219,8 +236,8 @@
         field[x] = both[:, :NG]
         field[x + 1] = both[:, NG:]
 
-    def pack(d, carry):
-        rows = pl.ds(pl.multiple_of(d * ROWS, ROWS), ROWS)
+    for d in range(SLABS):
+        rows = pl.ds(d * ROWS, ROWS)
         largest = jnp.abs(field[0, rows])
         for x in range(1, PLANES):
             largest = jnp.maximum(largest, jnp.abs(field[x, rows]))
@@ -235,9 +252,6 @@
         out_ref[d, PLANES] = to_int16(code)
         low = jnp.concatenate(lows, axis=0) * (2.0 * QMAX)
         out_ref[d, PLANES + 1] = to_int16(jnp.round(low))
-        return carry
-
-    lax.fori_loop(0, SLABS, pack, 0, unroll=True)
 
 
 def solve_kernel(base, squares_ref, in_ref, fold_x_ref, fold_z_ref, left_ref, *rest):
@@ -251,11 +265,11 @@
         field[:, rows, :] = jnp.swapaxes(planes, 0, 1)
         field[0, rows, :] = field[0, rows, :] + low
     fold = fold_x_ref[...] + fold_z_ref[...]
-    slab = lax.axis_index("slab")
+    squares = squares_ref[pl.ds(lax.axis_index("slab"), 1), :]
     for r in range(0, ROWS, 2):
         halves = []
         for k in range(2):
-            total = fold + squares_ref[slab, r + k]
+            total = fold + squares[:, r + k : r + k + 1]
             halves.append(jnp.where(total > 0, KERNEL_SCALE / (total + SCREENING_RANGE), 0.0) * (1.0 / NG**3))
         columns = jnp.concatenate([field[r], field[r + 1]], axis=1)
         spectrum = times_left(left_ref, columns) * jnp.concatenate(halves, axis=1)
@@ -294,14 +308,18 @@
     sent_ref[pl.ds(PLANES * NG, PLANES), :] = to_int16(codes[...])
 
 
-def back_own_kernel(in_ref, own_ref, kept_ref, sent_ref, left_ref, right_ref, out_ref):
+def back_own_kernel(in_ref, own_ref, kept_ref, sent_ref, left_ref, right_ref, out_ref, held, sems):
+    copies = []
     steps = [step_size(from_int16(in_ref[s, PLANES])) for s in range(SLABS)]
     sent_steps = step_size(from_int16(sent_ref[pl.ds(PLANES * NG, PLANES), :]))
     for x in range(0, PLANES, 2):
         pair = potential_pair(in_ref, steps, x, left_ref, right_ref)
         for k in range(2):
             sent = from_int16(sent_ref[pl.ds((x + k) * NG, NG), :]) * sent_steps[x + k : x + k + 1]
-            out_ref[0, x + k] = kept_ref[x + k] + sent + pair[k] * own_ref[0, x + k].astype(F32)
+            held[x + k] = kept_ref[x + k] + sent + pair[k] * own_ref[0, x + k].astype(F32)
+        copies.append(streamed(out_ref.at[0], held, sems, x // 2, x, 2))
+    for copy in copies:
+        copy.wait()
 
 
 def hbm():
@@ -316,12 +334,13 @@
     return pl.BlockSpec(memory_space=pltpu.SMEM)
 
 
-def call(kernel, in_specs, out_shape, scratch, name, micros):
+def call(kernel, in_specs, out_shape, scratch, name, micros, out_specs=None):
     many = isinstance(out_shape, (list, tuple))
+    out_specs = out_specs or [vmem()] * (len(out_shape) if many else 1)
     return pl.pallas_call(
         kernel,
         in_specs=in_specs,
-        out_specs=[vmem() for _ in out_shape] if many else vmem(),
+        out_specs=out_specs if many else out_specs[0],
         out_shape=out_shape,
         scratch_shapes=scratch,
         name=name,
@@ -330,11 +349,6 @@
         ),
         compiler_params=pltpu.CompilerParams(vmem_limit_bytes=VMEM_LIMIT),
     )
-
-
-def mark(array):
-    whole = [pl.BlockSpec(memory_space=pl.ANY)]
-    return call(mark_kernel, whole, jax.ShapeDtypeStruct((8, NG), F32), [], "mark", 30)(array)
 
 
 def from_behind(block, axis, distance):
@@ -362,13 +376,14 @@
     all_proj = lax.all_to_all(messages, "band", split_axis=0, concat_axis=0, tiled=True)
 
     home_rows = atom_home.shape[1] // NG
-    blocks, places, here = call(
+    blocks, places, here, goes = call(
         local_kernel,
         [pl.BlockSpec(memory_space=pl.ANY), hbm(), vmem()],
         [
             jax.ShapeDtypeStruct((8, atom_dev * CHANNEL_ROWS, NG), BF),
             jax.ShapeDtypeStruct((home_rows, NG), jnp.int32),
             jax.ShapeDtypeStruct((home_rows, NG), F32),
+            jax.ShapeDtypeStruct((atom_dev, NG), F32),
         ],
         [pltpu.VMEM((8, atom_dev * CHANNEL_ROWS, NG), F32)] * 2
         + [pltpu.VMEM(atom_home.shape, jnp.int32), pltpu.SemaphoreType.DMA],
@@ -381,12 +396,13 @@
 
     charges = call(
         charge_kernel,
-        [hbm()] + [vmem()] * 2,
+        [vmem()] * 3,
         jax.ShapeDtypeStruct((owners, 16, NG), jnp.int16),
-        [pltpu.SMEM(atom_home.shape, jnp.int32), pltpu.SemaphoreType.DMA],
+        [pltpu.VMEM((owners, 16, NG), jnp.int16), pltpu.SemaphoreType.DMA((4,))],
         "charges",
         2,
-    )(atom_home, all_proj, blocks)
+        [hbm()],
+    )(goes, all_proj, blocks)
     charges = lax.all_to_all(charges, ("band", "slab"), split_axis=0, concat_axis=0, tiled=True)
 
     fold_y = jnp.asarray(squares[row_order()])
@@ -396,9 +412,14 @@
     def density(p, other, other_proj):
         return call(
             functools.partial(density_kernel, p),
-            [smem()] + [vmem()] * 8,
+            [vmem()] * 9,
             jax.ShapeDtypeStruct((n_slab, FWD_TILES, 16, NG), jnp.int16),
-            [pltpu.VMEM((PLANES, NG, NG), F32), pltpu.VMEM((owners, NG), F32)],
+            [
+                pltpu.VMEM((PLANES, NG, NG), F32),
+                pltpu.VMEM((owners, NG), F32),
+                pltpu.SMEM(places.shape, jnp.int32),
+                pltpu.SemaphoreType.DMA,
+            ],
             "density" + str(p),
             6,
         )(places, here, charges, own, other, proj, other_proj, right, left_y)
@@ -407,7 +428,7 @@
         tiles = BACK_TILES + FWD_TILES * len(more)
         return call(
             functools.partial(solve_kernel, base),
-            [smem()] + [vmem()] * (4 + len(more)),
+            [vmem()] * (5 + len(more)),
             jax.ShapeDtypeStruct((n_slab, tiles, 16, NG), jnp.int16),
             [pltpu.VMEM((ROWS, NG, NG), F32)],
             name,
@@ -433,14 +454,14 @@
         2,
     )(cross, own, nxt, left_y_back, right)
     got = from_behind(sent, "band", 1)
-    got, _ = lax.optimization_barrier((got, mark(mine)))
     return call(
         back_own_kernel,
         [vmem()] * 6,
         jax.ShapeDtypeStruct((1, PLANES, NG, NG), F32),
-        [],
+        [pltpu.VMEM((PLANES, NG, NG), F32), pltpu.SemaphoreType.DMA((PLANES // 2,))],
         "back_own",
         2,
+        [hbm()],
     )(mine, own, kept, got, left_y_back, right)
 
 

time: 102 us -> 97.5 us (0.956)
  blocking collectives: 18.5 us -> 30.2 us
  waiting for transfers between devices: 31.1 us -> 22.9 us
  Pallas kernels: 20 us -> 16.4 us
  starting transfers between devices: 28.3 us -> 24.8 us
    all_to_all x1 -> x2, blocking collectives: 18.5 us -> 30.2 us  [swap(): lax.all_to_all(block, 'slab', split_axis=0, concat_axis=0, tiled=True)]
    all_to_all x2 -> x1, waiting for transfers between devices: 11.3 us -> 5.72 us  [swap(): lax.all_to_all(block, 'slab', split_axis=0, concat_axis=0, tiled=True)]
    all_to_all x2 -> x1, starting transfers between devices: 7.08 us -> 3.55 us  [swap(): lax.all_to_all(block, 'slab', split_axis=0, concat_axis=0, tiled=True)]
    pallas_call x5, Pallas kernels: 15 us -> 12.4 us  [the longest x2 7.62 us: density(): call(functools.partial(density_kernel, p), [vmem()] * 9, jax.ShapeDtypeSt...]
    ppermute x3, waiting for transfers between devices: 6.75 us -> 4.18 us  [from_behind(): lax.ppermute(block, axis, [((i - distance) % count, i) for i in range(cou...]
    unnamed x26 -> x24, local copies, waits for them, and re-layouts: 3.04 us -> 2.34 us
  transfers between devices with their start and end apart: 7 -> 6, of which waited for: 6 -> 4; matrix products, arithmetic and copies ran while one was open for 0% -> 0% of each run, Pallas kernels for 9% -> 8%
where the time goes in v3:
time: 97.5 us; the launch traced here: 97 us
  blocking collectives  30.2 us (31%)
  starting transfers between devices  24.8 us (25%)
  waiting for transfers between devices  22.9 us (23%)
  Pallas kernels  16.4 us (17%)
  local copies, waits for them, and re-layouts  2.34 us (2%)
    all_to_all x2, blocking collectives, swap(): lax.all_to_all(block, 'slab', split_axis=0, concat_axis=0, tiled=True)  30.2 us
    all_to_all x1, starting transfers between devices, per_device(): lax.all_to_all(messages, 'band', split_axis=0, concat_axis=0, tiled=True)  9.27 us
    all_to_all x1, waiting for transfers between devices, per_device(): lax.all_to_all(charges, ('band', 'slab'), split_axis=0, concat_axis=0, ti...  8.08 us
    pallas_call x2, Pallas kernels, density(): call(functools.partial(density_kernel, p), [vmem()] * 9, jax.ShapeDtypeSt...  7.62 us
    ppermute x3, starting transfers between devices, from_behind(): lax.ppermute(block, axis, [((i - distance) % count, i) for i in range(cou...  6.46 us
    all_to_all x1, waiting for transfers between devices, swap(): lax.all_to_all(block, 'slab', split_axis=0, concat_axis=0, tiled=True)  5.72 us
    all_to_all x1, starting transfers between devices, per_device(): lax.all_to_all(charges, ('band', 'slab'), split_axis=0, concat_axis=0, ti...  5.57 us
    all_to_all x1, waiting for transfers between devices, per_device(): lax.all_to_all(messages, 'band', split_axis=0, concat_axis=0, tiled=True)  4.95 us
  transfers between devices with their start and end apart: 6, of which 4 were waited for; matrix products, arithmetic and copies ran while one was open for 0% of the time, Pallas kernels for 8%

profile of v3, /device:TPU:1, one launch (start us, length us, event | category | flops | bytes accessed | tf_op | source)
XLA Modules:
  0.0 97.0 jit_solution(14806702496959705251)
XLA Ops:
  0.0 0.7 copy-done.6
  0.7 0.7 messages.1.after_ref
  1.5 9.3 %all-to-all-start = ((bf16[16,16,128]{2,1,0:T(8,128)(2,1)}), bf16[16,16,128]{2,1,0:T(8,128)(2,1)S(1)}, u32[]{:S(2)}, u32[]{:S(2)}) async-start(bf16[16,16,128]{2,1,0:T(8,128)(2,1)} %messages.1.after_ref), calls=%async_computation | async-start | bytes 131072 | tf_op jit(solution)/shard_map/all_to_all | solution.py:376
  10.7 0.9 copy-done.10
  11.6 0.7 copy-done.11
  12.3 0.7 local.1
  13.0 0.2 collective-permute-start
  13.2 5.0 %all-to-all-done.proj_ref = bf16[16,16,128]{2,1,0:T(8,128)(2,1)S(1)} async-done(((bf16[16,16,128]{2,1,0:T(8,128)(2,1)}), bf16[16,16,128]{2,1,0:T(8,128)(2,1)S(1)}, u32[]{:S(2)}, u32[]{:S(2)}) %all-to-all-start) | async-done | bytes 65568 | tf_op jit(solution)/shard_map/all_to_all | solution.py:376
  18.1 1.8 %charges.1 = s16[128,16,128]{2,1,0:T(8,128)(2,1)} custom-call(f32[4,128]{1,0:T(4,128)S(1)} %get-tuple-element.16.goes_ref, bf16[16,16,128]{2,1,0:T(8,128)(2,1)S(1)} %all-to-all-done.proj_ref, bf16[8,64,128]{2,1,0:T(8,128)(2,1)S(1)} %get-tuple-element.18.block_ref), custom_call_target="tpu_custom_call" | custom-call | flops 200000000 | bytes 7000000 | tf_op jit(solution)/shard_map/charges/pallas_call | solution.py:397
  19.9 5.6 %all-to-all-start.1 = ((s16[128,16,128]{2,1,0:T(8,128)(2,1)}), s16[128,16,128]{2,1,0:T(8,128)(2,1)S(1)}, u32[]{:S(2)}, u32[]{:S(2)}) async-start(s16[128,16,128]{2,1,0:T(8,128)(2,1)} %charges.1), calls=%async_computation.1 | async-start | bytes 1048576 | tf_op jit(solution)/shard_map/all_to_all | solution.py:406
  25.5 1.1 %collective-permute-start.1 = (bf16[1,9,512]{2,1,0:T(8,128)(2,1)S(1)}, bf16[1,9,512]{2,1,0:T(8,128)(2,1)S(1)}, u32[]{:S(2)}, u32[]{:S(2)}) collective-permute-start(bf16[1,9,512]{2,1,0:T(8,128)(2,1)S(1)} %copy-done.7), channel_id=1, source_target_pairs={{8,0},{16,8},{24,16},{32,24},{40,32},{48,40},{56,48},{64,56},{72,6... | collective-permute-start | bytes 27656 | tf_op jit(solution)/shard_map/ppermute | solution.py:356
  26.7 4.2 %collective-permute-done.1.next_proj_ref = bf16[1,9,512]{2,1,0:T(8,128)(2,1)S(1)} collective-permute-done((bf16[1,9,512]{2,1,0:T(8,128)(2,1)S(1)}, bf16[1,9,512]{2,1,0:T(8,128)(2,1)S(1)}, u32[]{:S(2)}, u32[]{:S(2)}) %collective-permute-start.1) | collective-permute-done | bytes 9248 | tf_op jit(solution)/shard_map/ppermute | solution.py:356
  30.8 0.0 collective-permute-done.next_ref
  30.8 8.1 %all-to-all-done.1.charge_ref = s16[128,16,128]{2,1,0:T(8,128)(2,1)S(1)} async-done(((s16[128,16,128]{2,1,0:T(8,128)(2,1)}), s16[128,16,128]{2,1,0:T(8,128)(2,1)S(1)}, u32[]{:S(2)}, u32[]{:S(2)}) %all-to-all-start.1) | async-done | bytes 524320 | tf_op jit(solution)/shard_map/all_to_all | solution.py:406
  38.9 0.0 copy-done.1
  38.9 4.2 %density1.1 = s16[8,18,16,128]{3,2,1,0:T(8,128)(2,1)} custom-call(s32[4,128]{1,0:T(4,128)S(1)} %get-tuple-element.14.place_vmem, f32[4,128]{1,0:T(4,128)S(1)} %get-tuple-element.15.here_ref, s16[128,16,128]{2,1,0:T(8,128)(2,1)S(1)} %all-to-all-done.1.charge_ref, bf16[1,16,128,128]{3,2,1,0:T(8,128)(2,1)S(1)} %copy-done, ...), custom_call_target="tpu_custom_call" | custom-call | flops 600000000 | bytes 21000000 | tf_op jit(solution)/shard_map/density1/pallas_call | solution.py:413
  43.1 3.6 %all-to-all-start.2 = ((s16[8,18,16,128]{3,2,1,0:T(8,128)(2,1)}), s16[8,18,16,128]{3,2,1,0:T(8,128)(2,1)S(1)}, u32[]{:S(2)}, u32[]{:S(2)}) async-start(s16[8,18,16,128]{3,2,1,0:T(8,128)(2,1)} %density1.1), calls=%async_computation.2 | async-start | bytes 1179648 | tf_op jit(solution)/shard_map/all_to_all | solution.py:439
  46.7 0.0 copy-start.2
  46.7 0.0 copy-start.5
  46.7 0.0 copy-start.8
  46.7 0.0 copy-start.9
  46.8 3.4 %density0.1.rest_0_ = s16[8,18,16,128]{3,2,1,0:T(8,128)(2,1)S(1)} custom-call(s32[4,128]{1,0:T(4,128)S(1)} %get-tuple-element.14.place_vmem, f32[4,128]{1,0:T(4,128)S(1)} %get-tuple-element.15.here_ref, s16[128,16,128]{2,1,0:T(8,128)(2,1)S(1)} %all-to-all-done.1.charge_ref, bf16[1,16,128,128]{3,2,1,0:T(8,128)(2,1)S(1)} %copy-done, ...), custom_call_target="tpu_custom_call" | custom-call | flops 600000000 | bytes 21000000 | tf_op jit(solution)/shard_map/density0/pallas_call | solution.py:413
  50.2 5.7 %all-to-all-done.2.in_ref = s16[8,18,16,128]{3,2,1,0:T(8,128)(2,1)S(1)} async-done(((s16[8,18,16,128]{3,2,1,0:T(8,128)(2,1)}), s16[8,18,16,128]{3,2,1,0:T(8,128)(2,1)S(1)}, u32[]{:S(2)}, u32[]{:S(2)}) %all-to-all-start.2) | async-done | bytes 589856 | tf_op jit(solution)/shard_map/all_to_all | solution.py:439
  55.9 1.5 %solve1.1 = s16[8,35,16,128]{3,2,1,0:T(8,128)(2,1)S(1)} custom-call(f32[8,16]{1,0:T(8,128)S(1)} %copy-done.8, s16[8,18,16,128]{3,2,1,0:T(8,128)(2,1)S(1)} %all-to-all-done.2.in_ref, f32[128,128]{1,0:T(8,128)S(1)} %copy-done.5, f32[1,128]{1,0:T(1,128)S(1)} %copy-done.9, bf16[128,384]{1,0:T(8,128)(2,1)S(1)} %copy-done.2, ...), custom_call_target="tpu_custom_call" | custom-call | flops 300000000 | bytes 10500000 | tf_op jit(solution)/shard_map/solve1/pallas_call | solution.py:429
  57.4 0.0 copy-start.4
  57.4 18.5 %all_to_all.25.in_ref = s16[8,35,16,128]{3,2,1,0:T(8,128)(2,1)S(1)} all-to-all(s16[8,35,16,128]{3,2,1,0:T(8,128)(2,1)S(1)} %solve1.1), channel_id=1, replica_groups=mesh['band'=16,'slab'=8] {'slab'}, dimensions={0} | all-to-all | bytes 2293760 | tf_op jit(solution)/shard_map/all_to_all | solution.py:439
  76.0 1.0 %back_cross.1 = (f32[16,128,128]{2,1,0:T(8,128)S(1)}, s16[2064,128]{1,0:T(8,128)(2,1)S(1)}) custom-call(s16[8,35,16,128]{3,2,1,0:T(8,128)(2,1)S(1)} %all_to_all.25.in_ref, bf16[1,16,128,128]{3,2,1,0:T(8,128)(2,1)S(1)} %copy-done, bf16[1,16,128,128]{3,2,1,0:T(8,128)(2,1)S(1)} %collective-permute-done.next_ref, bf16[128,384]{1,0:T(8,128)(2,1)S(1)} %copy-done.4, ...), custom_call_target="tpu_custom_call" | custom-call | flops 200000000 | bytes 7000000 | tf_op jit(solution)/shard_map/back_cross/pallas_call | solution.py:445
  77.0 5.1 %collective-permute-start.2 = (s16[2064,128]{1,0:T(8,128)(2,1)S(1)}, s16[2064,128]{1,0:T(8,128)(2,1)S(1)}, u32[]{:S(2)}, u32[]{:S(2)}) collective-permute-start(s16[2064,128]{1,0:T(8,128)(2,1)S(1)} %get-tuple-element.22), channel_id=1, source_target_pairs={{120,0},{0,8},{8,16},{16,24},{24,32},{32,40},{40,48},{48,56},{56,6... | collective-permute-start | bytes 1585160 | tf_op jit(solution)/shard_map/ppermute | solution.py:356
  82.1 1.5 %solve0.1 = s16[8,17,16,128]{3,2,1,0:T(8,128)(2,1)S(1)} custom-call(f32[8,16]{1,0:T(8,128)S(1)} %copy-done.8, s16[8,35,16,128]{3,2,1,0:T(8,128)(2,1)S(1)} %all_to_all.25.in_ref, f32[128,128]{1,0:T(8,128)S(1)} %copy-done.5, f32[1,128]{1,0:T(1,128)S(1)} %copy-done.9, bf16[128,384]{1,0:T(8,128)(2,1)S(1)} %copy-done.2), custom_call_target="tpu_custom_call" | custom-call | flops 300000000 | bytes 10500000 | tf_op jit(solution)/shard_map/solve0/pallas_call | solution.py:429
  83.6 11.7 %all_to_all.26.in_ref = s16[8,17,16,128]{3,2,1,0:T(8,128)(2,1)S(1)} all-to-all(s16[8,17,16,128]{3,2,1,0:T(8,128)(2,1)S(1)} %solve0.1), channel_id=1, replica_groups=mesh['band'=16,'slab'=8] {'slab'}, dimensions={0} | all-to-all | bytes 1114112 | tf_op jit(solution)/shard_map/all_to_all | solution.py:439
  95.3 0.0 collective-permute-done.2.sent_ref
  95.3 1.7 %back_own.1 = f32[1,16,128,128]{3,2,1,0:T(8,128)} custom-call(s16[8,17,16,128]{3,2,1,0:T(8,128)(2,1)S(1)} %all_to_all.26.in_ref, bf16[1,16,128,128]{3,2,1,0:T(8,128)(2,1)S(1)} %copy-done, f32[16,128,128]{2,1,0:T(8,128)S(1)} %get-tuple-element.21.kept_ref, s16[2064,128]{1,0:T(8,128)(2,1)S(1)} %collective-permute-done.2.sent_ref, ...), custom_call_target="tpu_custom_call" | custom-call | flops 200000000 | bytes 7000000 | tf_op jit(solution)/shard_map/back_own/pallas_call | solution.py:457
  (15 shorter events, 0.0 us)
Async XLA Ops:
  0.0 0.7 copy-start.6
  1.4 24.1 %copy-start.7 = (bf16[1,9,512]{2,1,0:T(8,128)(2,1)S(1)}, bf16[1,9,512]{2,1,0:T(8,128)(2,1)}, u32[]{:S(2)}) copy-start(bf16[1,9,512]{2,1,0:T(8,128)(2,1)} %next_proj_ref) | copy-start | bytes 27652
  1.5 37.5 %copy-start = (bf16[1,16,128,128]{3,2,1,0:T(8,128)(2,1)S(1)}, bf16[1,16,128,128]{3,2,1,0:T(8,128)(2,1)}, u32[]{:S(2)}) copy-start(bf16[1,16,128,128]{3,2,1,0:T(8,128)(2,1)} %own_ref.3) | copy-start | bytes 1572868
  1.5 37.5 %copy-start.1 = (bf16[256,256]{1,0:T(8,128)(2,1)S(1)}, bf16[256,256]{1,0:T(8,128)(2,1)}, u32[]{:S(2)}) copy-start(bf16[256,256]{1,0:T(8,128)(2,1)} %constant.14.clone.right_ref) | copy-start | bytes 393220
  1.5 37.5 %copy-start.3 = (bf16[128,384]{1,0:T(8,128)(2,1)S(1)}, bf16[128,384]{1,0:T(8,128)(2,1)}, u32[]{:S(2)}) copy-start(bf16[128,384]{1,0:T(8,128)(2,1)} %constant.16.clone.left_ref) | copy-start | bytes 294916
  1.5 16.6 %all-to-all-start = ((bf16[16,16,128]{2,1,0:T(8,128)(2,1)}), bf16[16,16,128]{2,1,0:T(8,128)(2,1)S(1)}, u32[]{:S(2)}, u32[]{:S(2)}) async-start(bf16[16,16,128]{2,1,0:T(8,128)(2,1)} %messages.1.after_ref), calls=%async_computation | async-start | bytes 131072 | tf_op jit(solution)/shard_map/all_to_all | solution.py:376
  10.7 0.9 copy-start.10
  11.6 0.7 copy-start.11
  13.0 17.9 %collective-permute-start = (bf16[1,16,128,128]{3,2,1,0:T(8,128)(2,1)}, bf16[1,16,128,128]{3,2,1,0:T(8,128)(2,1)S(1)}, u32[]{:S(2)}, u32[]{:S(2)}) collective-permute-start(bf16[1,16,128,128]{3,2,1,0:T(8,128)(2,1)} %own_ref.3), channel_id=1, source_target_pairs={{8,0},{16,8},{24,16},{32,24},{40,32},{48,40},{56,48},{64,56},{72,6... | collective-permute-start | bytes 1572872 | tf_op jit(solution)/shard_map/ppermute | solution.py:356
  19.9 19.0 %all-to-all-start.1 = ((s16[128,16,128]{2,1,0:T(8,128)(2,1)}), s16[128,16,128]{2,1,0:T(8,128)(2,1)S(1)}, u32[]{:S(2)}, u32[]{:S(2)}) async-start(s16[128,16,128]{2,1,0:T(8,128)(2,1)} %charges.1), calls=%async_computation.1 | async-start | bytes 1048576 | tf_op jit(solution)/shard_map/all_to_all | solution.py:406
  25.5 5.3 %collective-permute-start.1 = (bf16[1,9,512]{2,1,0:T(8,128)(2,1)S(1)}, bf16[1,9,512]{2,1,0:T(8,128)(2,1)S(1)}, u32[]{:S(2)}, u32[]{:S(2)}) collective-permute-start(bf16[1,9,512]{2,1,0:T(8,128)(2,1)S(1)} %copy-done.7), channel_id=1, source_target_pairs={{8,0},{16,8},{24,16},{32,24},{40,32},{48,40},{56,48},{64,56},{72,6... | collective-permute-start | bytes 27656 | tf_op jit(solution)/shard_map/ppermute | solution.py:356
  43.1 12.7 %all-to-all-start.2 = ((s16[8,18,16,128]{3,2,1,0:T(8,128)(2,1)}), s16[8,18,16,128]{3,2,1,0:T(8,128)(2,1)S(1)}, u32[]{:S(2)}, u32[]{:S(2)}) async-start(s16[8,18,16,128]{3,2,1,0:T(8,128)(2,1)} %density1.1), calls=%async_computation.2 | async-start | bytes 1179648 | tf_op jit(solution)/shard_map/all_to_all | solution.py:439
  46.7 9.2 %copy-start.2 = (bf16[128,384]{1,0:T(8,128)(2,1)S(1)}, bf16[128,384]{1,0:T(8,128)(2,1)}, u32[]{:S(2)}) copy-start(bf16[128,384]{1,0:T(8,128)(2,1)} %constant.15.clone.left_ref) | copy-start | bytes 294916
  46.7 9.2 %copy-start.5 = (f32[128,128]{1,0:T(8,128)S(1)}, f32[128,128]{1,0:T(8,128)}, u32[]{:S(2)}) copy-start(f32[128,128]{1,0:T(8,128)} %constant.19.clone.fold_x_ref) | copy-start | bytes 196612
  46.7 9.2 %copy-start.8 = (f32[8,16]{1,0:T(8,128)S(1)}, f32[8,16]{1,0:T(8,128)}, u32[]{:S(2)}) copy-start(f32[8,16]{1,0:T(8,128)} %constant.18.clone.squares_ref) | copy-start | bytes 1540
  46.7 9.2 %copy-start.9 = (f32[1,128]{1,0:T(1,128)S(1)}, f32[1,128]{1,0:T(1,128)}, u32[]{:S(2)}) copy-start(f32[1,128]{1,0:T(1,128)} %constant.20.clone.fold_z_ref) | copy-start | bytes 1540
  57.4 18.6 %copy-start.4 = (bf16[128,384]{1,0:T(8,128)(2,1)S(1)}, bf16[128,384]{1,0:T(8,128)(2,1)}, u32[]{:S(2)}) copy-start(bf16[128,384]{1,0:T(8,128)(2,1)} %constant.17.clone.left_ref) | copy-start | bytes 294916
  77.0 18.3 %collective-permute-start.2 = (s16[2064,128]{1,0:T(8,128)(2,1)S(1)}, s16[2064,128]{1,0:T(8,128)(2,1)S(1)}, u32[]{:S(2)}, u32[]{:S(2)}) collective-permute-start(s16[2064,128]{1,0:T(8,128)(2,1)S(1)} %get-tuple-element.22), channel_id=1, source_target_pairs={{120,0},{0,8},{8,16},{16,24},{24,32},{32,40},{40,48},{48,56},{56,6... | collective-permute-start | bytes 1585160 | tf_op jit(solution)/shard_map/ppermute | solution.py:356

commit v4 on v3

--- a/solution.py
+++ b/solution.py
@@ -19,6 +19,7 @@
 QMAX = 32760.0
 STEPS = 8.0
 CHANNEL_ROWS = 16
+ROUND = (0, 2, 4, 6, 7, 5, 3, 1)
 FWD_TILES = PLANES + 2
 BACK_TILES = PLANES + 1
 BF = jnp.bfloat16
@@ -51,7 +52,7 @@
 def tables():
     table = hartley_host()
     high, low = split_host(table)
-    order = row_order().reshape(-1)
+    order = row_order()[list(ROUND)].reshape(-1)
     high_y, low_y = high[order], low[order]
     top = np.concatenate([high, low], axis=1)
     bottom = np.concatenate([high, np.zeros_like(high)], axis=1)
@@ -134,7 +135,7 @@
         here_ref[r : r + 1, :] = here[:, r * NG : (r + 1) * NG]
     owner = lax.axis_index("band") * SLABS + slab
     wide = home_ref.shape[1]
-    mine = pltpu.roll(home_ref[0:1, :] // half, wide - owner * atoms, 1)[:, :NG]
+    mine = pltpu.roll(home_ref[0:1, :] // half, (wide - owner * atoms) & (wide - 1), 1)[:, :NG]
     slab_lane = lax.broadcasted_iota(jnp.int32, (1, NG), 1) & (SLABS - 1)
     for t in range(atoms):
         goes_ref[t : t + 1, :] = jnp.where(mine[:, t : t + 1] == slab_lane, 1.0, 0.0)
@@ -192,7 +193,7 @@
         copy.wait()
 
 
-def density_kernel(p, place_vmem, here_ref, charge_ref, own_ref, next_ref, proj_ref, next_proj_ref, right_ref, left_ref, out_ref, field, scales, place_ref, sem):
+def density_kernel(p, place_vmem, here_ref, charge_ref, own_ref, next_ref, proj_ref, next_proj_ref, right_ref, left_ref, out_ref, field, second, scales, place_ref, sem):
     fetch = pltpu.make_async_copy(place_vmem, place_ref, sem)
     fetch.start()
     rows, owners = here_ref.shape[0], charge_ref.shape[0]
@@ -209,29 +210,35 @@
     lane = lax.broadcasted_iota(jnp.int32, (8, NG), 1)
     fetch.wait()
 
-    def add_row(r, carry):
-        for i in range(count):
-            add_atom(r * count + i, place_ref[r, i * atoms])
-        return carry
-
-    def add_atom(d, place):
+    second[...] = jnp.zeros_like(second)
+
+    def tiles_of(d, place, total):
         plane = place & 15
         brick_y = (place >> 4) & 15
         shift = (place >> 8) * 8
         inside = ((lane - shift) & (NG - 1)) < 16
+        tile = from_int16(charge_ref[d])[8 * p : 8 * p + 8] * scales[pl.ds(d, 1), :]
         places = []
-        tile = from_int16(charge_ref[d])[8 * p : 8 * p + 8] * scales[pl.ds(d, 1), :]
         for g in range(8):
             turned = pltpu.roll(tile, (shift + (NG - 16 * g)) & (NG - 1), 1)
             row = pl.multiple_of(((brick_y + g % 2) & (NG // 8 - 1)) * 8, 8)
             at = (plane + g // 2, pl.ds(row, 8))
-            places.append((at, field[at] + jnp.where(inside, turned, 0.0)))
-        for at, total in places:
-            field[at] = total
+            places.append((at, total[at] + jnp.where(inside, turned, 0.0)))
+        return places
+
+    def add_row(r, carry):
+        for i in range(0, count, 2):
+            pair = []
+            for k, total in enumerate((field, second)):
+                pair.append(tiles_of(r * count + i + k, place_ref[r, (i + k) * atoms], total))
+            for places, total in zip(pair, (field, second)):
+                for at, value in places:
+                    total[at] = value
+        return carry
 
     lax.fori_loop(0, rows, add_row, 0)
     for x in range(0, PLANES, 2):
-        both = times_right(jnp.concatenate([field[x], field[x + 1]], axis=0), right_ref)
+        both = times_right(jnp.concatenate([field[x] + second[x], field[x + 1] + second[x + 1]], axis=0), right_ref)
         both = times_left(left_ref, jnp.concatenate([both[:NG], both[NG:]], axis=1))
         field[x] = both[:, :NG]
         field[x + 1] = both[:, NG:]
@@ -261,7 +268,7 @@
         step = step_size(from_int16(in_ref[s, base + PLANES]))
         planes = from_int16(in_ref[s, pl.ds(base, PLANES)]) * step[None]
         low = from_int16(in_ref[s, base + PLANES + 1]) * (step[0:1] * (0.5 / QMAX))
-        rows = pl.ds(s * PLANES, PLANES)
+        rows = pl.ds(ROUND[s] * PLANES, PLANES)
         field[:, rows, :] = jnp.swapaxes(planes, 0, 1)
         field[0, rows, :] = field[0, rows, :] + low
     fold = fold_x_ref[...] + fold_z_ref[...]
@@ -277,7 +284,7 @@
         field[r] = columns[:, :NG]
         field[r + 1] = columns[:, NG:]
     for s in range(SLABS):
-        planes = jnp.swapaxes(field[:, pl.ds(s * PLANES, PLANES), :], 0, 1)
+        planes = jnp.swapaxes(field[:, pl.ds(ROUND[s] * PLANES, PLANES), :], 0, 1)
         code = step_code(jnp.max(jnp.abs(planes), axis=0))
         out_ref[s, pl.ds(0, PLANES)] = to_int16(jnp.round(planes * (1.0 / step_size(code))[None]))
         out_ref[s, PLANES] = to_int16(code)
@@ -373,7 +380,9 @@
         "messages",
         1,
     )(projections)
-    all_proj = lax.all_to_all(messages, "band", split_axis=0, concat_axis=0, tiled=True)
+    all_proj = lax.all_to_all(
+        messages, "band", split_axis=0, concat_axis=0, tiled=True, axis_index_groups=[list(range(n_band))]
+    )
 
     home_rows = atom_home.shape[1] // NG
     blocks, places, here, goes = call(
@@ -416,6 +425,7 @@
             jax.ShapeDtypeStruct((n_slab, FWD_TILES, 16, NG), jnp.int16),
             [
                 pltpu.VMEM((PLANES, NG, NG), F32),
+                pltpu.VMEM((PLANES, NG, NG), F32),
                 pltpu.VMEM((owners, NG), F32),
                 pltpu.SMEM(places.shape, jnp.int32),
                 pltpu.SemaphoreType.DMA,
@@ -436,7 +446,9 @@
         )(fold_y, spectrum, fold_x, fold_z, left, *more)
 
     def swap(block):
-        return lax.all_to_all(block, "slab", split_axis=0, concat_axis=0, tiled=True)
+        return lax.all_to_all(
+            block, "slab", split_axis=0, concat_axis=0, tiled=True, axis_index_groups=[list(ROUND)]
+        )
 
     cross = swap(density(1, nxt, next_proj))
     cross = swap(solve("solve1", 0, cross, density(0, own, proj)))

time: 97.5 us -> 97.2 us (level)
  starting transfers between devices: 24.8 us -> 27.3 us
  waiting for transfers between devices: 22.9 us -> 21.6 us
    ppermute x3, starting transfers between devices: 6.46 us -> 8.93 us  [from_behind(): lax.ppermute(block, axis, [((i - distance) % count, i) for i in range(cou...]
    all_to_all x2, waiting for transfers between devices: 10.7 us -> 9.38 us  [the longest x1 4.95 us: per_device(): lax.all_to_all(messages, 'band', split_axis=0, concat_axis=0, tiled=True,...]
  transfers between devices with their start and end apart: 6 -> 6, of which waited for: 4 -> 4; matrix products, arithmetic and copies ran while one was open for 0% -> 0% of each run, Pallas kernels for 8% -> 7%
where the time goes in v4:
time: 97.2 us; the launch traced here: 96.7 us
  blocking collectives  29.3 us (30%)
  starting transfers between devices  27.3 us (28%)
  waiting for transfers between devices  21.6 us (22%)
  Pallas kernels  15.9 us (16%)
  local copies, waits for them, and re-layouts  2.34 us (2%)
    all_to_all x2, blocking collectives, swap(): lax.all_to_all(block, 'slab', split_axis=0, concat_axis=0, tiled=True, ax...  29.3 us
    all_to_all x1, starting transfers between devices, per_device(): lax.all_to_all(messages, 'band', split_axis=0, concat_axis=0, tiled=True,...  9.27 us
    ppermute x3, starting transfers between devices, from_behind(): lax.ppermute(block, axis, [((i - distance) % count, i) for i in range(cou...  8.93 us
    all_to_all x1, waiting for transfers between devices, per_device(): lax.all_to_all(charges, ('band', 'slab'), split_axis=0, concat_axis=0, ti...  8.08 us
    pallas_call x2, Pallas kernels, density(): call(functools.partial(density_kernel, p), [vmem()] * 9, jax.ShapeDtypeSt...  7.11 us
    all_to_all x1, starting transfers between devices, per_device(): lax.all_to_all(charges, ('band', 'slab'), split_axis=0, concat_axis=0, ti...  5.57 us
    all_to_all x1, waiting for transfers between devices, per_device(): lax.all_to_all(messages, 'band', split_axis=0, concat_axis=0, tiled=True,...  4.95 us
    all_to_all x1, waiting for transfers between devices, swap(): lax.all_to_all(block, 'slab', split_axis=0, concat_axis=0, tiled=True, ax...  4.43 us
  transfers between devices with their start and end apart: 6, of which 4 were waited for; matrix products, arithmetic and copies ran while one was open for 0% of the time, Pallas kernels for 7%

profile of v4, /device:TPU:1, one launch (start us, length us, event | category | flops | bytes accessed | tf_op | source)
XLA Modules:
  0.0 96.7 jit_solution(13370316077769185044)
XLA Ops:
  0.0 0.7 copy-done.6
  0.7 0.7 messages.1.after_ref
  1.5 9.3 %all-to-all-start = ((bf16[16,16,128]{2,1,0:T(8,128)(2,1)}), bf16[16,16,128]{2,1,0:T(8,128)(2,1)S(1)}, u32[]{:S(2)}, u32[]{:S(2)}) async-start(bf16[16,16,128]{2,1,0:T(8,128)(2,1)} %messages.1.after_ref), calls=%async_computation | async-start | bytes 131072 | tf_op jit(solution)/shard_map/all_to_all | solution.py:383
  10.7 0.9 copy-done.10
  11.6 0.7 copy-done.11
  12.3 0.7 local.1
  13.0 0.2 collective-permute-start
  13.2 5.0 %all-to-all-done.proj_ref = bf16[16,16,128]{2,1,0:T(8,128)(2,1)S(1)} async-done(((bf16[16,16,128]{2,1,0:T(8,128)(2,1)}), bf16[16,16,128]{2,1,0:T(8,128)(2,1)S(1)}, u32[]{:S(2)}, u32[]{:S(2)}) %all-to-all-start) | async-done | bytes 65568 | tf_op jit(solution)/shard_map/all_to_all | solution.py:383
  18.1 1.8 %charges.1 = s16[128,16,128]{2,1,0:T(8,128)(2,1)} custom-call(f32[4,128]{1,0:T(4,128)S(1)} %get-tuple-element.16.goes_ref, bf16[16,16,128]{2,1,0:T(8,128)(2,1)S(1)} %all-to-all-done.proj_ref, bf16[8,64,128]{2,1,0:T(8,128)(2,1)S(1)} %get-tuple-element.18.block_ref), custom_call_target="tpu_custom_call" | custom-call | flops 200000000 | bytes 7000000 | tf_op jit(solution)/shard_map/charges/pallas_call | solution.py:406
  19.9 5.6 %all-to-all-start.1 = ((s16[128,16,128]{2,1,0:T(8,128)(2,1)}), s16[128,16,128]{2,1,0:T(8,128)(2,1)S(1)}, u32[]{:S(2)}, u32[]{:S(2)}) async-start(s16[128,16,128]{2,1,0:T(8,128)(2,1)} %charges.1), calls=%async_computation.1 | async-start | bytes 1048576 | tf_op jit(solution)/shard_map/all_to_all | solution.py:415
  25.5 1.1 %collective-permute-start.1 = (bf16[1,9,512]{2,1,0:T(8,128)(2,1)S(1)}, bf16[1,9,512]{2,1,0:T(8,128)(2,1)S(1)}, u32[]{:S(2)}, u32[]{:S(2)}) collective-permute-start(bf16[1,9,512]{2,1,0:T(8,128)(2,1)S(1)} %copy-done.7), channel_id=1, source_target_pairs={{8,0},{16,8},{24,16},{32,24},{40,32},{48,40},{56,48},{64,56},{72,6... | collective-permute-start | bytes 27656 | tf_op jit(solution)/shard_map/ppermute | solution.py:363
  26.7 4.2 %collective-permute-done.1.next_proj_ref = bf16[1,9,512]{2,1,0:T(8,128)(2,1)S(1)} collective-permute-done((bf16[1,9,512]{2,1,0:T(8,128)(2,1)S(1)}, bf16[1,9,512]{2,1,0:T(8,128)(2,1)S(1)}, u32[]{:S(2)}, u32[]{:S(2)}) %collective-permute-start.1) | collective-permute-done | bytes 9248 | tf_op jit(solution)/shard_map/ppermute | solution.py:363
  30.8 0.0 collective-permute-done.next_ref
  30.8 8.1 %all-to-all-done.1.charge_ref = s16[128,16,128]{2,1,0:T(8,128)(2,1)S(1)} async-done(((s16[128,16,128]{2,1,0:T(8,128)(2,1)}), s16[128,16,128]{2,1,0:T(8,128)(2,1)S(1)}, u32[]{:S(2)}, u32[]{:S(2)}) %all-to-all-start.1) | async-done | bytes 524320 | tf_op jit(solution)/shard_map/all_to_all | solution.py:415
  38.9 0.0 copy-done.1
  38.9 4.0 %density1.1 = s16[8,18,16,128]{3,2,1,0:T(8,128)(2,1)} custom-call(s32[4,128]{1,0:T(4,128)S(1)} %get-tuple-element.14.place_vmem, f32[4,128]{1,0:T(4,128)S(1)} %get-tuple-element.15.here_ref, s16[128,16,128]{2,1,0:T(8,128)(2,1)S(1)} %all-to-all-done.1.charge_ref, bf16[1,16,128,128]{3,2,1,0:T(8,128)(2,1)S(1)} %copy-done, ...), custom_call_target="tpu_custom_call" | custom-call | flops 600000000 | bytes 21000000 | tf_op jit(solution)/shard_map/density1/pallas_call | solution.py:422
  42.9 3.6 %all-to-all-start.2 = ((s16[8,18,16,128]{3,2,1,0:T(8,128)(2,1)}), s16[8,18,16,128]{3,2,1,0:T(8,128)(2,1)S(1)}, u32[]{:S(2)}, u32[]{:S(2)}) async-start(s16[8,18,16,128]{3,2,1,0:T(8,128)(2,1)} %density1.1), calls=%async_computation.2 | async-start | bytes 1179648 | tf_op jit(solution)/shard_map/all_to_all | solution.py:449
  46.5 0.0 copy-start.2
  46.5 0.0 copy-start.5
  46.5 0.0 copy-start.8
  46.5 0.0 copy-start.9
  46.5 3.1 %density0.1.rest_0_ = s16[8,18,16,128]{3,2,1,0:T(8,128)(2,1)S(1)} custom-call(s32[4,128]{1,0:T(4,128)S(1)} %get-tuple-element.14.place_vmem, f32[4,128]{1,0:T(4,128)S(1)} %get-tuple-element.15.here_ref, s16[128,16,128]{2,1,0:T(8,128)(2,1)S(1)} %all-to-all-done.1.charge_ref, bf16[1,16,128,128]{3,2,1,0:T(8,128)(2,1)S(1)} %copy-done, ...), custom_call_target="tpu_custom_call" | custom-call | flops 600000000 | bytes 21000000 | tf_op jit(solution)/shard_map/density0/pallas_call | solution.py:422
  49.7 4.4 %all-to-all-done.2.in_ref = s16[8,18,16,128]{3,2,1,0:T(8,128)(2,1)S(1)} async-done(((s16[8,18,16,128]{3,2,1,0:T(8,128)(2,1)}), s16[8,18,16,128]{3,2,1,0:T(8,128)(2,1)S(1)}, u32[]{:S(2)}, u32[]{:S(2)}) %all-to-all-start.2) | async-done | bytes 589856 | tf_op jit(solution)/shard_map/all_to_all | solution.py:449
  54.1 1.5 %solve1.1 = s16[8,35,16,128]{3,2,1,0:T(8,128)(2,1)S(1)} custom-call(f32[8,16]{1,0:T(8,128)S(1)} %copy-done.8, s16[8,18,16,128]{3,2,1,0:T(8,128)(2,1)S(1)} %all-to-all-done.2.in_ref, f32[128,128]{1,0:T(8,128)S(1)} %copy-done.5, f32[1,128]{1,0:T(1,128)S(1)} %copy-done.9, bf16[128,384]{1,0:T(8,128)(2,1)S(1)} %copy-done.2, ...), custom_call_target="tpu_custom_call" | custom-call | flops 300000000 | bytes 10500000 | tf_op jit(solution)/shard_map/solve1/pallas_call | solution.py:439
  55.6 0.0 copy-start.4
  55.6 18.3 %all_to_all.25.in_ref = s16[8,35,16,128]{3,2,1,0:T(8,128)(2,1)S(1)} all-to-all(s16[8,35,16,128]{3,2,1,0:T(8,128)(2,1)S(1)} %solve1.1), channel_id=1, replica_groups={{0,2,4,6,7,5,3,1},{8,10,12,14,15,13,11,9},{16,18,20,22,23,21,19,17},{24..., dimensions={0} | all-to-all | bytes 2293760 | tf_op jit(solution)/shard_map/all_to_all | solution.py:449
  73.9 1.0 %back_cross.1 = (f32[16,128,128]{2,1,0:T(8,128)S(1)}, s16[2064,128]{1,0:T(8,128)(2,1)S(1)}) custom-call(s16[8,35,16,128]{3,2,1,0:T(8,128)(2,1)S(1)} %all_to_all.25.in_ref, bf16[1,16,128,128]{3,2,1,0:T(8,128)(2,1)S(1)} %copy-done, bf16[1,16,128,128]{3,2,1,0:T(8,128)(2,1)S(1)} %collective-permute-done.next_ref, bf16[128,384]{1,0:T(8,128)(2,1)S(1)} %copy-done.4, ...), custom_call_target="tpu_custom_call" | custom-call | flops 200000000 | bytes 7000000 | tf_op jit(solution)/shard_map/back_cross/pallas_call | solution.py:457
  74.9 7.6 %collective-permute-start.2 = (s16[2064,128]{1,0:T(8,128)(2,1)S(1)}, s16[2064,128]{1,0:T(8,128)(2,1)S(1)}, u32[]{:S(2)}, u32[]{:S(2)}) collective-permute-start(s16[2064,128]{1,0:T(8,128)(2,1)S(1)} %get-tuple-element.22), channel_id=1, source_target_pairs={{120,0},{0,8},{8,16},{16,24},{24,32},{32,40},{40,48},{48,56},{56,6... | collective-permute-start | bytes 1585160 | tf_op jit(solution)/shard_map/ppermute | solution.py:363
  82.5 1.5 %solve0.1 = s16[8,17,16,128]{3,2,1,0:T(8,128)(2,1)S(1)} custom-call(f32[8,16]{1,0:T(8,128)S(1)} %copy-done.8, s16[8,35,16,128]{3,2,1,0:T(8,128)(2,1)S(1)} %all_to_all.25.in_ref, f32[128,128]{1,0:T(8,128)S(1)} %copy-done.5, f32[1,128]{1,0:T(1,128)S(1)} %copy-done.9, bf16[128,384]{1,0:T(8,128)(2,1)S(1)} %copy-done.2), custom_call_target="tpu_custom_call" | custom-call | flops 300000000 | bytes 10500000 | tf_op jit(solution)/shard_map/solve0/pallas_call | solution.py:439
  84.0 11.0 %all_to_all.26.in_ref = s16[8,17,16,128]{3,2,1,0:T(8,128)(2,1)S(1)} all-to-all(s16[8,17,16,128]{3,2,1,0:T(8,128)(2,1)S(1)} %solve0.1), channel_id=1, replica_groups={{0,2,4,6,7,5,3,1},{8,10,12,14,15,13,11,9},{16,18,20,22,23,21,19,17},{24..., dimensions={0} | all-to-all | bytes 1114112 | tf_op jit(solution)/shard_map/all_to_all | solution.py:449
  95.1 0.0 collective-permute-done.2.sent_ref
  95.1 1.6 %back_own.1 = f32[1,16,128,128]{3,2,1,0:T(8,128)} custom-call(s16[8,17,16,128]{3,2,1,0:T(8,128)(2,1)S(1)} %all_to_all.26.in_ref, bf16[1,16,128,128]{3,2,1,0:T(8,128)(2,1)S(1)} %copy-done, f32[16,128,128]{2,1,0:T(8,128)S(1)} %get-tuple-element.21.kept_ref, s16[2064,128]{1,0:T(8,128)(2,1)S(1)} %collective-permute-done.2.sent_ref, ...), custom_call_target="tpu_custom_call" | custom-call | flops 200000000 | bytes 7000000 | tf_op jit(solution)/shard_map/back_own/pallas_call | solution.py:469
  (15 shorter events, 0.0 us)
Async XLA Ops:
  0.0 0.7 copy-start.6
  1.4 24.1 %copy-start.7 = (bf16[1,9,512]{2,1,0:T(8,128)(2,1)S(1)}, bf16[1,9,512]{2,1,0:T(8,128)(2,1)}, u32[]{:S(2)}) copy-start(bf16[1,9,512]{2,1,0:T(8,128)(2,1)} %next_proj_ref) | copy-start | bytes 27652
  1.5 37.5 %copy-start = (bf16[1,16,128,128]{3,2,1,0:T(8,128)(2,1)S(1)}, bf16[1,16,128,128]{3,2,1,0:T(8,128)(2,1)}, u32[]{:S(2)}) copy-start(bf16[1,16,128,128]{3,2,1,0:T(8,128)(2,1)} %own_ref.3) | copy-start | bytes 1572868
  1.5 37.5 %copy-start.1 = (bf16[256,256]{1,0:T(8,128)(2,1)S(1)}, bf16[256,256]{1,0:T(8,128)(2,1)}, u32[]{:S(2)}) copy-start(bf16[256,256]{1,0:T(8,128)(2,1)} %constant.14.clone.right_ref) | copy-start | bytes 393220
  1.5 37.5 %copy-start.3 = (bf16[128,384]{1,0:T(8,128)(2,1)S(1)}, bf16[128,384]{1,0:T(8,128)(2,1)}, u32[]{:S(2)}) copy-start(bf16[128,384]{1,0:T(8,128)(2,1)} %constant.16.clone.left_ref) | copy-start | bytes 294916
  1.5 16.6 %all-to-all-start = ((bf16[16,16,128]{2,1,0:T(8,128)(2,1)}), bf16[16,16,128]{2,1,0:T(8,128)(2,1)S(1)}, u32[]{:S(2)}, u32[]{:S(2)}) async-start(bf16[16,16,128]{2,1,0:T(8,128)(2,1)} %messages.1.after_ref), calls=%async_computation | async-start | bytes 131072 | tf_op jit(solution)/shard_map/all_to_all | solution.py:383
  10.7 0.9 copy-start.10
  11.6 0.7 copy-start.11
  13.0 17.9 %collective-permute-start = (bf16[1,16,128,128]{3,2,1,0:T(8,128)(2,1)}, bf16[1,16,128,128]{3,2,1,0:T(8,128)(2,1)S(1)}, u32[]{:S(2)}, u32[]{:S(2)}) collective-permute-start(bf16[1,16,128,128]{3,2,1,0:T(8,128)(2,1)} %own_ref.3), channel_id=1, source_target_pairs={{8,0},{16,8},{24,16},{32,24},{40,32},{48,40},{56,48},{64,56},{72,6... | collective-permute-start | bytes 1572872 | tf_op jit(solution)/shard_map/ppermute | solution.py:363
  19.9 19.0 %all-to-all-start.1 = ((s16[128,16,128]{2,1,0:T(8,128)(2,1)}), s16[128,16,128]{2,1,0:T(8,128)(2,1)S(1)}, u32[]{:S(2)}, u32[]{:S(2)}) async-start(s16[128,16,128]{2,1,0:T(8,128)(2,1)} %charges.1), calls=%async_computation.1 | async-start | bytes 1048576 | tf_op jit(solution)/shard_map/all_to_all | solution.py:415
  25.5 5.3 %collective-permute-start.1 = (bf16[1,9,512]{2,1,0:T(8,128)(2,1)S(1)}, bf16[1,9,512]{2,1,0:T(8,128)(2,1)S(1)}, u32[]{:S(2)}, u32[]{:S(2)}) collective-permute-start(bf16[1,9,512]{2,1,0:T(8,128)(2,1)S(1)} %copy-done.7), channel_id=1, source_target_pairs={{8,0},{16,8},{24,16},{32,24},{40,32},{48,40},{56,48},{64,56},{72,6... | collective-permute-start | bytes 27656 | tf_op jit(solution)/shard_map/ppermute | solution.py:363
  42.9 11.2 %all-to-all-start.2 = ((s16[8,18,16,128]{3,2,1,0:T(8,128)(2,1)}), s16[8,18,16,128]{3,2,1,0:T(8,128)(2,1)S(1)}, u32[]{:S(2)}, u32[]{:S(2)}) async-start(s16[8,18,16,128]{3,2,1,0:T(8,128)(2,1)} %density1.1), calls=%async_computation.2 | async-start | bytes 1179648 | tf_op jit(solution)/shard_map/all_to_all | solution.py:449
  46.5 7.6 %copy-start.2 = (bf16[128,384]{1,0:T(8,128)(2,1)S(1)}, bf16[128,384]{1,0:T(8,128)(2,1)}, u32[]{:S(2)}) copy-start(bf16[128,384]{1,0:T(8,128)(2,1)} %constant.15.clone.left_ref) | copy-start | bytes 294916
  46.5 7.6 %copy-start.5 = (f32[128,128]{1,0:T(8,128)S(1)}, f32[128,128]{1,0:T(8,128)}, u32[]{:S(2)}) copy-start(f32[128,128]{1,0:T(8,128)} %constant.19.clone.fold_x_ref) | copy-start | bytes 196612
  46.5 7.6 %copy-start.8 = (f32[8,16]{1,0:T(8,128)S(1)}, f32[8,16]{1,0:T(8,128)}, u32[]{:S(2)}) copy-start(f32[8,16]{1,0:T(8,128)} %constant.18.clone.squares_ref) | copy-start | bytes 1540
  46.5 7.6 %copy-start.9 = (f32[1,128]{1,0:T(1,128)S(1)}, f32[1,128]{1,0:T(1,128)}, u32[]{:S(2)}) copy-start(f32[1,128]{1,0:T(1,128)} %constant.20.clone.fold_z_ref) | copy-start | bytes 1540
  55.6 18.3 %copy-start.4 = (bf16[128,384]{1,0:T(8,128)(2,1)S(1)}, bf16[128,384]{1,0:T(8,128)(2,1)}, u32[]{:S(2)}) copy-start(bf16[128,384]{1,0:T(8,128)(2,1)} %constant.17.clone.left_ref) | copy-start | bytes 294916
  74.9 20.1 %collective-permute-start.2 = (s16[2064,128]{1,0:T(8,128)(2,1)S(1)}, s16[2064,128]{1,0:T(8,128)(2,1)S(1)}, u32[]{:S(2)}, u32[]{:S(2)}) collective-permute-start(s16[2064,128]{1,0:T(8,128)(2,1)S(1)} %get-tuple-element.22), channel_id=1, source_target_pairs={{120,0},{0,8},{8,16},{16,24},{24,32},{32,40},{40,48},{48,56},{56,6... | collective-permute-start | bytes 1585160 | tf_op jit(solution)/shard_map/ppermute | solution.py:363

commit v5 on v4

--- a/solution.py
+++ b/solution.py
@@ -19,7 +19,7 @@
 QMAX = 32760.0
 STEPS = 8.0
 CHANNEL_ROWS = 16
-ROUND = (0, 2, 4, 6, 7, 5, 3, 1)
+ROUND = (0, 1, 2, 3, 4, 5, 6, 7)
 FWD_TILES = PLANES + 2
 BACK_TILES = PLANES + 1
 BF = jnp.bfloat16
@@ -170,7 +170,7 @@
             weights[t] = jnp.where(lane // SLABS == b, mine[:, t : t + 1], weights[t])
     pieces = []
     for t in range(atoms):
-        behind = pltpu.roll(weights[t], NG - SLABS, 1)
+        behind = pltpu.roll(weights[t], SLABS, 1)
         picked = weights[t] * goes_ref[t : t + 1, :]
         pieces.append(jnp.concatenate([picked * weights[t], picked * behind], axis=1))
     weight = jnp.concatenate(pieces, axis=0)
@@ -193,20 +193,20 @@
         copy.wait()
 
 
-def density_kernel(p, place_vmem, here_ref, charge_ref, own_ref, next_ref, proj_ref, next_proj_ref, right_ref, left_ref, out_ref, field, second, scales, place_ref, sem):
+def density_kernel(p, place_vmem, here_ref, charge_ref, own_ref, prev_ref, proj_ref, prev_proj_ref, right_ref, left_ref, out_ref, field, second, scales, place_ref, sem):
     fetch = pltpu.make_async_copy(place_vmem, place_ref, sem)
     fetch.start()
     rows, owners = here_ref.shape[0], charge_ref.shape[0]
     count = owners // rows
     atoms = NG // count
     own_lane = lax.broadcasted_iota(jnp.int32, (count, NG), 1) // atoms == lax.broadcasted_iota(jnp.int32, (count, NG), 0)
-    sizes = jnp.sum(jnp.abs(proj_ref[0].astype(F32) * next_proj_ref[0].astype(F32)), axis=0, keepdims=True)
+    sizes = jnp.sum(jnp.abs(proj_ref[0].astype(F32) * prev_proj_ref[0].astype(F32)), axis=0, keepdims=True)
     for r in range(rows):
         bound = sizes[:, r * NG : (r + 1) * NG] * here_ref[r : r + 1, :]
         total = jnp.sum(jnp.where(own_lane, bound, 0.0), axis=1, keepdims=True)
         scales[pl.ds(r * count, count), :] = jnp.broadcast_to(total, (count, NG))
     for x in range(PLANES):
-        field[x] = own_ref[0, x].astype(F32) * next_ref[0, x].astype(F32)
+        field[x] = own_ref[0, x].astype(F32) * prev_ref[0, x].astype(F32)
     lane = lax.broadcasted_iota(jnp.int32, (8, NG), 1)
     fetch.wait()
 
@@ -301,13 +301,13 @@
     return both[:NG], both[NG:]
 
 
-def back_cross_kernel(in_ref, own_ref, next_ref, left_ref, right_ref, kept_ref, sent_ref, codes):
+def back_cross_kernel(in_ref, own_ref, prev_ref, left_ref, right_ref, kept_ref, sent_ref, codes):
     steps = [step_size(from_int16(in_ref[s, PLANES])) for s in range(SLABS)]
     for x in range(0, PLANES, 2):
         pair = potential_pair(in_ref, steps, x, left_ref, right_ref)
         for k in range(2):
             potential = pair[k]
-            kept_ref[x + k] = potential * next_ref[0, x + k].astype(F32)
+            kept_ref[x + k] = potential * prev_ref[0, x + k].astype(F32)
             product = potential * own_ref[0, x + k].astype(F32)
             code = step_code(jnp.max(jnp.abs(product), axis=0, keepdims=True))
             codes[x + k : x + k + 1, :] = code
@@ -399,9 +399,10 @@
         "local",
         1,
     )(messages, atom_home, aug_blocks.transpose(0, 2, 1, 3))
-    own, proj, blocks = lax.optimization_barrier((orbitals, projections, blocks))
-    next_proj = from_behind(proj, "band", -1)
-    nxt = from_behind(own, "band", -1)
+    own = orbitals
+    proj, blocks = lax.optimization_barrier((projections, blocks))
+    prev_proj = from_behind(proj, "band", 1)
+    prev = from_behind(own, "band", 1)
 
     charges = call(
         charge_kernel,
@@ -450,7 +451,7 @@
             block, "slab", split_axis=0, concat_axis=0, tiled=True, axis_index_groups=[list(ROUND)]
         )
 
-    cross = swap(density(1, nxt, next_proj))
+    cross = swap(density(1, prev, prev_proj))
     cross = swap(solve("solve1", 0, cross, density(0, own, proj)))
     mine = swap(solve("solve0", BACK_TILES, cross))
 
@@ -464,8 +465,8 @@
         [pltpu.VMEM((PLANES, NG), F32)],
         "back_cross",
         2,
-    )(cross, own, nxt, left_y_back, right)
-    got = from_behind(sent, "band", 1)
+    )(cross, own, prev, left_y_back, right)
+    got = from_behind(sent, "band", -1)
     return call(
         back_own_kernel,
         [vmem()] * 6,

time: 97.2 us -> 96.8 us (level)
  waiting for transfers between devices: 21.6 us -> 17.6 us
  blocking collectives: 29.3 us -> 32.2 us
    ppermute x3, waiting for transfers between devices: 4.18 us -> 0.88 us  [from_behind(): lax.ppermute(block, axis, [((i - distance) % count, i) for i in range(cou...]
    all_to_all x1, waiting for transfers between devices: 4.95 us -> 1.99 us  [per_device(): lax.all_to_all(messages, 'band', split_axis=0, concat_axis=0, tiled=True,...]
    all_to_all x2, blocking collectives: 29.3 us -> 32.2 us  [swap(): lax.all_to_all(block, 'slab', split_axis=0, concat_axis=0, tiled=True, ax...]
    all_to_all x1, waiting for transfers between devices: 4.43 us -> 5.8 us  [swap(): lax.all_to_all(block, 'slab', split_axis=0, concat_axis=0, tiled=True, ax...]
where the time goes in v5:
time: 96.8 us; the launch traced here: 96.3 us
  blocking collectives  32.2 us (33%)
  starting transfers between devices  28 us (29%)
  waiting for transfers between devices  17.6 us (18%)
  Pallas kernels  15.9 us (16%)
  local copies, waits for them, and re-layouts  2.35 us (2%)
    all_to_all x2, blocking collectives, swap(): lax.all_to_all(block, 'slab', split_axis=0, concat_axis=0, tiled=True, ax...  32.2 us
    ppermute x3, starting transfers between devices, from_behind(): lax.ppermute(block, axis, [((i - distance) % count, i) for i in range(cou...  9.62 us
    all_to_all x1, starting transfers between devices, per_device(): lax.all_to_all(messages, 'band', split_axis=0, concat_axis=0, tiled=True,...  9.27 us
    all_to_all x1, waiting for transfers between devices, per_device(): lax.all_to_all(charges, ('band', 'slab'), split_axis=0, concat_axis=0, ti...  8.93 us
    pallas_call x2, Pallas kernels, density(): call(functools.partial(density_kernel, p), [vmem()] * 9, jax.ShapeDtypeSt...  7.11 us
    all_to_all x1, waiting for transfers between devices, swap(): lax.all_to_all(block, 'slab', split_axis=0, concat_axis=0, tiled=True, ax...  5.8 us
    all_to_all x1, starting transfers between devices, per_device(): lax.all_to_all(charges, ('band', 'slab'), split_axis=0, concat_axis=0, ti...  5.57 us
    all_to_all x1, starting transfers between devices, swap(): lax.all_to_all(block, 'slab', split_axis=0, concat_axis=0, tiled=True, ax...  3.55 us
  transfers between devices with their start and end apart: 6, of which 4 were waited for; matrix products, arithmetic and copies ran while one was open for 0% of the time, Pallas kernels for 7%

profile of v5, /device:TPU:1, one launch (start us, length us, event | category | flops | bytes accessed | tf_op | source)
XLA Modules:
  0.0 96.3 jit_solution(12636155136441926266)
XLA Ops:
  0.0 0.7 copy-done.6
  0.7 0.7 messages.1.after_ref
  1.5 9.3 %all-to-all-start = ((bf16[16,16,128]{2,1,0:T(8,128)(2,1)}), bf16[16,16,128]{2,1,0:T(8,128)(2,1)S(1)}, u32[]{:S(2)}, u32[]{:S(2)}) async-start(bf16[16,16,128]{2,1,0:T(8,128)(2,1)} %messages.1.after_ref), calls=%async_computation | async-start | bytes 131072 | tf_op jit(solution)/shard_map/all_to_all | solution.py:383
  10.7 3.1 %collective-permute-start = (bf16[1,16,128,128]{3,2,1,0:T(8,128)(2,1)}, bf16[1,16,128,128]{3,2,1,0:T(8,128)(2,1)S(1)}, u32[]{:S(2)}, u32[]{:S(2)}) collective-permute-start(bf16[1,16,128,128]{3,2,1,0:T(8,128)(2,1)} %own_ref.7), channel_id=1, source_target_pairs={{120,0},{0,8},{8,16},{16,24},{24,32},{32,40},{40,48},{48,56},{56,6... | collective-permute-start | bytes 1572872 | tf_op jit(solution)/shard_map/ppermute | solution.py:363
  13.9 0.9 copy-done.10
  14.8 0.7 copy-done.11
  15.5 0.7 local.1
  16.1 2.0 %all-to-all-done.proj_ref = bf16[16,16,128]{2,1,0:T(8,128)(2,1)S(1)} async-done(((bf16[16,16,128]{2,1,0:T(8,128)(2,1)}), bf16[16,16,128]{2,1,0:T(8,128)(2,1)S(1)}, u32[]{:S(2)}, u32[]{:S(2)}) %all-to-all-start) | async-done | bytes 65568 | tf_op jit(solution)/shard_map/all_to_all | solution.py:383
  18.1 1.8 %charges.1 = s16[128,16,128]{2,1,0:T(8,128)(2,1)} custom-call(f32[4,128]{1,0:T(4,128)S(1)} %get-tuple-element.15.goes_ref, bf16[16,16,128]{2,1,0:T(8,128)(2,1)S(1)} %all-to-all-done.proj_ref, bf16[8,64,128]{2,1,0:T(8,128)(2,1)S(1)} %get-tuple-element.17.block_ref), custom_call_target="tpu_custom_call" | custom-call | flops 200000000 | bytes 7000000 | tf_op jit(solution)/shard_map/charges/pallas_call | solution.py:407
  19.9 5.6 %all-to-all-start.1 = ((s16[128,16,128]{2,1,0:T(8,128)(2,1)}), s16[128,16,128]{2,1,0:T(8,128)(2,1)S(1)}, u32[]{:S(2)}, u32[]{:S(2)}) async-start(s16[128,16,128]{2,1,0:T(8,128)(2,1)} %charges.1), calls=%async_computation.1 | async-start | bytes 1048576 | tf_op jit(solution)/shard_map/all_to_all | solution.py:416
  25.5 0.0 copy-done.7
  25.5 3.6 %collective-permute-start.1 = (bf16[1,9,512]{2,1,0:T(8,128)(2,1)S(1)}, bf16[1,9,512]{2,1,0:T(8,128)(2,1)S(1)}, u32[]{:S(2)}, u32[]{:S(2)}) collective-permute-start(bf16[1,9,512]{2,1,0:T(8,128)(2,1)S(1)} %copy-done.7), channel_id=1, source_target_pairs={{120,0},{0,8},{8,16},{16,24},{24,32},{32,40},{40,48},{48,56},{56,6... | collective-permute-start | bytes 27656 | tf_op jit(solution)/shard_map/ppermute | solution.py:363
  29.1 0.9 collective-permute-done.1.prev_proj_ref
  30.0 0.0 collective-permute-done.prev_ref
  30.0 8.9 %all-to-all-done.1.charge_ref = s16[128,16,128]{2,1,0:T(8,128)(2,1)S(1)} async-done(((s16[128,16,128]{2,1,0:T(8,128)(2,1)}), s16[128,16,128]{2,1,0:T(8,128)(2,1)S(1)}, u32[]{:S(2)}, u32[]{:S(2)}) %all-to-all-start.1) | async-done | bytes 524320 | tf_op jit(solution)/shard_map/all_to_all | solution.py:416
  38.9 4.0 %density1.1 = s16[8,18,16,128]{3,2,1,0:T(8,128)(2,1)} custom-call(s32[4,128]{1,0:T(4,128)S(1)} %get-tuple-element.13.place_vmem, f32[4,128]{1,0:T(4,128)S(1)} %get-tuple-element.14.here_ref, s16[128,16,128]{2,1,0:T(8,128)(2,1)S(1)} %all-to-all-done.1.charge_ref, bf16[1,16,128,128]{3,2,1,0:T(8,128)(2,1)S(1)} %copy-done, ...), custom_call_target="tpu_custom_call" | custom-call | flops 600000000 | bytes 21000000 | tf_op jit(solution)/shard_map/density1/pallas_call | solution.py:423
  42.9 3.6 %all-to-all-start.2 = ((s16[8,18,16,128]{3,2,1,0:T(8,128)(2,1)}), s16[8,18,16,128]{3,2,1,0:T(8,128)(2,1)S(1)}, u32[]{:S(2)}, u32[]{:S(2)}) async-start(s16[8,18,16,128]{3,2,1,0:T(8,128)(2,1)} %density1.1), calls=%async_computation.2 | async-start | bytes 1179648 | tf_op jit(solution)/shard_map/all_to_all | solution.py:450
  46.5 0.0 copy-start.2
  46.5 0.0 copy-start.5
  46.5 0.0 copy-start.8
  46.5 0.0 copy-start.9
  46.5 3.1 %density0.1.rest_0_ = s16[8,18,16,128]{3,2,1,0:T(8,128)(2,1)S(1)} custom-call(s32[4,128]{1,0:T(4,128)S(1)} %get-tuple-element.13.place_vmem, f32[4,128]{1,0:T(4,128)S(1)} %get-tuple-element.14.here_ref, s16[128,16,128]{2,1,0:T(8,128)(2,1)S(1)} %all-to-all-done.1.charge_ref, bf16[1,16,128,128]{3,2,1,0:T(8,128)(2,1)S(1)} %copy-done, ...), custom_call_target="tpu_custom_call" | custom-call | flops 600000000 | bytes 21000000 | tf_op jit(solution)/shard_map/density0/pallas_call | solution.py:423
  49.7 5.8 %all-to-all-done.2.in_ref = s16[8,18,16,128]{3,2,1,0:T(8,128)(2,1)S(1)} async-done(((s16[8,18,16,128]{3,2,1,0:T(8,128)(2,1)}), s16[8,18,16,128]{3,2,1,0:T(8,128)(2,1)S(1)}, u32[]{:S(2)}, u32[]{:S(2)}) %all-to-all-start.2) | async-done | bytes 589856 | tf_op jit(solution)/shard_map/all_to_all | solution.py:450
  55.5 1.5 %solve1.1 = s16[8,35,16,128]{3,2,1,0:T(8,128)(2,1)S(1)} custom-call(f32[8,16]{1,0:T(8,128)S(1)} %copy-done.8, s16[8,18,16,128]{3,2,1,0:T(8,128)(2,1)S(1)} %all-to-all-done.2.in_ref, f32[128,128]{1,0:T(8,128)S(1)} %copy-done.5, f32[1,128]{1,0:T(1,128)S(1)} %copy-done.9, bf16[128,384]{1,0:T(8,128)(2,1)S(1)} %copy-done.2, ...), custom_call_target="tpu_custom_call" | custom-call | flops 300000000 | bytes 10500000 | tf_op jit(solution)/shard_map/solve1/pallas_call | solution.py:440
  57.0 0.0 copy-start.4
  57.0 18.7 %all_to_all.25.in_ref = s16[8,35,16,128]{3,2,1,0:T(8,128)(2,1)S(1)} all-to-all(s16[8,35,16,128]{3,2,1,0:T(8,128)(2,1)S(1)} %solve1.1), channel_id=1, replica_groups={{0,1,2,3,4,5,6,7},{8,9,10,11,12,13,14,15},{16,17,18,19,20,21,22,23},{24..., dimensions={0} | all-to-all | bytes 2293760 | tf_op jit(solution)/shard_map/all_to_all | solution.py:450
  75.7 1.0 %back_cross.1 = (f32[16,128,128]{2,1,0:T(8,128)S(1)}, s16[2064,128]{1,0:T(8,128)(2,1)S(1)}) custom-call(s16[8,35,16,128]{3,2,1,0:T(8,128)(2,1)S(1)} %all_to_all.25.in_ref, bf16[1,16,128,128]{3,2,1,0:T(8,128)(2,1)S(1)} %copy-done, bf16[1,16,128,128]{3,2,1,0:T(8,128)(2,1)S(1)} %collective-permute-done.prev_ref, bf16[128,384]{1,0:T(8,128)(2,1)S(1)} %copy-done.4, ...), custom_call_target="tpu_custom_call" | custom-call | flops 200000000 | bytes 7000000 | tf_op jit(solution)/shard_map/back_cross/pallas_call | solution.py:458
  76.7 2.9 %collective-permute-start.2 = (s16[2064,128]{1,0:T(8,128)(2,1)S(1)}, s16[2064,128]{1,0:T(8,128)(2,1)S(1)}, u32[]{:S(2)}, u32[]{:S(2)}) collective-permute-start(s16[2064,128]{1,0:T(8,128)(2,1)S(1)} %get-tuple-element.20), channel_id=1, source_target_pairs={{8,0},{16,8},{24,16},{32,24},{40,32},{48,40},{56,48},{64,56},{72,6... | collective-permute-start | bytes 1585160 | tf_op jit(solution)/shard_map/ppermute | solution.py:363
  79.6 1.5 %solve0.1 = s16[8,17,16,128]{3,2,1,0:T(8,128)(2,1)S(1)} custom-call(f32[8,16]{1,0:T(8,128)S(1)} %copy-done.8, s16[8,35,16,128]{3,2,1,0:T(8,128)(2,1)S(1)} %all_to_all.25.in_ref, f32[128,128]{1,0:T(8,128)S(1)} %copy-done.5, f32[1,128]{1,0:T(1,128)S(1)} %copy-done.9, bf16[128,384]{1,0:T(8,128)(2,1)S(1)} %copy-done.2), custom_call_target="tpu_custom_call" | custom-call | flops 300000000 | bytes 10500000 | tf_op jit(solution)/shard_map/solve0/pallas_call | solution.py:440
  81.1 13.5 %all_to_all.26.in_ref = s16[8,17,16,128]{3,2,1,0:T(8,128)(2,1)S(1)} all-to-all(s16[8,17,16,128]{3,2,1,0:T(8,128)(2,1)S(1)} %solve0.1), channel_id=1, replica_groups={{0,1,2,3,4,5,6,7},{8,9,10,11,12,13,14,15},{16,17,18,19,20,21,22,23},{24..., dimensions={0} | all-to-all | bytes 1114112 | tf_op jit(solution)/shard_map/all_to_all | solution.py:450
  94.6 0.0 collective-permute-done.2.sent_ref
  94.6 1.7 %back_own.1 = f32[1,16,128,128]{3,2,1,0:T(8,128)} custom-call(s16[8,17,16,128]{3,2,1,0:T(8,128)(2,1)S(1)} %all_to_all.26.in_ref, bf16[1,16,128,128]{3,2,1,0:T(8,128)(2,1)S(1)} %copy-done, f32[16,128,128]{2,1,0:T(8,128)S(1)} %get-tuple-element.19.kept_ref, s16[2064,128]{1,0:T(8,128)(2,1)S(1)} %collective-permute-done.2.sent_ref, ...), custom_call_target="tpu_custom_call" | custom-call | flops 200000000 | bytes 7000000 | tf_op jit(solution)/shard_map/back_own/pallas_call | solution.py:470
  (15 shorter events, 0.0 us)
Async XLA Ops:
  0.0 0.7 copy-start.6
  1.4 24.1 %copy-start.7 = (bf16[1,9,512]{2,1,0:T(8,128)(2,1)S(1)}, bf16[1,9,512]{2,1,0:T(8,128)(2,1)}, u32[]{:S(2)}) copy-start(bf16[1,9,512]{2,1,0:T(8,128)(2,1)} %prev_proj_ref) | copy-start | bytes 27652
  1.5 37.5 %copy-start = (bf16[1,16,128,128]{3,2,1,0:T(8,128)(2,1)S(1)}, bf16[1,16,128,128]{3,2,1,0:T(8,128)(2,1)}, u32[]{:S(2)}) copy-start(bf16[1,16,128,128]{3,2,1,0:T(8,128)(2,1)} %own_ref.7) | copy-start | bytes 1572868
  1.5 37.5 %copy-start.1 = (bf16[256,256]{1,0:T(8,128)(2,1)S(1)}, bf16[256,256]{1,0:T(8,128)(2,1)}, u32[]{:S(2)}) copy-start(bf16[256,256]{1,0:T(8,128)(2,1)} %constant.14.clone.right_ref) | copy-start | bytes 393220
  1.5 37.5 %copy-start.3 = (bf16[128,384]{1,0:T(8,128)(2,1)S(1)}, bf16[128,384]{1,0:T(8,128)(2,1)}, u32[]{:S(2)}) copy-start(bf16[128,384]{1,0:T(8,128)(2,1)} %constant.16.clone.left_ref) | copy-start | bytes 294916
  1.5 16.6 %all-to-all-start = ((bf16[16,16,128]{2,1,0:T(8,128)(2,1)}), bf16[16,16,128]{2,1,0:T(8,128)(2,1)S(1)}, u32[]{:S(2)}, u32[]{:S(2)}) async-start(bf16[16,16,128]{2,1,0:T(8,128)(2,1)} %messages.1.after_ref), calls=%async_computation | async-start | bytes 131072 | tf_op jit(solution)/shard_map/all_to_all | solution.py:383
  10.7 19.3 %collective-permute-start = (bf16[1,16,128,128]{3,2,1,0:T(8,128)(2,1)}, bf16[1,16,128,128]{3,2,1,0:T(8,128)(2,1)S(1)}, u32[]{:S(2)}, u32[]{:S(2)}) collective-permute-start(bf16[1,16,128,128]{3,2,1,0:T(8,128)(2,1)} %own_ref.7), channel_id=1, source_target_pairs={{120,0},{0,8},{8,16},{16,24},{24,32},{32,40},{40,48},{48,56},{56,6... | collective-permute-start | bytes 1572872 | tf_op jit(solution)/shard_map/ppermute | solution.py:363
  13.9 0.9 copy-start.10
  14.8 0.7 copy-start.11
  19.9 19.0 %all-to-all-start.1 = ((s16[128,16,128]{2,1,0:T(8,128)(2,1)}), s16[128,16,128]{2,1,0:T(8,128)(2,1)S(1)}, u32[]{:S(2)}, u32[]{:S(2)}) async-start(s16[128,16,128]{2,1,0:T(8,128)(2,1)} %charges.1), calls=%async_computation.1 | async-start | bytes 1048576 | tf_op jit(solution)/shard_map/all_to_all | solution.py:416
  25.5 4.5 %collective-permute-start.1 = (bf16[1,9,512]{2,1,0:T(8,128)(2,1)S(1)}, bf16[1,9,512]{2,1,0:T(8,128)(2,1)S(1)}, u32[]{:S(2)}, u32[]{:S(2)}) collective-permute-start(bf16[1,9,512]{2,1,0:T(8,128)(2,1)S(1)} %copy-done.7), channel_id=1, source_target_pairs={{120,0},{0,8},{8,16},{16,24},{24,32},{32,40},{40,48},{48,56},{56,6... | collective-permute-start | bytes 27656 | tf_op jit(solution)/shard_map/ppermute | solution.py:363
  42.9 12.6 %all-to-all-start.2 = ((s16[8,18,16,128]{3,2,1,0:T(8,128)(2,1)}), s16[8,18,16,128]{3,2,1,0:T(8,128)(2,1)S(1)}, u32[]{:S(2)}, u32[]{:S(2)}) async-start(s16[8,18,16,128]{3,2,1,0:T(8,128)(2,1)} %density1.1), calls=%async_computation.2 | async-start | bytes 1179648 | tf_op jit(solution)/shard_map/all_to_all | solution.py:450
  46.5 9.0 %copy-start.2 = (bf16[128,384]{1,0:T(8,128)(2,1)S(1)}, bf16[128,384]{1,0:T(8,128)(2,1)}, u32[]{:S(2)}) copy-start(bf16[128,384]{1,0:T(8,128)(2,1)} %constant.15.clone.left_ref) | copy-start | bytes 294916
  46.5 9.0 %copy-start.5 = (f32[128,128]{1,0:T(8,128)S(1)}, f32[128,128]{1,0:T(8,128)}, u32[]{:S(2)}) copy-start(f32[128,128]{1,0:T(8,128)} %constant.19.clone.fold_x_ref) | copy-start | bytes 196612
  46.5 9.0 %copy-start.8 = (f32[8,16]{1,0:T(8,128)S(1)}, f32[8,16]{1,0:T(8,128)}, u32[]{:S(2)}) copy-start(f32[8,16]{1,0:T(8,128)} %constant.18.clone.squares_ref) | copy-start | bytes 1540
  46.5 9.0 %copy-start.9 = (f32[1,128]{1,0:T(1,128)S(1)}, f32[1,128]{1,0:T(1,128)}, u32[]{:S(2)}) copy-start(f32[1,128]{1,0:T(1,128)} %constant.20.clone.fold_z_ref) | copy-start | bytes 1540
  57.0 18.7 %copy-start.4 = (bf16[128,384]{1,0:T(8,128)(2,1)S(1)}, bf16[128,384]{1,0:T(8,128)(2,1)}, u32[]{:S(2)}) copy-start(bf16[128,384]{1,0:T(8,128)(2,1)} %constant.17.clone.left_ref) | copy-start | bytes 294916
  76.7 17.9 %collective-permute-start.2 = (s16[2064,128]{1,0:T(8,128)(2,1)S(1)}, s16[2064,128]{1,0:T(8,128)(2,1)S(1)}, u32[]{:S(2)}, u32[]{:S(2)}) collective-permute-start(s16[2064,128]{1,0:T(8,128)(2,1)S(1)} %get-tuple-element.20), channel_id=1, source_target_pairs={{8,0},{16,8},{24,16},{32,24},{40,32},{48,40},{56,48},{64,56},{72,6... | collective-permute-start | bytes 1585160 | tf_op jit(solution)/shard_map/ppermute | solution.py:363

commit v6 on v5

--- a/solution.py
+++ b/solution.py
@@ -261,7 +261,15 @@
         out_ref[d, PLANES + 1] = to_int16(jnp.round(low))
 
 
-def solve_kernel(base, squares_ref, in_ref, fold_x_ref, fold_z_ref, left_ref, *rest):
+def table_kernel(after_ref, squares_ref, fold_x_ref, fold_z_ref, out_ref):
+    squares = squares_ref[pl.ds(lax.axis_index("slab"), 1), :]
+    fold = fold_x_ref[...] + fold_z_ref[...]
+    for r in range(ROWS):
+        total = fold + squares[:, r : r + 1]
+        out_ref[r] = jnp.where(total > 0, KERNEL_SCALE / (total + SCREENING_RANGE), 0.0) * (1.0 / NG**3)
+
+
+def solve_kernel(base, in_ref, table_ref, left_ref, *rest):
     *more, out_ref, field = rest
 
     for s in range(SLABS):
@@ -271,15 +279,9 @@
         rows = pl.ds(ROUND[s] * PLANES, PLANES)
         field[:, rows, :] = jnp.swapaxes(planes, 0, 1)
         field[0, rows, :] = field[0, rows, :] + low
-    fold = fold_x_ref[...] + fold_z_ref[...]
-    squares = squares_ref[pl.ds(lax.axis_index("slab"), 1), :]
     for r in range(0, ROWS, 2):
-        halves = []
-        for k in range(2):
-            total = fold + squares[:, r + k : r + k + 1]
-            halves.append(jnp.where(total > 0, KERNEL_SCALE / (total + SCREENING_RANGE), 0.0) * (1.0 / NG**3))
         columns = jnp.concatenate([field[r], field[r + 1]], axis=1)
-        spectrum = times_left(left_ref, columns) * jnp.concatenate(halves, axis=1)
+        spectrum = times_left(left_ref, columns) * jnp.concatenate([table_ref[r], table_ref[r + 1]], axis=1)
         columns = times_left(left_ref, spectrum)
         field[r] = columns[:, :NG]
         field[r + 1] = columns[:, NG:]
@@ -439,12 +441,12 @@
         tiles = BACK_TILES + FWD_TILES * len(more)
         return call(
             functools.partial(solve_kernel, base),
-            [vmem()] * (5 + len(more)),
+            [vmem()] * (3 + len(more)),
             jax.ShapeDtypeStruct((n_slab, tiles, 16, NG), jnp.int16),
             [pltpu.VMEM((ROWS, NG, NG), F32)],
             name,
             3,
-        )(fold_y, spectrum, fold_x, fold_z, left, *more)
+        )(spectrum, table, left, *more)
 
     def swap(block):
         return lax.all_to_all(
@@ -452,7 +454,16 @@
         )
 
     cross = swap(density(1, prev, prev_proj))
-    cross = swap(solve("solve1", 0, cross, density(0, own, proj)))
+    mine = density(0, own, proj)
+    table = call(
+        table_kernel,
+        [pl.BlockSpec(memory_space=pl.ANY)] + [vmem()] * 3,
+        jax.ShapeDtypeStruct((ROWS, NG, NG), F32),
+        [],
+        "table",
+        1,
+    )(mine, fold_y, fold_x, fold_z)
+    cross = swap(solve("solve1", 0, cross, mine))
     mine = swap(solve("solve0", BACK_TILES, cross))
 
     kept, sent = call(

time: 96.8 us -> 96.6 us (level)
    pallas_call x2 -> x3, Pallas kernels: 2.95 us -> 2.87 us  [the longest x2 2.53 us: solve(): call(functools.partial(solve_kernel, base), [vmem()] * (3 + len(more)), j...]
  transfers between devices with their start and end apart: 6 -> 6, of which waited for: 4 -> 4; matrix products, arithmetic and copies ran while one was open for 0% -> 0% of each run, Pallas kernels for 7% -> 8%
where the time goes in v6:
time: 96.6 us; the launch traced here: 96 us
  blocking collectives  32.5 us (34%)
  starting transfers between devices  28 us (29%)
  waiting for transfers between devices  17.2 us (18%)
  Pallas kernels  15.8 us (16%)
  local copies, waits for them, and re-layouts  2.35 us (2%)
    all_to_all x2, blocking collectives, swap(): lax.all_to_all(block, 'slab', split_axis=0, concat_axis=0, tiled=True, ax...  32.5 us
    ppermute x3, starting transfers between devices, from_behind(): lax.ppermute(block, axis, [((i - distance) % count, i) for i in range(cou...  9.61 us
    all_to_all x1, starting transfers between devices, per_device(): lax.all_to_all(messages, 'band', split_axis=0, concat_axis=0, tiled=True,...  9.27 us
    all_to_all x1, waiting for transfers between devices, per_device(): lax.all_to_all(charges, ('band', 'slab'), split_axis=0, concat_axis=0, ti...  8.93 us
    pallas_call x2, Pallas kernels, density(): call(functools.partial(density_kernel, p), [vmem()] * 9, jax.ShapeDtypeSt...  7.11 us
    all_to_all x1, starting transfers between devices, per_device(): lax.all_to_all(charges, ('band', 'slab'), split_axis=0, concat_axis=0, ti...  5.57 us
    all_to_all x1, waiting for transfers between devices, swap(): lax.all_to_all(block, 'slab', split_axis=0, concat_axis=0, tiled=True, ax...  5.42 us
    all_to_all x1, starting transfers between devices, swap(): lax.all_to_all(block, 'slab', split_axis=0, concat_axis=0, tiled=True, ax...  3.55 us
  transfers between devices with their start and end apart: 6, of which 4 were waited for; matrix products, arithmetic and copies ran while one was open for 0% of the time, Pallas kernels for 8%

profile of v6, /device:TPU:1, one launch (start us, length us, event | category | flops | bytes accessed | tf_op | source)
XLA Modules:
  0.0 96.0 jit_solution(687577366845852828)
XLA Ops:
  0.0 0.7 copy-done.5
  0.7 0.7 messages.1.after_ref
  1.5 9.3 %all-to-all-start = ((bf16[16,16,128]{2,1,0:T(8,128)(2,1)}), bf16[16,16,128]{2,1,0:T(8,128)(2,1)S(1)}, u32[]{:S(2)}, u32[]{:S(2)}) async-start(bf16[16,16,128]{2,1,0:T(8,128)(2,1)} %messages.1.after_ref), calls=%async_computation | async-start | bytes 131072 | tf_op jit(solution)/shard_map/all_to_all | solution.py:385
  10.7 3.1 %collective-permute-start = (bf16[1,16,128,128]{3,2,1,0:T(8,128)(2,1)}, bf16[1,16,128,128]{3,2,1,0:T(8,128)(2,1)S(1)}, u32[]{:S(2)}, u32[]{:S(2)}) collective-permute-start(bf16[1,16,128,128]{3,2,1,0:T(8,128)(2,1)} %own_ref.7), channel_id=1, source_target_pairs={{120,0},{0,8},{8,16},{16,24},{24,32},{32,40},{40,48},{48,56},{56,6... | collective-permute-start | bytes 1572872 | tf_op jit(solution)/shard_map/ppermute | solution.py:365
  13.9 0.9 copy-done.10
  14.8 0.7 copy-done.11
  15.5 0.7 local.1
  16.1 2.0 %all-to-all-done.proj_ref = bf16[16,16,128]{2,1,0:T(8,128)(2,1)S(1)} async-done(((bf16[16,16,128]{2,1,0:T(8,128)(2,1)}), bf16[16,16,128]{2,1,0:T(8,128)(2,1)S(1)}, u32[]{:S(2)}, u32[]{:S(2)}) %all-to-all-start) | async-done | bytes 65568 | tf_op jit(solution)/shard_map/all_to_all | solution.py:385
  18.1 1.8 %charges.1 = s16[128,16,128]{2,1,0:T(8,128)(2,1)} custom-call(f32[4,128]{1,0:T(4,128)S(1)} %get-tuple-element.15.goes_ref, bf16[16,16,128]{2,1,0:T(8,128)(2,1)S(1)} %all-to-all-done.proj_ref, bf16[8,64,128]{2,1,0:T(8,128)(2,1)S(1)} %get-tuple-element.17.block_ref), custom_call_target="tpu_custom_call" | custom-call | flops 200000000 | bytes 7000000 | tf_op jit(solution)/shard_map/charges/pallas_call | solution.py:409
  19.9 5.6 %all-to-all-start.1 = ((s16[128,16,128]{2,1,0:T(8,128)(2,1)}), s16[128,16,128]{2,1,0:T(8,128)(2,1)S(1)}, u32[]{:S(2)}, u32[]{:S(2)}) async-start(s16[128,16,128]{2,1,0:T(8,128)(2,1)} %charges.1), calls=%async_computation.1 | async-start | bytes 1048576 | tf_op jit(solution)/shard_map/all_to_all | solution.py:418
  25.5 3.6 %collective-permute-start.1 = (bf16[1,9,512]{2,1,0:T(8,128)(2,1)S(1)}, bf16[1,9,512]{2,1,0:T(8,128)(2,1)S(1)}, u32[]{:S(2)}, u32[]{:S(2)}) collective-permute-start(bf16[1,9,512]{2,1,0:T(8,128)(2,1)S(1)} %copy-done.6), channel_id=1, source_target_pairs={{120,0},{0,8},{8,16},{16,24},{24,32},{32,40},{40,48},{48,56},{56,6... | collective-permute-start | bytes 27656 | tf_op jit(solution)/shard_map/ppermute | solution.py:365
  29.1 0.9 collective-permute-done.1.prev_proj_ref
  30.0 0.0 collective-permute-done.prev_ref
  30.0 8.9 %all-to-all-done.1.charge_ref = s16[128,16,128]{2,1,0:T(8,128)(2,1)S(1)} async-done(((s16[128,16,128]{2,1,0:T(8,128)(2,1)}), s16[128,16,128]{2,1,0:T(8,128)(2,1)S(1)}, u32[]{:S(2)}, u32[]{:S(2)}) %all-to-all-start.1) | async-done | bytes 524320 | tf_op jit(solution)/shard_map/all_to_all | solution.py:418
  38.9 4.0 %density1.1 = s16[8,18,16,128]{3,2,1,0:T(8,128)(2,1)} custom-call(s32[4,128]{1,0:T(4,128)S(1)} %get-tuple-element.13.place_vmem, f32[4,128]{1,0:T(4,128)S(1)} %get-tuple-element.14.here_ref, s16[128,16,128]{2,1,0:T(8,128)(2,1)S(1)} %all-to-all-done.1.charge_ref, bf16[1,16,128,128]{3,2,1,0:T(8,128)(2,1)S(1)} %copy-done, ...), custom_call_target="tpu_custom_call" | custom-call | flops 600000000 | bytes 21000000 | tf_op jit(solution)/shard_map/density1/pallas_call | solution.py:425
  42.9 3.6 %all-to-all-start.2 = ((s16[8,18,16,128]{3,2,1,0:T(8,128)(2,1)}), s16[8,18,16,128]{3,2,1,0:T(8,128)(2,1)S(1)}, u32[]{:S(2)}, u32[]{:S(2)}) async-start(s16[8,18,16,128]{3,2,1,0:T(8,128)(2,1)} %density1.1), calls=%async_computation.2 | async-start | bytes 1179648 | tf_op jit(solution)/shard_map/all_to_all | solution.py:452
  46.5 0.0 copy-start.7
  46.5 0.0 copy-start.8
  46.5 0.0 copy-start.9
  46.5 3.1 %density0.1.after_ref.rest_0_ = s16[8,18,16,128]{3,2,1,0:T(8,128)(2,1)S(1)} custom-call(s32[4,128]{1,0:T(4,128)S(1)} %get-tuple-element.13.place_vmem, f32[4,128]{1,0:T(4,128)S(1)} %get-tuple-element.14.here_ref, s16[128,16,128]{2,1,0:T(8,128)(2,1)S(1)} %all-to-all-done.1.charge_ref, bf16[1,16,128,128]{3,2,1,0:T(8,128)(2,1)S(1)} %copy-done, ...), custom_call_target="tpu_custom_call" | custom-call | flops 600000000 | bytes 21000000 | tf_op jit(solution)/shard_map/density0/pallas_call | solution.py:425
  49.7 0.0 copy-start.4
  49.7 0.3 table.1.table_ref
  50.0 5.4 %all-to-all-done.2.in_ref = s16[8,18,16,128]{3,2,1,0:T(8,128)(2,1)S(1)} async-done(((s16[8,18,16,128]{3,2,1,0:T(8,128)(2,1)}), s16[8,18,16,128]{3,2,1,0:T(8,128)(2,1)S(1)}, u32[]{:S(2)}, u32[]{:S(2)}) %all-to-all-start.2) | async-done | bytes 589856 | tf_op jit(solution)/shard_map/all_to_all | solution.py:452
  55.5 1.3 %solve1.1 = s16[8,35,16,128]{3,2,1,0:T(8,128)(2,1)S(1)} custom-call(s16[8,18,16,128]{3,2,1,0:T(8,128)(2,1)S(1)} %all-to-all-done.2.in_ref, f32[16,128,128]{2,1,0:T(8,128)S(1)} %table.1.table_ref, bf16[128,384]{1,0:T(8,128)(2,1)S(1)} %copy-done.4, s16[8,18,16,128]{3,2,1,0:T(8,128)(2,1)S(1)} %density0.1.after_ref.rest_0_), custom_call_target="tpu_custom_call" | custom-call | flops 300000000 | bytes 10500000 | tf_op jit(solution)/shard_map/solve1/pallas_call | solution.py:442
  56.7 0.0 copy-start.3
  56.7 18.7 %all_to_all.25.in_ref = s16[8,35,16,128]{3,2,1,0:T(8,128)(2,1)S(1)} all-to-all(s16[8,35,16,128]{3,2,1,0:T(8,128)(2,1)S(1)} %solve1.1), channel_id=1, replica_groups={{0,1,2,3,4,5,6,7},{8,9,10,11,12,13,14,15},{16,17,18,19,20,21,22,23},{24..., dimensions={0} | all-to-all | bytes 2293760 | tf_op jit(solution)/shard_map/all_to_all | solution.py:452
  75.5 1.0 %back_cross.1 = (f32[16,128,128]{2,1,0:T(8,128)S(1)}, s16[2064,128]{1,0:T(8,128)(2,1)S(1)}) custom-call(s16[8,35,16,128]{3,2,1,0:T(8,128)(2,1)S(1)} %all_to_all.25.in_ref, bf16[1,16,128,128]{3,2,1,0:T(8,128)(2,1)S(1)} %copy-done, bf16[1,16,128,128]{3,2,1,0:T(8,128)(2,1)S(1)} %collective-permute-done.prev_ref, bf16[128,384]{1,0:T(8,128)(2,1)S(1)} %copy-done.3, ...), custom_call_target="tpu_custom_call" | custom-call | flops 200000000 | bytes 7000000 | tf_op jit(solution)/shard_map/back_cross/pallas_call | solution.py:469
  76.5 2.9 %collective-permute-start.2 = (s16[2064,128]{1,0:T(8,128)(2,1)S(1)}, s16[2064,128]{1,0:T(8,128)(2,1)S(1)}, u32[]{:S(2)}, u32[]{:S(2)}) collective-permute-start(s16[2064,128]{1,0:T(8,128)(2,1)S(1)} %get-tuple-element.20), channel_id=1, source_target_pairs={{8,0},{16,8},{24,16},{32,24},{40,32},{48,40},{56,48},{64,56},{72,6... | collective-permute-start | bytes 1585160 | tf_op jit(solution)/shard_map/ppermute | solution.py:365
  79.4 1.3 %solve0.1 = s16[8,17,16,128]{3,2,1,0:T(8,128)(2,1)S(1)} custom-call(s16[8,35,16,128]{3,2,1,0:T(8,128)(2,1)S(1)} %all_to_all.25.in_ref, f32[16,128,128]{2,1,0:T(8,128)S(1)} %table.1.table_ref, bf16[128,384]{1,0:T(8,128)(2,1)S(1)} %copy-done.4), custom_call_target="tpu_custom_call" | custom-call | flops 300000000 | bytes 10500000 | tf_op jit(solution)/shard_map/solve0/pallas_call | solution.py:442
  80.6 13.7 %all_to_all.26.in_ref = s16[8,17,16,128]{3,2,1,0:T(8,128)(2,1)S(1)} all-to-all(s16[8,17,16,128]{3,2,1,0:T(8,128)(2,1)S(1)} %solve0.1), channel_id=1, replica_groups={{0,1,2,3,4,5,6,7},{8,9,10,11,12,13,14,15},{16,17,18,19,20,21,22,23},{24..., dimensions={0} | all-to-all | bytes 1114112 | tf_op jit(solution)/shard_map/all_to_all | solution.py:452
  94.4 0.0 collective-permute-done.2.sent_ref
  94.4 1.6 %back_own.1 = f32[1,16,128,128]{3,2,1,0:T(8,128)} custom-call(s16[8,17,16,128]{3,2,1,0:T(8,128)(2,1)S(1)} %all_to_all.26.in_ref, bf16[1,16,128,128]{3,2,1,0:T(8,128)(2,1)S(1)} %copy-done, f32[16,128,128]{2,1,0:T(8,128)S(1)} %get-tuple-element.19.kept_ref, s16[2064,128]{1,0:T(8,128)(2,1)S(1)} %collective-permute-done.2.sent_ref, ...), custom_call_target="tpu_custom_call" | custom-call | flops 200000000 | bytes 7000000 | tf_op jit(solution)/shard_map/back_own/pallas_call | solution.py:481
  (16 shorter events, 0.0 us)
Async XLA Ops:
  0.0 0.7 copy-start.5
  1.4 24.1 %copy-start.6 = (bf16[1,9,512]{2,1,0:T(8,128)(2,1)S(1)}, bf16[1,9,512]{2,1,0:T(8,128)(2,1)}, u32[]{:S(2)}) copy-start(bf16[1,9,512]{2,1,0:T(8,128)(2,1)} %prev_proj_ref) | copy-start | bytes 27652
  1.5 37.5 %copy-start = (bf16[1,16,128,128]{3,2,1,0:T(8,128)(2,1)S(1)}, bf16[1,16,128,128]{3,2,1,0:T(8,128)(2,1)}, u32[]{:S(2)}) copy-start(bf16[1,16,128,128]{3,2,1,0:T(8,128)(2,1)} %own_ref.7) | copy-start | bytes 1572868
  1.5 37.5 %copy-start.1 = (bf16[256,256]{1,0:T(8,128)(2,1)S(1)}, bf16[256,256]{1,0:T(8,128)(2,1)}, u32[]{:S(2)}) copy-start(bf16[256,256]{1,0:T(8,128)(2,1)} %constant.14.clone.right_ref) | copy-start | bytes 393220
  1.5 37.5 %copy-start.2 = (bf16[128,384]{1,0:T(8,128)(2,1)S(1)}, bf16[128,384]{1,0:T(8,128)(2,1)}, u32[]{:S(2)}) copy-start(bf16[128,384]{1,0:T(8,128)(2,1)} %constant.16.clone.left_ref) | copy-start | bytes 294916
  1.5 16.6 %all-to-all-start = ((bf16[16,16,128]{2,1,0:T(8,128)(2,1)}), bf16[16,16,128]{2,1,0:T(8,128)(2,1)S(1)}, u32[]{:S(2)}, u32[]{:S(2)}) async-start(bf16[16,16,128]{2,1,0:T(8,128)(2,1)} %messages.1.after_ref), calls=%async_computation | async-start | bytes 131072 | tf_op jit(solution)/shard_map/all_to_all | solution.py:385
  10.7 19.3 %collective-permute-start = (bf16[1,16,128,128]{3,2,1,0:T(8,128)(2,1)}, bf16[1,16,128,128]{3,2,1,0:T(8,128)(2,1)S(1)}, u32[]{:S(2)}, u32[]{:S(2)}) collective-permute-start(bf16[1,16,128,128]{3,2,1,0:T(8,128)(2,1)} %own_ref.7), channel_id=1, source_target_pairs={{120,0},{0,8},{8,16},{16,24},{24,32},{32,40},{40,48},{48,56},{56,6... | collective-permute-start | bytes 1572872 | tf_op jit(solution)/shard_map/ppermute | solution.py:365
  13.9 0.9 copy-start.10
  14.8 0.7 copy-start.11
  19.9 19.0 %all-to-all-start.1 = ((s16[128,16,128]{2,1,0:T(8,128)(2,1)}), s16[128,16,128]{2,1,0:T(8,128)(2,1)S(1)}, u32[]{:S(2)}, u32[]{:S(2)}) async-start(s16[128,16,128]{2,1,0:T(8,128)(2,1)} %charges.1), calls=%async_computation.1 | async-start | bytes 1048576 | tf_op jit(solution)/shard_map/all_to_all | solution.py:418
  25.5 4.5 %collective-permute-start.1 = (bf16[1,9,512]{2,1,0:T(8,128)(2,1)S(1)}, bf16[1,9,512]{2,1,0:T(8,128)(2,1)S(1)}, u32[]{:S(2)}, u32[]{:S(2)}) collective-permute-start(bf16[1,9,512]{2,1,0:T(8,128)(2,1)S(1)} %copy-done.6), channel_id=1, source_target_pairs={{120,0},{0,8},{8,16},{16,24},{24,32},{32,40},{40,48},{48,56},{56,6... | collective-permute-start | bytes 27656 | tf_op jit(solution)/shard_map/ppermute | solution.py:365
  42.9 12.6 %all-to-all-start.2 = ((s16[8,18,16,128]{3,2,1,0:T(8,128)(2,1)}), s16[8,18,16,128]{3,2,1,0:T(8,128)(2,1)S(1)}, u32[]{:S(2)}, u32[]{:S(2)}) async-start(s16[8,18,16,128]{3,2,1,0:T(8,128)(2,1)} %density1.1), calls=%async_computation.2 | async-start | bytes 1179648 | tf_op jit(solution)/shard_map/all_to_all | solution.py:452
  46.5 3.2 %copy-start.7 = (f32[128,128]{1,0:T(8,128)S(1)}, f32[128,128]{1,0:T(8,128)}, u32[]{:S(2)}) copy-start(f32[128,128]{1,0:T(8,128)} %constant.19.clone.fold_x_ref) | copy-start | bytes 196612
  46.5 3.2 %copy-start.8 = (f32[8,16]{1,0:T(8,128)S(1)}, f32[8,16]{1,0:T(8,128)}, u32[]{:S(2)}) copy-start(f32[8,16]{1,0:T(8,128)} %constant.18.clone.squares_ref) | copy-start | bytes 1540
  46.5 3.2 %copy-start.9 = (f32[1,128]{1,0:T(1,128)S(1)}, f32[1,128]{1,0:T(1,128)}, u32[]{:S(2)}) copy-start(f32[1,128]{1,0:T(1,128)} %constant.20.clone.fold_z_ref) | copy-start | bytes 1540
  49.7 5.8 %copy-start.4 = (bf16[128,384]{1,0:T(8,128)(2,1)S(1)}, bf16[128,384]{1,0:T(8,128)(2,1)}, u32[]{:S(2)}) copy-start(bf16[128,384]{1,0:T(8,128)(2,1)} %constant.15.clone.left_ref) | copy-start | bytes 294916
  56.7 18.7 %copy-start.3 = (bf16[128,384]{1,0:T(8,128)(2,1)S(1)}, bf16[128,384]{1,0:T(8,128)(2,1)}, u32[]{:S(2)}) copy-start(bf16[128,384]{1,0:T(8,128)(2,1)} %constant.17.clone.left_ref) | copy-start | bytes 294916
  76.5 17.9 %collective-permute-start.2 = (s16[2064,128]{1,0:T(8,128)(2,1)S(1)}, s16[2064,128]{1,0:T(8,128)(2,1)S(1)}, u32[]{:S(2)}, u32[]{:S(2)}) collective-permute-start(s16[2064,128]{1,0:T(8,128)(2,1)S(1)} %get-tuple-element.20), channel_id=1, source_target_pairs={{8,0},{16,8},{24,16},{32,24},{40,32},{48,40},{56,48},{64,56},{72,6... | collective-permute-start | bytes 1585160 | tf_op jit(solution)/shard_map/ppermute | solution.py:365

commit v7 on v6

--- a/solution.py
+++ b/solution.py
@@ -193,7 +193,7 @@
         copy.wait()
 
 
-def density_kernel(p, place_vmem, here_ref, charge_ref, own_ref, prev_ref, proj_ref, prev_proj_ref, right_ref, left_ref, out_ref, field, second, scales, place_ref, sem):
+def density_kernel(p, place_vmem, here_ref, charge_ref, own_ref, prev_ref, proj_ref, prev_proj_ref, right_ref, left_ref, out_ref, field, second, scales, place_ref, sem, *stream):
     fetch = pltpu.make_async_copy(place_vmem, place_ref, sem)
     fetch.start()
     rows, owners = here_ref.shape[0], charge_ref.shape[0]
@@ -236,13 +236,15 @@
                     total[at] = value
         return carry
 
-    lax.fori_loop(0, rows, add_row, 0)
+    lax.fori_loop(0, rows, add_row, 0, unroll=True)
     for x in range(0, PLANES, 2):
         both = times_right(jnp.concatenate([field[x] + second[x], field[x + 1] + second[x + 1]], axis=0), right_ref)
         both = times_left(left_ref, jnp.concatenate([both[:NG], both[NG:]], axis=1))
         field[x] = both[:, :NG]
         field[x + 1] = both[:, NG:]
 
+    packed = stream[0] if stream else out_ref
+    copies = []
     for d in range(SLABS):
         rows = pl.ds(d * ROWS, ROWS)
         largest = jnp.abs(field[0, rows])
@@ -254,11 +256,15 @@
         for x in range(PLANES):
             scaled = field[x, rows] * factor
             whole = jnp.round(scaled)
-            out_ref[d, x] = to_int16(whole)
+            packed[d, x] = to_int16(whole)
             lows.append((scaled - whole)[0:1])
-        out_ref[d, PLANES] = to_int16(code)
+        packed[d, PLANES] = to_int16(code)
         low = jnp.concatenate(lows, axis=0) * (2.0 * QMAX)
-        out_ref[d, PLANES + 1] = to_int16(jnp.round(low))
+        packed[d, PLANES + 1] = to_int16(jnp.round(low))
+        if stream:
+            copies.append(streamed(out_ref, packed, stream[1], d, d, 1))
+    for copy in copies:
+        copy.wait()
 
 
 def table_kernel(after_ref, squares_ref, fold_x_ref, fold_z_ref, out_ref):
@@ -422,6 +428,8 @@
     fold_z = jnp.asarray(squares[None, :])
 
     def density(p, other, other_proj):
+        shape = (n_slab, FWD_TILES, 16, NG)
+        stream = [pltpu.VMEM(shape, jnp.int16), pltpu.SemaphoreType.DMA((SLABS,))] if p == 1 else []
         return call(
             functools.partial(density_kernel, p),
             [vmem()] * 9,
@@ -432,9 +440,11 @@
                 pltpu.VMEM((owners, NG), F32),
                 pltpu.SMEM(places.shape, jnp.int32),
                 pltpu.SemaphoreType.DMA,
-            ],
+            ]
+            + stream,
             "density" + str(p),
             6,
+            [hbm()] if stream else None,
         )(places, here, charges, own, other, proj, other_proj, right, left_y)
 
     def solve(name, base, spectrum, *more):

time: 96.6 us -> 96.2 us (level)
  transfers between devices with their start and end apart: 6 -> 6, of which waited for: 4 -> 4; matrix products, arithmetic and copies ran while one was open for 0% -> 0% of each run, Pallas kernels for 8% -> 7%
where the time goes in v7:
time: 96.2 us; the launch traced here: 95.7 us
  blocking collectives  32.5 us (34%)
  starting transfers between devices  28 us (29%)
  waiting for transfers between devices  17.5 us (18%)
  Pallas kernels  15.2 us (16%)
  local copies, waits for them, and re-layouts  2.35 us (2%)
    all_to_all x2, blocking collectives, swap(): lax.all_to_all(block, 'slab', split_axis=0, concat_axis=0, tiled=True, ax...  32.5 us
    ppermute x3, starting transfers between devices, from_behind(): lax.ppermute(block, axis, [((i - distance) % count, i) for i in range(cou...  9.61 us
    all_to_all x1, starting transfers between devices, per_device(): lax.all_to_all(messages, 'band', split_axis=0, concat_axis=0, tiled=True,...  9.27 us
    all_to_all x1, waiting for transfers between devices, per_device(): lax.all_to_all(charges, ('band', 'slab'), split_axis=0, concat_axis=0, ti...  8.93 us
    pallas_call x2, Pallas kernels, density(): call(functools.partial(density_kernel, p), [vmem()] * 9, jax.ShapeDtypeSt...  6.51 us
    all_to_all x1, waiting for transfers between devices, swap(): lax.all_to_all(block, 'slab', split_axis=0, concat_axis=0, tiled=True, ax...  5.69 us
    all_to_all x1, starting transfers between devices, per_device(): lax.all_to_all(charges, ('band', 'slab'), split_axis=0, concat_axis=0, ti...  5.57 us
    all_to_all x1, starting transfers between devices, swap(): lax.all_to_all(block, 'slab', split_axis=0, concat_axis=0, tiled=True, ax...  3.55 us
  transfers between devices with their start and end apart: 6, of which 4 were waited for; matrix products, arithmetic and copies ran while one was open for 0% of the time, Pallas kernels for 7%

profile of v7, /device:TPU:1, one launch (start us, length us, event | category | flops | bytes accessed | tf_op | source)
XLA Modules:
  0.0 95.7 jit_solution(18075571142876280914)
XLA Ops:
  0.0 0.7 copy-done.5
  0.7 0.7 messages.1.after_ref
  1.5 9.3 %all-to-all-start = ((bf16[16,16,128]{2,1,0:T(8,128)(2,1)}), bf16[16,16,128]{2,1,0:T(8,128)(2,1)S(1)}, u32[]{:S(2)}, u32[]{:S(2)}) async-start(bf16[16,16,128]{2,1,0:T(8,128)(2,1)} %messages.1.after_ref), calls=%async_computation | async-start | bytes 131072 | tf_op jit(solution)/shard_map/all_to_all | solution.py:391
  10.7 3.1 %collective-permute-start = (bf16[1,16,128,128]{3,2,1,0:T(8,128)(2,1)}, bf16[1,16,128,128]{3,2,1,0:T(8,128)(2,1)S(1)}, u32[]{:S(2)}, u32[]{:S(2)}) collective-permute-start(bf16[1,16,128,128]{3,2,1,0:T(8,128)(2,1)} %own_ref.7), channel_id=1, source_target_pairs={{120,0},{0,8},{8,16},{16,24},{24,32},{32,40},{40,48},{48,56},{56,6... | collective-permute-start | bytes 1572872 | tf_op jit(solution)/shard_map/ppermute | solution.py:371
  13.9 0.9 copy-done.10
  14.8 0.7 copy-done.11
  15.5 0.7 local.1
  16.1 2.0 %all-to-all-done.proj_ref = bf16[16,16,128]{2,1,0:T(8,128)(2,1)S(1)} async-done(((bf16[16,16,128]{2,1,0:T(8,128)(2,1)}), bf16[16,16,128]{2,1,0:T(8,128)(2,1)S(1)}, u32[]{:S(2)}, u32[]{:S(2)}) %all-to-all-start) | async-done | bytes 65568 | tf_op jit(solution)/shard_map/all_to_all | solution.py:391
  18.1 1.8 %charges.1 = s16[128,16,128]{2,1,0:T(8,128)(2,1)} custom-call(f32[4,128]{1,0:T(4,128)S(1)} %get-tuple-element.15.goes_ref, bf16[16,16,128]{2,1,0:T(8,128)(2,1)S(1)} %all-to-all-done.proj_ref, bf16[8,64,128]{2,1,0:T(8,128)(2,1)S(1)} %get-tuple-element.17.block_ref), custom_call_target="tpu_custom_call" | custom-call | flops 200000000 | bytes 7000000 | tf_op jit(solution)/shard_map/charges/pallas_call | solution.py:415
  19.9 5.6 %all-to-all-start.1 = ((s16[128,16,128]{2,1,0:T(8,128)(2,1)}), s16[128,16,128]{2,1,0:T(8,128)(2,1)S(1)}, u32[]{:S(2)}, u32[]{:S(2)}) async-start(s16[128,16,128]{2,1,0:T(8,128)(2,1)} %charges.1), calls=%async_computation.1 | async-start | bytes 1048576 | tf_op jit(solution)/shard_map/all_to_all | solution.py:424
  25.5 3.6 %collective-permute-start.1 = (bf16[1,9,512]{2,1,0:T(8,128)(2,1)S(1)}, bf16[1,9,512]{2,1,0:T(8,128)(2,1)S(1)}, u32[]{:S(2)}, u32[]{:S(2)}) collective-permute-start(bf16[1,9,512]{2,1,0:T(8,128)(2,1)S(1)} %copy-done.6), channel_id=1, source_target_pairs={{120,0},{0,8},{8,16},{16,24},{24,32},{32,40},{40,48},{48,56},{56,6... | collective-permute-start | bytes 27656 | tf_op jit(solution)/shard_map/ppermute | solution.py:371
  29.1 0.9 collective-permute-done.1.prev_proj_ref
  30.0 0.0 collective-permute-done.prev_ref
  30.0 8.9 %all-to-all-done.1.charge_ref = s16[128,16,128]{2,1,0:T(8,128)(2,1)S(1)} async-done(((s16[128,16,128]{2,1,0:T(8,128)(2,1)}), s16[128,16,128]{2,1,0:T(8,128)(2,1)S(1)}, u32[]{:S(2)}, u32[]{:S(2)}) %all-to-all-start.1) | async-done | bytes 524320 | tf_op jit(solution)/shard_map/all_to_all | solution.py:424
  38.9 3.6 %density1.1 = s16[8,18,16,128]{3,2,1,0:T(8,128)(2,1)} custom-call(s32[4,128]{1,0:T(4,128)S(1)} %get-tuple-element.13.place_vmem, f32[4,128]{1,0:T(4,128)S(1)} %get-tuple-element.14.here_ref, s16[128,16,128]{2,1,0:T(8,128)(2,1)S(1)} %all-to-all-done.1.charge_ref, bf16[1,16,128,128]{3,2,1,0:T(8,128)(2,1)S(1)} %copy-done, ...), custom_call_target="tpu_custom_call" | custom-call | flops 600000000 | bytes 21000000 | tf_op jit(solution)/shard_map/density1/pallas_call | solution.py:433
  42.6 3.6 %all-to-all-start.2 = ((s16[8,18,16,128]{3,2,1,0:T(8,128)(2,1)}), s16[8,18,16,128]{3,2,1,0:T(8,128)(2,1)S(1)}, u32[]{:S(2)}, u32[]{:S(2)}) async-start(s16[8,18,16,128]{3,2,1,0:T(8,128)(2,1)} %density1.1), calls=%async_computation.2 | async-start | bytes 1179648 | tf_op jit(solution)/shard_map/all_to_all | solution.py:462
  46.1 0.0 copy-start.7
  46.1 0.0 copy-start.8
  46.1 0.0 copy-start.9
  46.2 2.9 %density0.1.after_ref.rest_0_ = s16[8,18,16,128]{3,2,1,0:T(8,128)(2,1)S(1)} custom-call(s32[4,128]{1,0:T(4,128)S(1)} %get-tuple-element.13.place_vmem, f32[4,128]{1,0:T(4,128)S(1)} %get-tuple-element.14.here_ref, s16[128,16,128]{2,1,0:T(8,128)(2,1)S(1)} %all-to-all-done.1.charge_ref, bf16[1,16,128,128]{3,2,1,0:T(8,128)(2,1)S(1)} %copy-done, ...), custom_call_target="tpu_custom_call" | custom-call | flops 600000000 | bytes 21000000 | tf_op jit(solution)/shard_map/density0/pallas_call | solution.py:433
  49.1 0.0 copy-start.4
  49.1 0.3 table.1.table_ref
  49.4 5.7 %all-to-all-done.2.in_ref = s16[8,18,16,128]{3,2,1,0:T(8,128)(2,1)S(1)} async-done(((s16[8,18,16,128]{3,2,1,0:T(8,128)(2,1)}), s16[8,18,16,128]{3,2,1,0:T(8,128)(2,1)S(1)}, u32[]{:S(2)}, u32[]{:S(2)}) %all-to-all-start.2) | async-done | bytes 589856 | tf_op jit(solution)/shard_map/all_to_all | solution.py:462
  55.1 1.3 %solve1.1 = s16[8,35,16,128]{3,2,1,0:T(8,128)(2,1)S(1)} custom-call(s16[8,18,16,128]{3,2,1,0:T(8,128)(2,1)S(1)} %all-to-all-done.2.in_ref, f32[16,128,128]{2,1,0:T(8,128)S(1)} %table.1.table_ref, bf16[128,384]{1,0:T(8,128)(2,1)S(1)} %copy-done.4, s16[8,18,16,128]{3,2,1,0:T(8,128)(2,1)S(1)} %density0.1.after_ref.rest_0_), custom_call_target="tpu_custom_call" | custom-call | flops 300000000 | bytes 10500000 | tf_op jit(solution)/shard_map/solve1/pallas_call | solution.py:452
  56.4 0.0 copy-start.3
  56.4 18.7 %all_to_all.25.in_ref = s16[8,35,16,128]{3,2,1,0:T(8,128)(2,1)S(1)} all-to-all(s16[8,35,16,128]{3,2,1,0:T(8,128)(2,1)S(1)} %solve1.1), channel_id=1, replica_groups={{0,1,2,3,4,5,6,7},{8,9,10,11,12,13,14,15},{16,17,18,19,20,21,22,23},{24..., dimensions={0} | all-to-all | bytes 2293760 | tf_op jit(solution)/shard_map/all_to_all | solution.py:462
  75.1 1.0 %back_cross.1 = (f32[16,128,128]{2,1,0:T(8,128)S(1)}, s16[2064,128]{1,0:T(8,128)(2,1)S(1)}) custom-call(s16[8,35,16,128]{3,2,1,0:T(8,128)(2,1)S(1)} %all_to_all.25.in_ref, bf16[1,16,128,128]{3,2,1,0:T(8,128)(2,1)S(1)} %copy-done, bf16[1,16,128,128]{3,2,1,0:T(8,128)(2,1)S(1)} %collective-permute-done.prev_ref, bf16[128,384]{1,0:T(8,128)(2,1)S(1)} %copy-done.3, ...), custom_call_target="tpu_custom_call" | custom-call | flops 200000000 | bytes 7000000 | tf_op jit(solution)/shard_map/back_cross/pallas_call | solution.py:479
  76.1 2.9 %collective-permute-start.2 = (s16[2064,128]{1,0:T(8,128)(2,1)S(1)}, s16[2064,128]{1,0:T(8,128)(2,1)S(1)}, u32[]{:S(2)}, u32[]{:S(2)}) collective-permute-start(s16[2064,128]{1,0:T(8,128)(2,1)S(1)} %get-tuple-element.20), channel_id=1, source_target_pairs={{8,0},{16,8},{24,16},{32,24},{40,32},{48,40},{56,48},{64,56},{72,6... | collective-permute-start | bytes 1585160 | tf_op jit(solution)/shard_map/ppermute | solution.py:371
  79.0 1.3 %solve0.1 = s16[8,17,16,128]{3,2,1,0:T(8,128)(2,1)S(1)} custom-call(s16[8,35,16,128]{3,2,1,0:T(8,128)(2,1)S(1)} %all_to_all.25.in_ref, f32[16,128,128]{2,1,0:T(8,128)S(1)} %table.1.table_ref, bf16[128,384]{1,0:T(8,128)(2,1)S(1)} %copy-done.4), custom_call_target="tpu_custom_call" | custom-call | flops 300000000 | bytes 10500000 | tf_op jit(solution)/shard_map/solve0/pallas_call | solution.py:452
  80.3 13.7 %all_to_all.26.in_ref = s16[8,17,16,128]{3,2,1,0:T(8,128)(2,1)S(1)} all-to-all(s16[8,17,16,128]{3,2,1,0:T(8,128)(2,1)S(1)} %solve0.1), channel_id=1, replica_groups={{0,1,2,3,4,5,6,7},{8,9,10,11,12,13,14,15},{16,17,18,19,20,21,22,23},{24..., dimensions={0} | all-to-all | bytes 1114112 | tf_op jit(solution)/shard_map/all_to_all | solution.py:462
  94.0 0.0 collective-permute-done.2.sent_ref
  94.1 1.6 %back_own.1 = f32[1,16,128,128]{3,2,1,0:T(8,128)} custom-call(s16[8,17,16,128]{3,2,1,0:T(8,128)(2,1)S(1)} %all_to_all.26.in_ref, bf16[1,16,128,128]{3,2,1,0:T(8,128)(2,1)S(1)} %copy-done, f32[16,128,128]{2,1,0:T(8,128)S(1)} %get-tuple-element.19.kept_ref, s16[2064,128]{1,0:T(8,128)(2,1)S(1)} %collective-permute-done.2.sent_ref, ...), custom_call_target="tpu_custom_call" | custom-call | flops 200000000 | bytes 7000000 | tf_op jit(solution)/shard_map/back_own/pallas_call | solution.py:491
  (16 shorter events, 0.0 us)
Async XLA Ops:
  0.0 0.7 copy-start.5
  1.4 24.1 %copy-start.6 = (bf16[1,9,512]{2,1,0:T(8,128)(2,1)S(1)}, bf16[1,9,512]{2,1,0:T(8,128)(2,1)}, u32[]{:S(2)}) copy-start(bf16[1,9,512]{2,1,0:T(8,128)(2,1)} %prev_proj_ref) | copy-start | bytes 27652
  1.5 37.5 %copy-start = (bf16[1,16,128,128]{3,2,1,0:T(8,128)(2,1)S(1)}, bf16[1,16,128,128]{3,2,1,0:T(8,128)(2,1)}, u32[]{:S(2)}) copy-start(bf16[1,16,128,128]{3,2,1,0:T(8,128)(2,1)} %own_ref.7) | copy-start | bytes 1572868
  1.5 37.5 %copy-start.1 = (bf16[256,256]{1,0:T(8,128)(2,1)S(1)}, bf16[256,256]{1,0:T(8,128)(2,1)}, u32[]{:S(2)}) copy-start(bf16[256,256]{1,0:T(8,128)(2,1)} %constant.14.clone.right_ref) | copy-start | bytes 393220
  1.5 37.5 %copy-start.2 = (bf16[128,384]{1,0:T(8,128)(2,1)S(1)}, bf16[128,384]{1,0:T(8,128)(2,1)}, u32[]{:S(2)}) copy-start(bf16[128,384]{1,0:T(8,128)(2,1)} %constant.16.clone.left_ref) | copy-start | bytes 294916
  1.5 16.6 %all-to-all-start = ((bf16[16,16,128]{2,1,0:T(8,128)(2,1)}), bf16[16,16,128]{2,1,0:T(8,128)(2,1)S(1)}, u32[]{:S(2)}, u32[]{:S(2)}) async-start(bf16[16,16,128]{2,1,0:T(8,128)(2,1)} %messages.1.after_ref), calls=%async_computation | async-start | bytes 131072 | tf_op jit(solution)/shard_map/all_to_all | solution.py:391
  10.7 19.3 %collective-permute-start = (bf16[1,16,128,128]{3,2,1,0:T(8,128)(2,1)}, bf16[1,16,128,128]{3,2,1,0:T(8,128)(2,1)S(1)}, u32[]{:S(2)}, u32[]{:S(2)}) collective-permute-start(bf16[1,16,128,128]{3,2,1,0:T(8,128)(2,1)} %own_ref.7), channel_id=1, source_target_pairs={{120,0},{0,8},{8,16},{16,24},{24,32},{32,40},{40,48},{48,56},{56,6... | collective-permute-start | bytes 1572872 | tf_op jit(solution)/shard_map/ppermute | solution.py:371
  13.9 0.9 copy-start.10
  14.8 0.7 copy-start.11
  19.9 19.0 %all-to-all-start.1 = ((s16[128,16,128]{2,1,0:T(8,128)(2,1)}), s16[128,16,128]{2,1,0:T(8,128)(2,1)S(1)}, u32[]{:S(2)}, u32[]{:S(2)}) async-start(s16[128,16,128]{2,1,0:T(8,128)(2,1)} %charges.1), calls=%async_computation.1 | async-start | bytes 1048576 | tf_op jit(solution)/shard_map/all_to_all | solution.py:424
  25.5 4.5 %collective-permute-start.1 = (bf16[1,9,512]{2,1,0:T(8,128)(2,1)S(1)}, bf16[1,9,512]{2,1,0:T(8,128)(2,1)S(1)}, u32[]{:S(2)}, u32[]{:S(2)}) collective-permute-start(bf16[1,9,512]{2,1,0:T(8,128)(2,1)S(1)} %copy-done.6), channel_id=1, source_target_pairs={{120,0},{0,8},{8,16},{16,24},{24,32},{32,40},{40,48},{48,56},{56,6... | collective-permute-start | bytes 27656 | tf_op jit(solution)/shard_map/ppermute | solution.py:371
  42.6 12.6 %all-to-all-start.2 = ((s16[8,18,16,128]{3,2,1,0:T(8,128)(2,1)}), s16[8,18,16,128]{3,2,1,0:T(8,128)(2,1)S(1)}, u32[]{:S(2)}, u32[]{:S(2)}) async-start(s16[8,18,16,128]{3,2,1,0:T(8,128)(2,1)} %density1.1), calls=%async_computation.2 | async-start | bytes 1179648 | tf_op jit(solution)/shard_map/all_to_all | solution.py:462
  46.1 2.9 %copy-start.7 = (f32[128,128]{1,0:T(8,128)S(1)}, f32[128,128]{1,0:T(8,128)}, u32[]{:S(2)}) copy-start(f32[128,128]{1,0:T(8,128)} %constant.19.clone.fold_x_ref) | copy-start | bytes 196612
  46.1 2.9 %copy-start.8 = (f32[8,16]{1,0:T(8,128)S(1)}, f32[8,16]{1,0:T(8,128)}, u32[]{:S(2)}) copy-start(f32[8,16]{1,0:T(8,128)} %constant.18.clone.squares_ref) | copy-start | bytes 1540
  46.1 2.9 %copy-start.9 = (f32[1,128]{1,0:T(1,128)S(1)}, f32[1,128]{1,0:T(1,128)}, u32[]{:S(2)}) copy-start(f32[1,128]{1,0:T(1,128)} %constant.20.clone.fold_z_ref) | copy-start | bytes 1540
  49.1 6.0 %copy-start.4 = (bf16[128,384]{1,0:T(8,128)(2,1)S(1)}, bf16[128,384]{1,0:T(8,128)(2,1)}, u32[]{:S(2)}) copy-start(bf16[128,384]{1,0:T(8,128)(2,1)} %constant.15.clone.left_ref) | copy-start | bytes 294916
  56.4 18.7 %copy-start.3 = (bf16[128,384]{1,0:T(8,128)(2,1)S(1)}, bf16[128,384]{1,0:T(8,128)(2,1)}, u32[]{:S(2)}) copy-start(bf16[128,384]{1,0:T(8,128)(2,1)} %constant.17.clone.left_ref) | copy-start | bytes 294916
  76.1 17.9 %collective-permute-start.2 = (s16[2064,128]{1,0:T(8,128)(2,1)S(1)}, s16[2064,128]{1,0:T(8,128)(2,1)S(1)}, u32[]{:S(2)}, u32[]{:S(2)}) collective-permute-start(s16[2064,128]{1,0:T(8,128)(2,1)S(1)} %get-tuple-element.20), channel_id=1, source_target_pairs={{8,0},{16,8},{24,16},{32,24},{40,32},{48,40},{56,48},{64,56},{72,6... | collective-permute-start | bytes 1585160 | tf_op jit(solution)/shard_map/ppermute | solution.py:371
